TPU v7x, 32 devices: a whole 2x2x4 slice. The times are simulated.
32 devices in a mesh: dp: 4 (over y, x), tensor: 8 (over z, core).
Axes of the slice: x: 2, y: 2, z: 4, core: 2. Of those that a mesh axis runs over, the one named last changes fastest.
Arguments:
- inputs: bfloat16 [8192, 2048], P(('dp', 'tensor')), may hold values from -6 to 6
- out_grad: bfloat16 [8192, 2048], P(('dp', 'tensor')), may hold values from -6 to 6
- segments: int32 [4, 2048], P('dp'), may hold values from 0 to 3, never falling along the last dimension, each value on 1 to 1024 neighbouring positions
- w_qkv: float32 [3, 2048, 2048], P(None, 'dp', 'tensor'), may hold values from -0.125 to 0.125
- w_out: float32 [2048, 2048], P('tensor', 'dp'), may hold values from -2 to 2
- w_gate_up: float32 [2, 2048, 5632], P(None, 'dp', 'tensor'), may hold values from -0.125 to 0.125
- w_down: float32 [5632, 2048], P('tensor', 'dp'), may hold values from -0.15625 to 0.15625
- qkv_bias: float32 [3, 2048], P(None, 'tensor'), may hold values from -3 to 3
- norm_gain: float32 [2, 2048], replicated, may hold values from 0.5 to 1.5
- norm_bias: float32 [2, 2048], replicated, may hold values from -2 to 2
- first_qkv: float32 [3, 2048, 2048], P(None, 'dp', 'tensor'), may hold values from -271.529 to 271.529
- first_out: float32 [2048, 2048], P('tensor', 'dp'), may hold values from -54.3058 to 54.3058
- first_gate_up: float32 [2, 2048, 5632], P(None, 'dp', 'tensor'), may hold values from -54.3058 to 54.3058
- first_down: float32 [5632, 2048], P('tensor', 'dp'), may hold values from -54.3058 to 54.3058
- first_bias: float32 [3, 2048], P(None, 'tensor'), may hold values from -271.529 to 271.529
- first_gain: float32 [2, 2048], replicated, may hold values from -271.529 to 271.529
- first_shift: float32 [2, 2048], replicated, may hold values from -271.529 to 271.529
- second_qkv: float32 [3, 2048, 2048], P(None, 'dp', 'tensor'), may hold values from 163.84 to 1638.4
- second_out: float32 [2048, 2048], P('tensor', 'dp'), may hold values from 8.192 to 32.768
- second_gate_up: float32 [2, 2048, 5632], P(None, 'dp', 'tensor'), may hold values from 8.192 to 32.768
- second_down: float32 [5632, 2048], P('tensor', 'dp'), may hold values from 8.192 to 32.768
- second_bias: float32 [3, 2048], P(None, 'tensor'), may hold values from 16.384 to 163.84
- second_gain: float32 [2, 2048], replicated, may hold values from 16.384 to 163.84
- second_shift: float32 [2, 2048], replicated, may hold values from 16.384 to 163.84
Outputs:
- outputs: bfloat16 [8192, 2048], P(('dp', 'tensor'))
- input_grad: bfloat16 [8192, 2048], P(('dp', 'tensor'))
- grad_w_qkv: float32 [3, 2048, 2048], P(None, 'dp', 'tensor')
- grad_w_out: float32 [2048, 2048], P('tensor', 'dp')
- grad_w_gate_up: float32 [2, 2048, 5632], P(None, 'dp', 'tensor')
- grad_w_down: float32 [5632, 2048], P('tensor', 'dp')
- grad_qkv_bias: float32 [3, 2048], P(None, 'tensor')
- grad_norm_gain: float32 [2, 2048], replicated
- grad_norm_bias: float32 [2, 2048], replicated
- new_w_qkv: float32 [3, 2048, 2048], P(None, 'dp', 'tensor')
- new_w_out: float32 [2048, 2048], P('tensor', 'dp')
- new_w_gate_up: float32 [2, 2048, 5632], P(None, 'dp', 'tensor')
- new_w_down: float32 [5632, 2048], P('tensor', 'dp')
- new_qkv_bias: float32 [3, 2048], P(None, 'tensor')
- new_norm_gain: float32 [2, 2048], replicated
- new_norm_bias: float32 [2, 2048], replicated
- new_first_qkv: float32 [3, 2048, 2048], P(None, 'dp', 'tensor')
- new_first_out: float32 [2048, 2048], P('tensor', 'dp')
- new_first_gate_up: float32 [2, 2048, 5632], P(None, 'dp', 'tensor')
- new_first_down: float32 [5632, 2048], P('tensor', 'dp')
- new_first_bias: float32 [3, 2048], P(None, 'tensor')
- new_first_gain: float32 [2, 2048], replicated
- new_first_shift: float32 [2, 2048], replicated
- new_second_qkv: float32 [3, 2048, 2048], P(None, 'dp', 'tensor')
- new_second_out: float32 [2048, 2048], P('tensor', 'dp')
- new_second_gate_up: float32 [2, 2048, 5632], P(None, 'dp', 'tensor')
- new_second_down: float32 [5632, 2048], P('tensor', 'dp')
- new_second_bias: float32 [3, 2048], P(None, 'tensor')
- new_second_gain: float32 [2, 2048], replicated
- new_second_shift: float32 [2, 2048], replicated
Inputs may be any that keep to these rules, and one draw needn't show every extreme that they name: `segments`: segment numbers never fall along a sequence; a document has at most 1024 tokens.
All inputs are finite; a program needn't handle non-finite values.
Results may differ from a plain program's by a relative error of at most 0.019.
Values may be sent and summed in bfloat16 or wider, within the bound.
A program may use at most 192 MiB of HBM per device.

v0:
```python
import jax
import jax.numpy as jnp
from jax import lax
from jax.sharding import PartitionSpec as P

HD = 64
ROT = 16
STEP = 10


def layer_norm_parts(values, gain_row, shift_row):
    average = jnp.mean(values, axis=-1, keepdims=True)
    centred = values - average
    inverse = lax.rsqrt(jnp.mean(centred * centred, axis=-1, keepdims=True) + 1e-05)
    normed = centred * inverse
    return (normed * gain_row + shift_row, normed, inverse)


def layer_norm_back(incoming, normed, inverse, gain_row):
    scaled = incoming * gain_row
    inner = (
        scaled
        - jnp.mean(scaled, axis=-1, keepdims=True)
        - normed * jnp.mean(scaled * normed, axis=-1, keepdims=True)
    )
    return (inner * inverse, jnp.sum(incoming * normed, axis=0), jnp.sum(incoming, axis=0))


def positions(segment_ids):
    length = segment_ids.shape[-1]
    indices = jnp.broadcast_to(jnp.arange(length, dtype=jnp.int32), segment_ids.shape)
    before = jnp.concatenate(
        [jnp.full(segment_ids.shape[:-1] + (1,), -1, jnp.int32), segment_ids[..., :-1]], axis=-1
    )
    starts = lax.cummax(jnp.where(segment_ids != before, indices, 0), axis=segment_ids.ndim - 1)
    return indices - starts


def rotary_tables(position_ids, float_type):
    half_rot = ROT // 2
    frequency = 10000.0 ** (-(2.0 * jnp.arange(half_rot, dtype=float_type)) / ROT)
    angles = position_ids.astype(float_type)[..., None] * frequency
    return (jnp.cos(angles)[..., None, :], jnp.sin(angles)[..., None, :])


def rotate(values, cosine, sine):
    half_rot = ROT // 2
    lower_half = values[..., :half_rot]
    upper_half = values[..., half_rot:ROT]
    return jnp.concatenate(
        [
            lower_half * cosine - upper_half * sine,
            upper_half * cosine + lower_half * sine,
            values[..., ROT:],
        ],
        axis=-1,
    )


def visible_mask(segment_row, offset, block_rows):
    length = segment_row.shape[0]
    query_ids = offset + jnp.arange(block_rows, dtype=jnp.int32)
    key_ids = jnp.arange(length, dtype=jnp.int32)
    query_segs = lax.dynamic_slice_in_dim(segment_row, offset, block_rows, 0)
    return (query_segs[:, None] == segment_row[None, :]) & (query_ids[:, None] >= key_ids[None, :])


def attention_forward(queries, keys, values, segment_row, block_rows):

    def one_block(number):
        offset = number * block_rows
        query_block = lax.dynamic_slice_in_dim(queries, offset, block_rows, 0)
        scores = (
            jnp.einsum("qhd,khd->hqk", query_block, keys, preferred_element_type=jnp.float32)
            * 0.125
        )
        scores = jnp.where(visible_mask(segment_row, offset, block_rows)[None], scores, -1e30)
        peak_value = jnp.max(scores, axis=-1, keepdims=True)
        exponent = jnp.exp(scores - peak_value)
        summed = jnp.sum(exponent, axis=-1, keepdims=True)
        weights_low = (exponent / summed).astype(jnp.bfloat16)
        context = jnp.einsum(
            "hqk,khd->qhd", weights_low, values, preferred_element_type=jnp.float32
        )
        return (context.astype(jnp.bfloat16), (peak_value + jnp.log(summed))[..., 0])

    context, log_totals = lax.map(
        one_block, jnp.arange(queries.shape[0] // block_rows, dtype=jnp.int32)
    )
    return (context.reshape(queries.shape), log_totals)


def attention_backward(queries, keys, values, segment_row, log_totals, context_grad, block_rows):

    def one_block(carried, number):
        key_grad, value_grad = carried
        offset = number * block_rows
        query_block = lax.dynamic_slice_in_dim(queries, offset, block_rows, 0)
        grad_block = lax.dynamic_slice_in_dim(context_grad, offset, block_rows, 0)
        scores = (
            jnp.einsum("qhd,khd->hqk", query_block, keys, preferred_element_type=jnp.float32)
            * 0.125
        )
        allowed = visible_mask(segment_row, offset, block_rows)[None]
        attention = jnp.where(allowed, jnp.exp(scores - log_totals[number][..., None]), 0.0)
        weight_grad = jnp.einsum(
            "qhd,khd->hqk", grad_block, values, preferred_element_type=jnp.float32
        )
        inner_sum = jnp.sum(attention * weight_grad, axis=-1, keepdims=True)
        score_grad = (attention * (weight_grad - inner_sum)).astype(jnp.bfloat16)
        query_grad = (
            jnp.einsum("hqk,khd->qhd", score_grad, keys, preferred_element_type=jnp.float32) * 0.125
        )
        key_grad = (
            key_grad
            + jnp.einsum(
                "hqk,qhd->khd", score_grad, query_block, preferred_element_type=jnp.float32
            )
            * 0.125
        )
        value_grad = value_grad + jnp.einsum(
            "hqk,qhd->khd",
            attention.astype(jnp.bfloat16),
            grad_block,
            preferred_element_type=jnp.float32,
        )
        return ((key_grad, value_grad), query_grad)

    zero_grad = jnp.zeros(keys.shape, jnp.float32)
    carried, query_grad = lax.scan(
        one_block,
        (zero_grad, zero_grad),
        jnp.arange(queries.shape[0] // block_rows, dtype=jnp.int32),
    )
    return (query_grad.reshape(queries.shape), carried[0], carried[1])


def adam_update(master, gradient, moment_one, moment_two, correct_one, correct_two, rate):
    one_new = 0.9 * moment_one + 0.1 * gradient
    two_new = 0.999 * moment_two + 0.001 * gradient * gradient
    change = one_new / correct_one / (jnp.sqrt(two_new / correct_two) + 1e-08) + 0.1 * master
    return (master - rate * change, one_new, two_new)


def per_device(
    inputs,
    out_grad,
    segments,
    w_qkv,
    w_out,
    w_gate_up,
    w_down,
    qkv_bias,
    norm_gain,
    norm_bias,
    first_qkv,
    first_out,
    first_gate_up,
    first_down,
    first_bias,
    first_gain,
    first_shift,
    second_qkv,
    second_out,
    second_gate_up,
    second_down,
    second_bias,
    second_gain,
    second_shift,
):
    low_type = jnp.bfloat16
    full_type = jnp.float32
    qkv_all, gate_up_all, out_all, down_all = (
        lax.all_gather(w_qkv.astype(low_type), "dp", axis=1, tiled=True),
        lax.all_gather(w_gate_up.astype(low_type), "dp", axis=1, tiled=True),
        lax.all_gather(w_out.astype(low_type), "dp", axis=1, tiled=True),
        lax.all_gather(w_down.astype(low_type), "dp", axis=1, tiled=True),
    )
    seq_count = segments.shape[0]
    length = segments.shape[1]
    total_rows = seq_count * length
    head_width = w_qkv.shape[2]
    heads_local = head_width // HD
    block_rows = min(512, length)
    inputs_full = inputs.astype(full_type)
    normed_one, plain_one, inverse_one = layer_norm_parts(inputs_full, norm_gain[0], norm_bias[0])
    normed_one = normed_one.astype(low_type)
    projected = jnp.einsum(
        "rd,cdh->rch",
        lax.all_gather(normed_one, "tensor", axis=0, tiled=True),
        qkv_all,
        preferred_element_type=full_type,
    )
    cosine, sine = rotary_tables(positions(segments), full_type)
    cosine = cosine.reshape(total_rows, 1, ROT // 2)
    sine = sine.reshape(total_rows, 1, ROT // 2)
    query_lin = (projected[:, 0] + qkv_bias[0]).reshape(total_rows, heads_local, HD)
    key_lin = (projected[:, 1] + qkv_bias[1]).reshape(total_rows, heads_local, HD)
    value_low = (
        (projected[:, 2] + qkv_bias[2]).astype(low_type).reshape(seq_count, length, heads_local, HD)
    )
    query_low = (
        rotate(query_lin, cosine, sine).astype(low_type).reshape(seq_count, length, heads_local, HD)
    )
    key_low = (
        rotate(key_lin, cosine, sine).astype(low_type).reshape(seq_count, length, heads_local, HD)
    )

    def forward_sequence(operands):
        return attention_forward(operands[0], operands[1], operands[2], operands[3], block_rows)

    context_low, log_totals = lax.map(forward_sequence, (query_low, key_low, value_low, segments))
    context_flat = context_low.reshape(total_rows, head_width)
    middle = inputs_full + lax.psum_scatter(
        jnp.dot(context_flat, out_all, preferred_element_type=full_type),
        "tensor",
        scatter_dimension=0,
        tiled=True,
    )
    normed_two, plain_two, inverse_two = layer_norm_parts(middle, norm_gain[1], norm_bias[1])
    normed_two = normed_two.astype(low_type)
    gate_pair = jnp.einsum(
        "rd,cdf->rcf",
        lax.all_gather(normed_two, "tensor", axis=0, tiled=True),
        gate_up_all,
        preferred_element_type=full_type,
    )
    gate_parts = (gate_pair,)
    gate_proj = gate_parts[0][:, 0]
    up_proj = gate_parts[0][:, 1]
    sigmoid_gate = jax.nn.sigmoid(gate_proj)
    activated = gate_proj * sigmoid_gate
    hidden_low = (activated * up_proj).astype(low_type)
    outputs = (
        middle
        + lax.psum_scatter(
            jnp.dot(hidden_low, down_all, preferred_element_type=full_type).astype(jnp.bfloat16),
            "tensor",
            scatter_dimension=0,
            tiled=True,
        ).astype(jnp.float32)
    ).astype(low_type)
    mlp_grad = lax.all_gather(out_grad, "tensor", axis=0, tiled=True)
    grad_down = jnp.einsum("rf,rd->fd", hidden_low, mlp_grad, preferred_element_type=full_type)
    hidden_grad = jnp.einsum("rd,fd->rf", mlp_grad, down_all, preferred_element_type=full_type)
    gate_grad = hidden_grad * up_proj * (sigmoid_gate * (1.0 + gate_proj * (1.0 - sigmoid_gate)))
    up_grad = hidden_grad * activated
    pair_grad = jnp.stack([gate_grad, up_grad], axis=1).astype(low_type)
    normed_two_grad = lax.psum_scatter(
        jnp.einsum("rcf,cdf->rd", pair_grad, gate_up_all, preferred_element_type=full_type),
        "tensor",
        scatter_dimension=0,
        tiled=True,
    )
    rows_grad = pair_grad
    grad_gate_up = jnp.einsum(
        "rd,rcf->cdf",
        lax.all_gather(normed_two, "tensor", axis=0, tiled=True),
        rows_grad,
        preferred_element_type=full_type,
    )
    middle_ln_grad, gain_two_grad, shift_two_grad = layer_norm_back(
        normed_two_grad, plain_two, inverse_two, norm_gain[1]
    )
    middle_grad = out_grad.astype(full_type) + middle_ln_grad
    attn_grad_all = lax.all_gather(middle_grad.astype(low_type), "tensor", axis=0, tiled=True)
    grad_out = jnp.einsum(
        "rh,rd->hd", context_flat, attn_grad_all, preferred_element_type=full_type
    )
    context_grad = jnp.einsum(
        "rd,hd->rh", attn_grad_all, out_all, preferred_element_type=full_type
    ).astype(low_type)
    context_grad = context_grad.reshape(seq_count, length, heads_local, HD)

    def backward_sequence(operands):
        return attention_backward(
            operands[0], operands[1], operands[2], operands[3], operands[4], operands[5], block_rows
        )

    query_rot_grad, key_rot_grad, value_grad = lax.map(
        backward_sequence, (query_low, key_low, value_low, segments, log_totals, context_grad)
    )
    query_grad = rotate(query_rot_grad.reshape(total_rows, heads_local, HD), cosine, -sine)
    key_grad = rotate(key_rot_grad.reshape(total_rows, heads_local, HD), cosine, -sine)
    triple_grad = jnp.stack(
        [query_grad, key_grad, value_grad.reshape(total_rows, heads_local, HD)], axis=1
    )
    triple_grad = triple_grad.astype(low_type).reshape(total_rows, 3, head_width)
    grad_bias = jnp.sum(triple_grad, axis=0, dtype=full_type)
    normed_one_grad = lax.psum_scatter(
        jnp.einsum("rch,cdh->rd", triple_grad, qkv_all, preferred_element_type=full_type).astype(
            jnp.bfloat16
        ),
        "tensor",
        scatter_dimension=0,
        tiled=True,
    ).astype(jnp.float32)
    rows_grad = triple_grad
    grad_qkv = jnp.einsum(
        "rd,rch->cdh",
        lax.all_gather(normed_one, "tensor", axis=0, tiled=True),
        rows_grad,
        preferred_element_type=full_type,
    )
    input_ln_grad, gain_one_grad, shift_one_grad = layer_norm_back(
        normed_one_grad, plain_one, inverse_one, norm_gain[0]
    )
    input_grad = (middle_grad + input_ln_grad).astype(low_type)
    grad_qkv, grad_gate_up, grad_out, grad_down = (
        lax.psum_scatter(
            grad_qkv.astype(jnp.bfloat16), "dp", scatter_dimension=1, tiled=True
        ).astype(jnp.float32),
        lax.psum_scatter(
            grad_gate_up.astype(jnp.bfloat16), "dp", scatter_dimension=1, tiled=True
        ).astype(jnp.float32),
        lax.psum_scatter(
            grad_out.astype(jnp.bfloat16), "dp", scatter_dimension=1, tiled=True
        ).astype(jnp.float32),
        lax.psum_scatter(
            grad_down.astype(jnp.bfloat16), "dp", scatter_dimension=1, tiled=True
        ).astype(jnp.float32),
    )
    grad_bias = lax.psum(grad_bias, "dp")
    grad_gain, grad_shift = lax.psum(
        (jnp.stack([gain_one_grad, gain_two_grad]), jnp.stack([shift_one_grad, shift_two_grad])),
        ("dp", "tensor"),
    )
    correct_one = 1.0 - 0.9**STEP
    correct_two = 1.0 - 0.999**STEP
    rates = (0.02, 0.3, 0.02, 0.02, 0.3, 0.3, 0.3)
    masters = (w_qkv, w_out, w_gate_up, w_down, qkv_bias, norm_gain, norm_bias)
    gradients = (grad_qkv, grad_out, grad_gate_up, grad_down, grad_bias, grad_gain, grad_shift)
    firsts = (first_qkv, first_out, first_gate_up, first_down, first_bias, first_gain, first_shift)
    seconds = (
        second_qkv,
        second_out,
        second_gate_up,
        second_down,
        second_bias,
        second_gain,
        second_shift,
    )
    updated = [
        adam_update(
            masters[number],
            gradients[number],
            firsts[number],
            seconds[number],
            correct_one,
            correct_two,
            rates[number],
        )
        for number in range(7)
    ]
    return (
        outputs,
        input_grad,
        grad_qkv,
        grad_out,
        grad_gate_up,
        grad_down,
        grad_bias,
        grad_gain,
        grad_shift,
        updated[0][0],
        updated[1][0],
        updated[2][0],
        updated[3][0],
        updated[4][0],
        updated[5][0],
        updated[6][0],
        updated[0][1],
        updated[1][1],
        updated[2][1],
        updated[3][1],
        updated[4][1],
        updated[5][1],
        updated[6][1],
        updated[0][2],
        updated[1][2],
        updated[2][2],
        updated[3][2],
        updated[4][2],
        updated[5][2],
        updated[6][2],
    )


def solution(mesh):
    in_specs = (
        P(("dp", "tensor"), None),
        P(("dp", "tensor"), None),
        P("dp", None),
        P(None, "dp", "tensor"),
        P("tensor", "dp"),
        P(None, "dp", "tensor"),
        P("tensor", "dp"),
        P(None, "tensor"),
        P(),
        P(),
        P(None, "dp", "tensor"),
        P("tensor", "dp"),
        P(None, "dp", "tensor"),
        P("tensor", "dp"),
        P(None, "tensor"),
        P(),
        P(),
        P(None, "dp", "tensor"),
        P("tensor", "dp"),
        P(None, "dp", "tensor"),
        P("tensor", "dp"),
        P(None, "tensor"),
        P(),
        P(),
    )
    out_specs = (
        P(("dp", "tensor"), None),
        P(("dp", "tensor"), None),
        P(None, "dp", "tensor"),
        P("tensor", "dp"),
        P(None, "dp", "tensor"),
        P("tensor", "dp"),
        P(None, "tensor"),
        P(),
        P(),
        P(None, "dp", "tensor"),
        P("tensor", "dp"),
        P(None, "dp", "tensor"),
        P("tensor", "dp"),
        P(None, "tensor"),
        P(),
        P(),
        P(None, "dp", "tensor"),
        P("tensor", "dp"),
        P(None, "dp", "tensor"),
        P("tensor", "dp"),
        P(None, "tensor"),
        P(),
        P(),
        P(None, "dp", "tensor"),
        P("tensor", "dp"),
        P(None, "dp", "tensor"),
        P("tensor", "dp"),
        P(None, "tensor"),
        P(),
        P(),
    )
    return jax.shard_map(
        per_device, mesh=mesh, in_specs=in_specs, out_specs=out_specs, check_vma=False
    )
```

profile of v0, /device:TPU:0, one launch (start us, length us, event | category | flops | bytes accessed | tf_op | source)
XLA Modules:
  0.0 1545.4 jit_solution(6390795264467794405)
XLA Ops:
  16.9 40.2 %all-gather.11.cloned.1.call-done = bf16[3,2048,256]{1,2,0:T(8,128)(2,1)} async-done(((bf16[3,512,256]{1,2,0:T(8,128)(2,1)}), bf16[3,2048,256]{1,2,0:T(8,128)(2,1)}) %all-gather.11.cloned.1.call-update) | async-done | bytes 3145744 | tf_op jit(solution)/shard_map/all_gather | solution.py:174
  57.1 84.3 %all-gather.9.cloned.1.call-done = bf16[2048,2048]{1,0:T(8,128)(2,1)} async-done(((bf16[256,2048]{1,0:T(8,128)(2,1)}), bf16[2048,2048]{1,0:T(8,128)(2,1)}) %all-gather.9.cloned.1.call-update) | async-done | bytes 8388624 | tf_op jit(solution)/shard_map/all_gather | solution.py:190
  141.3 10.1 fusion.44
  153.4 66.8 %while.47 = (s32[]{:T(128)}, bf16[4,512,4,64]{1,3,2,0:T(8,128)(2,1)}, f32[4,4,512]{2,1,0:T(4,128)}, s32[4]{0:T(128)S(1)}, s32[2048]{0:T(1024)S(1)}, /*index=5*/b...) while((s32[]{:T(128)}, ...), condition=%wide.region_7.8_spmd, body=%wide.region_4.7_spmd.sunk | while | flops 1127348736 | bytes 57231560 | solution.py:87
  159.2 4.3 fusion.145
  163.5 5.9 fusion.146
  175.8 4.3 fusion.145
  180.2 5.9 fusion.146
  192.5 4.3 fusion.145
  196.8 5.9 fusion.146
  209.1 4.3 fusion.145
  213.4 5.9 fusion.146
  224.3 9.7 fusion.97
  237.3 163.7 %reduce-scatter.9.cloned.1.call-done = f32[256,2048]{1,0:T(8,128)} async-done(((f32[2048,2048]{1,0:T(8,128)}), f32[256,2048]{1,0:T(8,128)}) %reduce-scatter.9.cloned.1.call-update) | async-done | bytes 2097168 | tf_op jit(solution)/shard_map/reduce_scatter | solution.py:214
  408.1 59.1 %all-gather.17.cloned.1.call-done = bf16[2,2048,704]{1,2,0:T(8,128)(2,1)} async-done(((bf16[2,512,704]{1,2,0:T(8,128)(2,1)}), bf16[2,2048,704]{1,2,0:T(8,128)(2,1)}) %all-gather.17.cloned.1.call-update) | async-done | bytes 5767184 | tf_op jit(solution)/shard_map/all_gather | solution.py:175
  467.2 84.1 %all-gather.15.cloned.1.call-done = bf16[2048,2048]{1,0:T(8,128)(2,1)} async-done(((bf16[256,2048]{1,0:T(8,128)(2,1)}), bf16[2048,2048]{1,0:T(8,128)(2,1)}) %all-gather.15.cloned.1.call-update) | async-done | bytes 8388624 | tf_op jit(solution)/shard_map/all_gather | solution.py:224
  551.3 18.8 %fusion.40 = f32[2048,2,704]{0,2,1:T(8,128)} fusion(bf16[2,2048,704]{1,2,0:T(8,128)(2,1)} %all-gather.17.cloned.1.call-done, bf16[2048,2048]{1,0:T(8,128)(2,1)} %all-gather.15.cloned.1.call-done), kind=kOutput, calls=%fused_computation.51 | convolution fusion | flops 11811160064 | bytes 25690112 | tf_op jit(solution)/shard_map/rd,cdf->rcf/dot_general | solution.py:222
  570.2 23.8 %all-gather.19.cloned.1.call-done = bf16[704,2048]{1,0:T(8,128)(2,1)} async-done(((bf16[704,512]{1,0:T(8,128)(2,1)}), bf16[704,2048]{1,0:T(8,128)(2,1)}) %all-gather.19.cloned.1.call-update) | async-done | bytes 2883600 | tf_op jit(solution)/shard_map/all_gather | solution.py:177
  594.0 83.7 %all-gather.21.cloned.1.call-done = bf16[2048,2048]{1,0:T(8,128)(2,1)} async-done(((bf16[256,2048]{1,0:T(8,128)(2,1)}), bf16[2048,2048]{1,0:T(8,128)(2,1)}) %all-gather.21.cloned.1.call-update) | async-done | bytes 8388624 | tf_op jit(solution)/shard_map/all_gather | solution.py:243
  677.7 15.0 fusion.60
  695.2 26.7 %convolution_bitcast_fusion = f32[2048,2048]{1,0:T(8,128)} fusion(bf16[2,2048,704]{1,2,0:T(8,128)(2,1)S(1)} %copy-done.54, bf16[2048,1,704]{0,2,1:T(8,128)(2,1)S(1)} %get-tuple-element.368, bf16[2048,1,704]{0,2,1:T(8,128)(2,1)S(1)} %get-tuple-element.367), kind=kOutput, calls=%fused_computation.48 | convolution fusion | flops 11814043648 | bytes 28311552 | tf_op jit(solution)/shard_map/rcf,cdf->rd/dot_general | solution.py:250
  722.0 11.3 convolution_convert_fusion
  733.4 155.5 %reduce-scatter.13.cloned.1.call-done = f32[256,2048]{1,0:T(8,128)} async-done(((f32[2048,2048]{1,0:T(8,128)}), f32[256,2048]{1,0:T(8,128)}) %reduce-scatter.13.cloned.1.call-update) | async-done | bytes 2097168 | tf_op jit(solution)/shard_map/reduce_scatter | solution.py:249
  892.0 87.0 %reduce-scatter.11.cloned.1.call-done = bf16[256,2048]{1,0:T(8,128)(2,1)} async-done(((bf16[2048,2048]{1,0:T(8,128)(2,1)}), bf16[256,2048]{1,0:T(8,128)(2,1)}) %reduce-scatter.11.cloned.1.call-update) | async-done | bytes 1048592 | tf_op jit(solution)/shard_map/reduce_scatter | solution.py:236
  979.0 5.3 fusion.92
  984.4 10.5 convolution_convert_fusion.1
  995.0 17.9 %convert_bitcast_fusion = bf16[2,2048,704]{1,2,0:T(8,128)(2,1)} fusion(bf16[2048,2048]{1,0:T(8,128)(2,1)} %all-gather.15.cloned.1.call-done, bf16[2048,1,704]{0,2,1:T(8,128)(2,1)} %copy-done.56, bf16[2048,1,704]{0,2,1:T(8,128)(2,1)} %copy-done.55), kind=kOutput, calls=%fused_computation.62 | convolution fusion | flops 11816927232 | bytes 19922944 | tf_op jit(solution)/shard_map/rd,rcf->cdf/dot_general | solution.py:256
  1013.0 51.9 %all-gather.23.cloned.1.call-done = bf16[2048,2048]{1,0:T(8,128)(2,1)} async-done(((bf16[256,2048]{1,0:T(8,128)(2,1)}), bf16[2048,2048]{1,0:T(8,128)(2,1)}) %all-gather.23.cloned.1.call-update) | async-done | bytes 8388624 | tf_op jit(solution)/shard_map/all_gather | solution.py:266
  1064.9 6.7 convolution_convert_fusion.3
  1071.6 245.2 %while.48 = (s32[]{:T(128)}, f32[2048,4,64]{0,2,1:T(8,128)}, f32[2048,4,64]{0,2,1:T(8,128)}, f32[4,512,4,64]{1,0,3,2:T(4,128)}, s32[4]{0:T(128)S(1)}, /*index=5*...) while((s32[]{:T(128)}, f32[2048,4,64]{0,2,1:T(8,128)}, ...), condition=%wide.region_17.18_spmd.clone, body=%wide.region_15.17_spmd.clone.sunk | while | flops 2753165824 | bytes 183118224 | solution.py:130
  1080.6 6.9 fusion.159
  1087.5 11.6 multiply_reduce_fusion.6
  1099.1 11.2 multiply_convert_fusion.5
  1110.3 6.2 fusion.160
  1116.5 3.9 fusion.158
  1121.0 11.2 dynamic_update_slice.33
  1140.9 7.3 fusion.159
  1148.2 12.0 multiply_reduce_fusion.6
  1160.2 11.2 multiply_convert_fusion.5
  1171.4 6.3 fusion.160
  1177.7 4.6 fusion.158
  1182.9 11.1 dynamic_update_slice.33
  1202.7 7.3 fusion.159
  1210.0 11.6 multiply_reduce_fusion.6
  1221.6 11.2 multiply_convert_fusion.5
  1232.7 6.2 fusion.160
  1238.9 4.6 fusion.158
  1244.1 11.1 dynamic_update_slice.33
  1264.0 7.3 fusion.159
  1271.2 11.6 multiply_reduce_fusion.6
  1282.8 11.2 multiply_convert_fusion.5
  1294.0 6.2 fusion.160
  1300.2 4.6 fusion.158
  1305.4 11.1 dynamic_update_slice.33
  1320.6 6.8 convolution_convert_fusion.2
  1336.1 10.8 fusion.52
  1348.1 11.0 bitcast_convert_fusion
  1365.3 5.0 multiply_subtract_fusion.2
  1370.3 9.6 multiply_subtract_fusion
  1380.5 10.4 psum.21
  1394.3 7.6 reduce-scatter.17.cloned.1.call-done
  1401.9 5.2 multiply_subtract_fusion.1
  1417.8 76.0 %reduce-scatter.15.cloned.1.call-done = bf16[256,2048]{1,0:T(8,128)(2,1)} async-done(((bf16[2048,2048]{1,0:T(8,128)(2,1)}), bf16[256,2048]{1,0:T(8,128)(2,1)}) %reduce-scatter.15.cloned.1.call-update) | async-done | bytes 1048592 | tf_op jit(solution)/shard_map/reduce_scatter | solution.py:290
  1496.1 38.0 %all-reduce = (f32[2,2048]{1,0:T(2,128)S(1)}, f32[2,2048]{1,0:T(2,128)S(1)}) all-reduce(f32[2,2048]{1,0:T(2,128)S(1)} %pad_maximum_fusion.8, f32[2,2048]{1,0:T(2,128)S(1)} %pad_maximum_fusion.9), channel_id=1, replica_groups=mesh['dp'=4,'tensor'=8] {'dp','tensor'}, use_global_device_ids=true, to_apply=%region_29.30 | all-reduce | flops 8192 | bytes 65536 | tf_op jit(solution)/shard_map/psum | solution.py:324
  (303 shorter events, 122.0 us)
Async XLA Ops:
  7.2 49.9 %all-gather.11.cloned.1.call-start = ((), (), s32[]{:S(2)}) async-start(), calls=%async_computation.9 | async-start | bytes 3932160 | tf_op jit(solution)/shard_map/all_gather | solution.py:174
  9.2 4.6 copy-start.7
  10.4 131.0 %all-gather.9.cloned.1.call-start = ((), (), s32[]{:S(2)}) async-start(), calls=%async_computation.8 | async-start | bytes 9437184 | tf_op jit(solution)/shard_map/all_gather | solution.py:190
  10.7 4.4 copy-start.22
  13.9 210.4 %all-gather.13.cloned.1.call-start = ((), (), s32[]{:S(2)}) async-start(), calls=%async_computation.10 | async-start | bytes 1310720 | tf_op jit(solution)/shard_map/all_gather | solution.py:176
  14.7 386.3 %reduce-scatter.9.cloned.1.call-start = ((), (), s32[]{:S(2)}) async-start(), calls=%async_computation.11 | async-start | bytes 18874368 | tf_op jit(solution)/shard_map/reduce_scatter | solution.py:214
  16.9 136.2 %copy-start.26 = (f32[2048,8]{0,1:T(8,128)}, f32[2048,8]{0,1:T(8,128)S(1)}, u32[]{:S(2)}) copy-start(f32[2048,8]{0,1:T(8,128)S(1)} %get-tuple-element.392) | copy-start | bytes 196612
  220.2 13.7 copy-start.3
  220.3 13.7 copy-start.6
  234.0 233.2 %all-gather.17.cloned.1.call-start = ((), (), s32[]{:S(2)}) async-start(), calls=%async_computation.13 | async-start | bytes 7208960 | tf_op jit(solution)/shard_map/all_gather | solution.py:175
  237.2 166.3 %copy-start.31 = (f32[1,2048]{1,0:T(1,128)S(1)}, f32[1,2048]{1,0:T(1,128)}, u32[]{:S(2)}) copy-start(f32[1,2048]{1,0:T(1,128)} %get-tuple-element.386) | copy-start | bytes 24580
  237.2 166.3 %copy-start.38 = (f32[1,2048]{1,0:T(1,128)S(1)}, f32[1,2048]{1,0:T(1,128)}, u32[]{:S(2)}) copy-start(f32[1,2048]{1,0:T(1,128)} %get-tuple-element.388) | copy-start | bytes 24580
  237.2 314.1 %all-gather.15.cloned.1.call-start = ((), (), s32[]{:S(2)}) async-start(), calls=%async_computation.12 | async-start | bytes 9437184 | tf_op jit(solution)/shard_map/all_gather | solution.py:224
  404.9 189.0 %all-gather.19.cloned.1.call-start = ((), (), s32[]{:S(2)}) async-start(), calls=%async_computation.14 | async-start | bytes 3604480 | tf_op jit(solution)/shard_map/all_gather | solution.py:177
  407.3 270.3 %all-gather.21.cloned.1.call-start = ((), (), s32[]{:S(2)}) async-start(), calls=%async_computation.16 | async-start | bytes 9437184 | tf_op jit(solution)/shard_map/all_gather | solution.py:243
  408.1 480.8 %reduce-scatter.13.cloned.1.call-start = ((), (), s32[]{:S(2)}) async-start(), calls=%async_computation.17 | async-start | bytes 18874368 | tf_op jit(solution)/shard_map/reduce_scatter | solution.py:249
  677.7 17.5 %copy-start.54 = (bf16[2,2048,704]{1,2,0:T(8,128)(2,1)S(1)}, bf16[2,2048,704]{1,2,0:T(8,128)(2,1)}, u32[]{:S(2)}) copy-start(bf16[2,2048,704]{1,2,0:T(8,128)(2,1)} %all-gather.17.cloned.1.call-done) | copy-start | bytes 17301508
  721.9 257.1 %reduce-scatter.11.cloned.1.call-start = ((), (), s32[]{:S(2)}) async-start(), calls=%async_computation.15 | async-start | bytes 9437184 | tf_op jit(solution)/shard_map/reduce_scatter | solution.py:236
  733.3 331.6 %all-gather.23.cloned.1.call-start = ((), (), s32[]{:S(2)}) async-start(), calls=%async_computation.18 | async-start | bytes 9437184 | tf_op jit(solution)/shard_map/all_gather | solution.py:266
  984.3 380.9 %reduce-scatter.23.cloned.1.call-start = ((), (), s32[]{:S(2)}) async-start(), calls=%async_computation.23 | async-start | bytes 3604480 | tf_op jit(solution)/shard_map/reduce_scatter | solution.py:319
  994.9 375.3 %reduce-scatter.21.cloned.1.call-start = ((), (), s32[]{:S(2)}) async-start(), calls=%async_computation.22 | async-start | bytes 7208960 | tf_op jit(solution)/shard_map/reduce_scatter | solution.py:313
  1012.9 52.0 %copy-start.25 = (bf16[256,2048]{1,0:T(8,128)(2,1)S(1)}, bf16[256,2048]{1,0:T(8,128)(2,1)}, u32[]{:S(2)}) copy-start(bf16[256,2048]{1,0:T(8,128)(2,1)} %all-gather.13.cloned.1.call-done) | copy-start | bytes 3145732
  1013.0 378.6 %reduce-scatter.19.cloned.1.call-start = ((), (), s32[]{:S(2)}) async-start(), calls=%async_computation.21 | async-start | bytes 1310720 | tf_op jit(solution)/shard_map/reduce_scatter | solution.py:316
  1110.3 6.2 copy-start
  1116.5 15.6 %copy-start.24 = (s32[2048]{0:T(1024)S(1)}, s32[2048]{0:T(1024)}, u32[]{:S(2)}) copy-start(s32[2048]{0:T(1024)} %copy-done.23) | copy-start | bytes 24580 | tf_op jit(solution)/shard_map/while/body/eval_jaxpr/while
  1171.4 6.3 copy-start
  1177.7 16.3 %copy-start.24 = (s32[2048]{0:T(1024)S(1)}, s32[2048]{0:T(1024)}, u32[]{:S(2)}) copy-start(s32[2048]{0:T(1024)} %copy-done.23) | copy-start | bytes 24580 | tf_op jit(solution)/shard_map/while/body/eval_jaxpr/while
  1232.7 6.2 copy-start
  1238.9 16.3 %copy-start.24 = (s32[2048]{0:T(1024)S(1)}, s32[2048]{0:T(1024)}, u32[]{:S(2)}) copy-start(s32[2048]{0:T(1024)} %copy-done.23) | copy-start | bytes 24580 | tf_op jit(solution)/shard_map/while/body/eval_jaxpr/while
  1294.0 6.2 copy-start
  1300.2 16.3 %copy-start.24 = (s32[2048]{0:T(1024)S(1)}, s32[2048]{0:T(1024)}, u32[]{:S(2)}) copy-start(s32[2048]{0:T(1024)} %copy-done.23) | copy-start | bytes 24580 | tf_op jit(solution)/shard_map/while/body/eval_jaxpr/while
  1320.6 6.9 copy-start.2
  1320.6 6.9 copy-start.27
  1320.6 6.9 copy-start.28
  1327.5 74.4 %reduce-scatter.17.cloned.1.call-start = ((), (), s32[]{:S(2)}) async-start(), calls=%async_computation.20 | async-start | bytes 3932160 | tf_op jit(solution)/shard_map/reduce_scatter | solution.py:310
  1331.9 15.0 copy-start.13
  1332.6 14.4 copy-start.15
  1346.9 146.9 %reduce-scatter.15.cloned.1.call-start = ((), (), s32[]{:S(2)}) async-start(), calls=%async_computation.19 | async-start | bytes 9437184 | tf_op jit(solution)/shard_map/reduce_scatter | solution.py:290
  1359.1 6.2 copy-start.11
  1370.3 9.6 copy-start.14
  1370.3 9.6 copy-start.16
  1370.3 9.6 copy-start.18
  1379.9 10.9 copy-start.51
  1379.9 10.9 copy-start.52
  1379.9 10.9 copy-start.53
  1380.0 11.6 copy-start.21
  1380.0 21.9 %copy-start.8 = (f32[3,512,256]{1,2,0:T(8,128)S(1)}, f32[3,512,256]{1,2,0:T(8,128)}, u32[]{:S(2)}) copy-start(f32[3,512,256]{1,2,0:T(8,128)} %copy-done.7) | copy-start | bytes 4718596
  1390.9 16.1 %copy-start.49 = (f32[3,256]{1,0:T(4,128)}, f32[3,256]{1,0:T(4,128)S(1)}, u32[]{:S(2)}) copy-start(f32[3,256]{1,0:T(4,128)S(1)} %psum.21) | copy-start | bytes 9220
  1407.0 6.3 copy-start.10
  1413.4 80.4 %copy-start.5 = (bf16[256,2048]{1,0:T(8,128)(2,1)S(1)}, bf16[256,2048]{1,0:T(8,128)(2,1)}, u32[]{:S(2)}) copy-start(bf16[256,2048]{1,0:T(8,128)(2,1)} %param.28) | copy-start | bytes 3145732
  1413.4 80.4 %copy-start.30 = (f32[1,2048]{1,0:T(1,128)S(1)}, f32[1,2048]{1,0:T(1,128)}, u32[]{:S(2)}) copy-start(f32[1,2048]{1,0:T(1,128)} %copy-done.29) | copy-start | bytes 24580
  1413.4 80.4 %copy-start.40 = (f32[256]{0:T(256)S(1)}, f32[256]{0:T(256)}, u32[]{:S(2)}) copy-start(f32[256]{0:T(256)} %copy-done.39) | copy-start | bytes 3076
  1413.4 80.4 %copy-start.42 = (f32[256]{0:T(256)S(1)}, f32[256]{0:T(256)}, u32[]{:S(2)}) copy-start(f32[256]{0:T(256)} %copy-done.41) | copy-start | bytes 3076
  1415.0 81.1 %copy-start.37 = (f32[2048]{0:T(1024)S(1)}, f32[2048]{0:T(1024)}, u32[]{:S(2)}) copy-start(f32[2048]{0:T(1024)} %get-tuple-element.284) | copy-start | bytes 24580
  1415.0 81.1 %copy-start.36 = (f32[2048]{0:T(1024)S(1)}, f32[2048]{0:T(1024)}, u32[]{:S(2)}) copy-start(f32[2048]{0:T(1024)} %get-tuple-element.289) | copy-start | bytes 24580
  1415.0 119.2 %copy-start.33 = (f32[2,2048]{1,0:T(2,128)S(1)}, f32[2,2048]{1,0:T(2,128)}, u32[]{:S(2)}) copy-start(f32[2,2048]{1,0:T(2,128)} %param.36) | copy-start | bytes 49156
  1415.0 119.2 %copy-start.43 = (f32[2,2048]{1,0:T(2,128)S(1)}, f32[2,2048]{1,0:T(2,128)}, u32[]{:S(2)}) copy-start(f32[2,2048]{1,0:T(2,128)} %param.43) | copy-start | bytes 49156
  1415.0 119.2 %copy-start.44 = (f32[2,2048]{1,0:T(2,128)S(1)}, f32[2,2048]{1,0:T(2,128)}, u32[]{:S(2)}) copy-start(f32[2,2048]{1,0:T(2,128)} %param.50) | copy-start | bytes 49156
  1415.0 119.9 %copy-start.35 = (f32[2,2048]{1,0:T(2,128)S(1)}, f32[2,2048]{1,0:T(2,128)}, u32[]{:S(2)}) copy-start(f32[2,2048]{1,0:T(2,128)} %param.37) | copy-start | bytes 49156
  1415.0 119.9 %copy-start.45 = (f32[2,2048]{1,0:T(2,128)S(1)}, f32[2,2048]{1,0:T(2,128)}, u32[]{:S(2)}) copy-start(f32[2,2048]{1,0:T(2,128)} %param.44) | copy-start | bytes 49156
  1415.0 119.9 %copy-start.46 = (f32[2,2048]{1,0:T(2,128)S(1)}, f32[2,2048]{1,0:T(2,128)}, u32[]{:S(2)}) copy-start(f32[2,2048]{1,0:T(2,128)} %param.51) | copy-start | bytes 49156
  1415.0 120.5 %copy-start.9 = (f32[256,2048]{1,0:T(8,128)S(1)}, f32[256,2048]{1,0:T(8,128)}, u32[]{:S(2)}) copy-start(f32[256,2048]{1,0:T(8,128)} %get-tuple-element.360) | copy-start | bytes 6291460
  1534.2 4.5 copy-start.47
  1534.2 4.5 copy-start.48
  (21 other events, 60.4 us)
Sparse Core Ops, SparseCore 0:
  10.5 46.5 all-gather.10
  59.3 82.0 all-gather.8
  143.8 25.0 all-gather.12
  234.1 166.7 reduce-scatter.8
  403.2 63.9 all-gather.16
  469.2 82.0 all-gather.14
  553.7 40.1 all-gather.18
  595.6 82.0 all-gather.20
  722.1 166.7 reduce-scatter.12
  891.0 87.9 reduce-scatter.10
  984.5 80.3 all-gather.22
  1068.4 40.2 reduce-scatter.22
  1111.7 65.8 reduce-scatter.20
  1327.6 27.1 reduce-scatter.18
  1357.9 43.9 reduce-scatter.16
  1404.1 89.5 reduce-scatter.14
where the time goes:
time: 1560 us; the launch traced here: 1550 us
  waiting for transfers between devices  918 us (59%)
  matrix products  324 us (21%)
  other arithmetic  132 us (8%)
  local copies, waits for them, and re-layouts  92.9 us (6%)
  blocking collectives  48.4 us (3%)
    reduce_scatter x1, waiting for transfers between devices, per_device(): lax.psum_scatter(jnp.dot(context_flat, out_all, preferred_element_type=fu...  164 us
    reduce_scatter x1, waiting for transfers between devices, per_device(): lax.psum_scatter(jnp.einsum('rcf,cdf->rd', pair_grad, gate_up_all, prefer...  155 us
    reduce_scatter x1, waiting for transfers between devices, per_device(): lax.psum_scatter(jnp.dot(hidden_low, down_all, preferred_element_type=ful...  87 us
    all_gather x1, waiting for transfers between devices, per_device(): lax.all_gather(normed_one, 'tensor', axis=0, tiled=True)  84.3 us
    all_gather x1, waiting for transfers between devices, per_device(): lax.all_gather(normed_two, 'tensor', axis=0, tiled=True)  84.1 us
    all_gather x1, waiting for transfers between devices, per_device(): mlp_grad = lax.all_gather(out_grad, 'tensor', axis=0, tiled=True)  83.7 us
    reduce_scatter x1, waiting for transfers between devices, per_device(): lax.psum_scatter(jnp.einsum('rch,cdh->rd', triple_grad, qkv_all, preferre...  76 us
    all_gather x1, waiting for transfers between devices, per_device(): lax.all_gather(w_gate_up.astype(low_type), 'dp', axis=1, tiled=True)  59.1 us
  transfers between devices with their start and end apart: 16, of which 12 were waited for; matrix products, arithmetic and copies ran while one was open for 31% of the time, Pallas kernels for 0%

commit v1 on v0

--- a/solution.py
+++ b/solution.py
@@ -1,6 +1,8 @@
 import jax
 import jax.numpy as jnp
 from jax import lax
+from jax.experimental import pallas as pl
+from jax.experimental.pallas import tpu as pltpu
 from jax.sharding import PartitionSpec as P
 
 HD = 64
@@ -36,103 +38,277 @@
     return indices - starts
 
 
-def rotary_tables(position_ids, float_type):
+def rotary_tables(position_ids, width):
     half_rot = ROT // 2
-    frequency = 10000.0 ** (-(2.0 * jnp.arange(half_rot, dtype=float_type)) / ROT)
-    angles = position_ids.astype(float_type)[..., None] * frequency
-    return (jnp.cos(angles)[..., None, :], jnp.sin(angles)[..., None, :])
-
-
-def rotate(values, cosine, sine):
-    half_rot = ROT // 2
-    lower_half = values[..., :half_rot]
-    upper_half = values[..., half_rot:ROT]
-    return jnp.concatenate(
-        [
-            lower_half * cosine - upper_half * sine,
-            upper_half * cosine + lower_half * sine,
-            values[..., ROT:],
+    frequency = 10000.0 ** (-(2.0 * jnp.arange(half_rot, dtype=jnp.float32)) / ROT)
+    angles = position_ids.astype(jnp.float32)[:, None] * frequency
+    cosine, sine = jnp.cos(angles), jnp.sin(angles)
+    zeros = jnp.zeros((angles.shape[0], HD - ROT), jnp.float32)
+    blank = jnp.zeros_like(sine)
+    copies = width // HD
+    return tuple(
+        jnp.tile(jnp.concatenate(parts, axis=1), (1, copies))
+        for parts in (
+            (cosine, cosine, zeros + 1.0),
+            (-sine, blank, zeros),
+            (blank, sine, zeros),
+        )
+    )
+
+
+def rope_whole(values, tables):
+    cosine, sine_low, sine_high = tables
+    ahead = jnp.roll(values, -(ROT // 2), axis=1)
+    behind = jnp.roll(values, ROT // 2, axis=1)
+    return values * cosine + ahead * sine_low + behind * sine_high
+
+
+NEG = -1e30
+BLK = 256
+NT = (((1,), (1,)), ((), ()))
+NN = (((1,), (0,)), ((), ()))
+
+
+def dot(left, right, dims=NN, precision=None):
+    return lax.dot_general(
+        left, right, dims, preferred_element_type=jnp.float32, precision=precision
+    )
+
+
+def head_masks(width, dtype):
+    lane = lax.broadcasted_iota(jnp.int32, (1, width), 1)
+    return [(lane // HD == h).astype(dtype) for h in range(width // HD)]
+
+
+def rope_tile(tile, cosine, sine_low, sine_high, sign):
+    width = tile.shape[-1]
+    ahead = pltpu.roll(tile, width - ROT // 2, 1)
+    behind = pltpu.roll(tile, ROT // 2, 1)
+    return tile * cosine + sign * (ahead * sine_low + behind * sine_high)
+
+
+def forward_kernel(low_ref, q_ref, k_ref, v_ref, start_ref, ctx_ref, lse_ref, v_turned, acc, stats):
+    block = pl.program_id(0)
+    length, width = k_ref.shape
+    heads = width // HD
+
+    @pl.when(block == 0)
+    def _():
+        for part in range(length // BLK):
+            rows = slice(part * BLK, (part + 1) * BLK)
+            v_turned[:, rows] = v_ref[rows, :].T
+
+    queries = q_ref[pl.ds(pl.multiple_of(block * BLK, BLK), BLK), :] * 0.125
+    queries = queries.astype(jnp.bfloat16)
+    masked = [queries * m for m in head_masks(width, jnp.bfloat16)]
+    start = start_ref[...]
+    query_ids = block * BLK + lax.broadcasted_iota(jnp.int32, (1, BLK), 1)
+    acc[...] = jnp.zeros_like(acc)
+    stats[0:8, :] = jnp.full((8, BLK), NEG, jnp.float32)
+    stats[8:16, :] = jnp.zeros((8, BLK), jnp.float32)
+
+    def step(number, _):
+        base = pl.multiple_of(number * BLK, BLK)
+        keys = k_ref[pl.ds(base, BLK), :]
+        key_ids = base + lax.broadcasted_iota(jnp.int32, (BLK, BLK), 0)
+        visible = (key_ids >= start) & (key_ids <= query_ids)
+        for h in range(heads):
+            scores = jnp.where(visible, dot(keys, masked[h], NT), NEG)
+            peak_old = stats[h : h + 1, :]
+            peak = jnp.maximum(peak_old, jnp.max(scores, axis=0, keepdims=True))
+            fade = jnp.exp(peak_old - peak)
+            prob = jnp.exp(scores - peak)
+            stats[h : h + 1, :] = peak
+            stats[8 + h : 9 + h, :] = stats[8 + h : 9 + h, :] * fade + jnp.sum(
+                prob, axis=0, keepdims=True
+            )
+            rows = slice(h * HD, (h + 1) * HD)
+            acc[rows, :] = acc[rows, :] * fade + dot(
+                v_turned[rows, pl.ds(base, BLK)], prob.astype(jnp.bfloat16)
+            )
+        return 0
+
+    lax.fori_loop(low_ref[block], block + 1, step, 0)
+    for h in range(heads):
+        rows = slice(h * HD, (h + 1) * HD)
+        acc[rows, :] = acc[rows, :] / stats[8 + h : 9 + h, :]
+    ctx_ref[...] = acc[...].T.astype(ctx_ref.dtype)
+    total = jnp.where(stats[8:16, :] > 0, stats[8:16, :], 1.0)
+    lse_ref[...] = stats[0:8, :] + jnp.log(total)
+
+
+def attention_forward(low_blocks, queries, keys, values, start):
+    length, width = queries.shape
+    whole = pl.BlockSpec((length, width), lambda i, low: (0, 0))
+    return pl.pallas_call(
+        forward_kernel,
+        grid_spec=pltpu.PrefetchScalarGridSpec(
+            num_scalar_prefetch=1,
+            grid=(length // BLK,),
+            in_specs=[whole, whole, whole, pl.BlockSpec((1, BLK), lambda i, low: (0, i))],
+            out_specs=[
+                pl.BlockSpec((BLK, width), lambda i, low: (i, 0)),
+                pl.BlockSpec((8, BLK), lambda i, low: (0, i)),
+            ],
+            scratch_shapes=[
+                pltpu.VMEM((width, length), jnp.bfloat16),
+                pltpu.VMEM((width, BLK), jnp.float32),
+                pltpu.VMEM((16, BLK), jnp.float32),
+            ],
+        ),
+        out_shape=[
+            jax.ShapeDtypeStruct((length, width), jnp.bfloat16),
+            jax.ShapeDtypeStruct((8, length), jnp.float32),
         ],
-        axis=-1,
-    )
-
-
-def visible_mask(segment_row, offset, block_rows):
-    length = segment_row.shape[0]
-    query_ids = offset + jnp.arange(block_rows, dtype=jnp.int32)
-    key_ids = jnp.arange(length, dtype=jnp.int32)
-    query_segs = lax.dynamic_slice_in_dim(segment_row, offset, block_rows, 0)
-    return (query_segs[:, None] == segment_row[None, :]) & (query_ids[:, None] >= key_ids[None, :])
-
-
-def attention_forward(queries, keys, values, segment_row, block_rows):
-
-    def one_block(number):
-        offset = number * block_rows
-        query_block = lax.dynamic_slice_in_dim(queries, offset, block_rows, 0)
-        scores = (
-            jnp.einsum("qhd,khd->hqk", query_block, keys, preferred_element_type=jnp.float32)
-            * 0.125
-        )
-        scores = jnp.where(visible_mask(segment_row, offset, block_rows)[None], scores, -1e30)
-        peak_value = jnp.max(scores, axis=-1, keepdims=True)
-        exponent = jnp.exp(scores - peak_value)
-        summed = jnp.sum(exponent, axis=-1, keepdims=True)
-        weights_low = (exponent / summed).astype(jnp.bfloat16)
-        context = jnp.einsum(
-            "hqk,khd->qhd", weights_low, values, preferred_element_type=jnp.float32
-        )
-        return (context.astype(jnp.bfloat16), (peak_value + jnp.log(summed))[..., 0])
-
-    context, log_totals = lax.map(
-        one_block, jnp.arange(queries.shape[0] // block_rows, dtype=jnp.int32)
-    )
-    return (context.reshape(queries.shape), log_totals)
-
-
-def attention_backward(queries, keys, values, segment_row, log_totals, context_grad, block_rows):
-
-    def one_block(carried, number):
-        key_grad, value_grad = carried
-        offset = number * block_rows
-        query_block = lax.dynamic_slice_in_dim(queries, offset, block_rows, 0)
-        grad_block = lax.dynamic_slice_in_dim(context_grad, offset, block_rows, 0)
-        scores = (
-            jnp.einsum("qhd,khd->hqk", query_block, keys, preferred_element_type=jnp.float32)
-            * 0.125
-        )
-        allowed = visible_mask(segment_row, offset, block_rows)[None]
-        attention = jnp.where(allowed, jnp.exp(scores - log_totals[number][..., None]), 0.0)
-        weight_grad = jnp.einsum(
-            "qhd,khd->hqk", grad_block, values, preferred_element_type=jnp.float32
-        )
-        inner_sum = jnp.sum(attention * weight_grad, axis=-1, keepdims=True)
-        score_grad = (attention * (weight_grad - inner_sum)).astype(jnp.bfloat16)
-        query_grad = (
-            jnp.einsum("hqk,khd->qhd", score_grad, keys, preferred_element_type=jnp.float32) * 0.125
-        )
-        key_grad = (
-            key_grad
-            + jnp.einsum(
-                "hqk,qhd->khd", score_grad, query_block, preferred_element_type=jnp.float32
+        compiler_params=pltpu.CompilerParams(vmem_limit_bytes=32 << 20),
+        name="attention_forward",
+    )(low_blocks, queries, keys, values, start)
+
+
+def backward_kernel(
+    low_ref,
+    q_ref,
+    k_ref,
+    v_ref,
+    start_ref,
+    lse_ref,
+    ctx_ref,
+    grad_ref,
+    cos_ref,
+    sin_low_ref,
+    sin_high_ref,
+    dq_ref,
+    dk_ref,
+    dv_ref,
+    bias_ref,
+    k_turned,
+    dq_acc,
+    dk_acc,
+    dv_acc,
+):
+    block = pl.program_id(0)
+    last = pl.num_programs(0) - 1
+    length, width = k_ref.shape
+    heads = width // HD
+    tile = min(width, 128)
+
+    @pl.when(block == 0)
+    def _():
+        for part in range(length // BLK):
+            rows = slice(part * BLK, (part + 1) * BLK)
+            k_turned[:, rows] = k_ref[rows, :].T
+        dk_acc[...] = jnp.zeros_like(dk_acc)
+        dv_acc[...] = jnp.zeros_like(dv_acc)
+        bias_ref[...] = jnp.zeros_like(bias_ref)
+
+    here = pl.ds(pl.multiple_of(block * BLK, BLK), BLK)
+    masks = head_masks(width, jnp.bfloat16)
+    queries = (q_ref[here, :] * 0.125).astype(jnp.bfloat16)
+    masked = [queries * m for m in masks]
+    grads = grad_ref[...]
+    grads_masked = [grads * m for m in masks]
+    product = grads.astype(jnp.float32) * ctx_ref[...].astype(jnp.float32)
+    select = (
+        lax.broadcasted_iota(jnp.int32, (8, width), 1) // HD
+        == lax.broadcasted_iota(jnp.int32, (8, width), 0)
+    ).astype(jnp.float32)
+    delta = dot(select, product, NT, lax.Precision.HIGHEST)
+    start = start_ref[...]
+    query_ids = block * BLK + lax.broadcasted_iota(jnp.int32, (1, BLK), 1)
+    dq_acc[...] = jnp.zeros_like(dq_acc)
+
+    def step(number, _):
+        base = pl.multiple_of(number * BLK, BLK)
+        rows_k = pl.ds(base, BLK)
+        keys = k_ref[rows_k, :]
+        vals = v_ref[rows_k, :]
+        key_ids = base + lax.broadcasted_iota(jnp.int32, (BLK, BLK), 0)
+        visible = (key_ids >= start) & (key_ids <= query_ids)
+        dk = dk_acc[rows_k, :]
+        dv = dv_acc[rows_k, :]
+        for h in range(heads):
+            scores = dot(keys, masked[h], NT)
+            prob = jnp.where(visible, jnp.exp(scores - lse_ref[h : h + 1, :]), 0.0)
+            dprob = dot(vals, grads_masked[h], NT)
+            dscore = (prob * (dprob - delta[h : h + 1, :])).astype(jnp.bfloat16)
+            dv = dv + dot(prob.astype(jnp.bfloat16), grads_masked[h])
+            dk = dk + dot(dscore, masked[h])
+            rows = slice(h * HD, (h + 1) * HD)
+            dq_acc[rows, :] += dot(k_turned[rows, rows_k], dscore)
+        dk_acc[rows_k, :] = dk
+        dv_acc[rows_k, :] = dv
+        return 0
+
+    lax.fori_loop(low_ref[block], block + 1, step, 0)
+
+    def turn_back(values, rows):
+        parts = []
+        for t in range(width // tile):
+            parts.append(
+                rope_tile(
+                    values[:, t * tile : (t + 1) * tile],
+                    cos_ref[rows, :],
+                    sin_low_ref[rows, :],
+                    sin_high_ref[rows, :],
+                    -1.0,
+                )
             )
-            * 0.125
-        )
-        value_grad = value_grad + jnp.einsum(
-            "hqk,qhd->khd",
-            attention.astype(jnp.bfloat16),
-            grad_block,
-            preferred_element_type=jnp.float32,
-        )
-        return ((key_grad, value_grad), query_grad)
-
-    zero_grad = jnp.zeros(keys.shape, jnp.float32)
-    carried, query_grad = lax.scan(
-        one_block,
-        (zero_grad, zero_grad),
-        jnp.arange(queries.shape[0] // block_rows, dtype=jnp.int32),
-    )
-    return (query_grad.reshape(queries.shape), carried[0], carried[1])
+        return jnp.concatenate(parts, axis=1) if len(parts) > 1 else parts[0]
+
+    dq = turn_back(dq_acc[...].T * 0.125, here).astype(jnp.bfloat16)
+    dq_ref[...] = dq
+    bias_ref[0:1, :] += jnp.sum(dq.astype(jnp.float32), axis=0, keepdims=True)
+
+    @pl.when(block == last)
+    def _():
+        def finish(part, _):
+            rows = pl.ds(pl.multiple_of(part * BLK, BLK), BLK)
+            dk = turn_back(dk_acc[rows, :], rows).astype(jnp.bfloat16)
+            dv = dv_acc[rows, :].astype(jnp.bfloat16)
+            dk_ref[rows, :] = dk
+            dv_ref[rows, :] = dv
+            bias_ref[1:2, :] += jnp.sum(dk.astype(jnp.float32), axis=0, keepdims=True)
+            bias_ref[2:3, :] += jnp.sum(dv.astype(jnp.float32), axis=0, keepdims=True)
+            return 0
+
+        lax.fori_loop(0, length // BLK, finish, 0)
+
+
+def attention_backward(low_blocks, queries, keys, values, start, lse, context, grads, tables):
+    length, width = queries.shape
+    whole = pl.BlockSpec((length, width), lambda i, low: (0, 0))
+    rows = pl.BlockSpec((BLK, width), lambda i, low: (i, 0))
+    table = pl.BlockSpec(tables[0].shape, lambda i, low: (0, 0))
+    return pl.pallas_call(
+        backward_kernel,
+        grid_spec=pltpu.PrefetchScalarGridSpec(
+            num_scalar_prefetch=1,
+            grid=(length // BLK,),
+            in_specs=[
+                whole,
+                whole,
+                whole,
+                pl.BlockSpec((1, BLK), lambda i, low: (0, i)),
+                pl.BlockSpec((8, BLK), lambda i, low: (0, i)),
+                rows,
+                rows,
+                table,
+                table,
+                table,
+            ],
+            out_specs=[rows, whole, whole, pl.BlockSpec((8, width), lambda i, low: (0, 0))],
+            scratch_shapes=[
+                pltpu.VMEM((width, length), jnp.bfloat16),
+                pltpu.VMEM((width, BLK), jnp.float32),
+                pltpu.VMEM((length, width), jnp.float32),
+                pltpu.VMEM((length, width), jnp.float32),
+            ],
+        ),
+        out_shape=[jax.ShapeDtypeStruct((length, width), jnp.bfloat16)] * 3
+        + [jax.ShapeDtypeStruct((8, width), jnp.float32)],
+        compiler_params=pltpu.CompilerParams(vmem_limit_bytes=40 << 20),
+        name="attention_backward",
+    )(low_blocks, queries, keys, values, start, lse, context, grads, *tables)
 
 
 def adam_update(master, gradient, moment_one, moment_two, correct_one, correct_two, rate):
@@ -176,47 +352,29 @@
         lax.all_gather(w_out.astype(low_type), "dp", axis=1, tiled=True),
         lax.all_gather(w_down.astype(low_type), "dp", axis=1, tiled=True),
     )
-    seq_count = segments.shape[0]
     length = segments.shape[1]
-    total_rows = seq_count * length
     head_width = w_qkv.shape[2]
-    heads_local = head_width // HD
-    block_rows = min(512, length)
     inputs_full = inputs.astype(full_type)
     normed_one, plain_one, inverse_one = layer_norm_parts(inputs_full, norm_gain[0], norm_bias[0])
     normed_one = normed_one.astype(low_type)
-    projected = jnp.einsum(
-        "rd,cdh->rch",
-        lax.all_gather(normed_one, "tensor", axis=0, tiled=True),
-        qkv_all,
-        preferred_element_type=full_type,
-    )
-    cosine, sine = rotary_tables(positions(segments), full_type)
-    cosine = cosine.reshape(total_rows, 1, ROT // 2)
-    sine = sine.reshape(total_rows, 1, ROT // 2)
-    query_lin = (projected[:, 0] + qkv_bias[0]).reshape(total_rows, heads_local, HD)
-    key_lin = (projected[:, 1] + qkv_bias[1]).reshape(total_rows, heads_local, HD)
-    value_low = (
-        (projected[:, 2] + qkv_bias[2]).astype(low_type).reshape(seq_count, length, heads_local, HD)
-    )
-    query_low = (
-        rotate(query_lin, cosine, sine).astype(low_type).reshape(seq_count, length, heads_local, HD)
-    )
-    key_low = (
-        rotate(key_lin, cosine, sine).astype(low_type).reshape(seq_count, length, heads_local, HD)
-    )
-
-    def forward_sequence(operands):
-        return attention_forward(operands[0], operands[1], operands[2], operands[3], block_rows)
-
-    context_low, log_totals = lax.map(forward_sequence, (query_low, key_low, value_low, segments))
-    context_flat = context_low.reshape(total_rows, head_width)
+    normed_all = lax.all_gather(normed_one, "tensor", axis=0, tiled=True)
+    projected = jnp.einsum("rd,cdh->crh", normed_all, qkv_all, preferred_element_type=full_type)
+    place = positions(segments)[0]
+    start = jnp.arange(length, dtype=jnp.int32) - place
+    low_blocks = start[::BLK] // BLK
+    start = start[None, :]
+    tables = rotary_tables(place, head_width)
+    half_tables = tuple(t[:, : min(head_width, 128)] for t in tables)
+    query_low = rope_whole(projected[0] + qkv_bias[0], tables).astype(low_type)
+    key_low = rope_whole(projected[1] + qkv_bias[1], tables).astype(low_type)
+    value_low = (projected[2] + qkv_bias[2]).astype(low_type)
+    context_flat, lse = attention_forward(low_blocks, query_low, key_low, value_low, start)
     middle = inputs_full + lax.psum_scatter(
-        jnp.dot(context_flat, out_all, preferred_element_type=full_type),
+        jnp.dot(context_flat, out_all, preferred_element_type=full_type).astype(low_type),
         "tensor",
         scatter_dimension=0,
         tiled=True,
-    )
+    ).astype(full_type)
     normed_two, plain_two, inverse_two = layer_norm_parts(middle, norm_gain[1], norm_bias[1])
     normed_two = normed_two.astype(low_type)
     gate_pair = jnp.einsum(
@@ -247,11 +405,13 @@
     up_grad = hidden_grad * activated
     pair_grad = jnp.stack([gate_grad, up_grad], axis=1).astype(low_type)
     normed_two_grad = lax.psum_scatter(
-        jnp.einsum("rcf,cdf->rd", pair_grad, gate_up_all, preferred_element_type=full_type),
+        jnp.einsum("rcf,cdf->rd", pair_grad, gate_up_all, preferred_element_type=full_type).astype(
+            low_type
+        ),
         "tensor",
         scatter_dimension=0,
         tiled=True,
-    )
+    ).astype(full_type)
     rows_grad = pair_grad
     grad_gate_up = jnp.einsum(
         "rd,rcf->cdf",
@@ -270,23 +430,19 @@
     context_grad = jnp.einsum(
         "rd,hd->rh", attn_grad_all, out_all, preferred_element_type=full_type
     ).astype(low_type)
-    context_grad = context_grad.reshape(seq_count, length, heads_local, HD)
-
-    def backward_sequence(operands):
-        return attention_backward(
-            operands[0], operands[1], operands[2], operands[3], operands[4], operands[5], block_rows
-        )
-
-    query_rot_grad, key_rot_grad, value_grad = lax.map(
-        backward_sequence, (query_low, key_low, value_low, segments, log_totals, context_grad)
-    )
-    query_grad = rotate(query_rot_grad.reshape(total_rows, heads_local, HD), cosine, -sine)
-    key_grad = rotate(key_rot_grad.reshape(total_rows, heads_local, HD), cosine, -sine)
-    triple_grad = jnp.stack(
-        [query_grad, key_grad, value_grad.reshape(total_rows, heads_local, HD)], axis=1
-    )
-    triple_grad = triple_grad.astype(low_type).reshape(total_rows, 3, head_width)
-    grad_bias = jnp.sum(triple_grad, axis=0, dtype=full_type)
+    query_grad, key_grad, value_grad, bias_sums = attention_backward(
+        low_blocks,
+        query_low,
+        key_low,
+        value_low,
+        start,
+        lse,
+        context_flat,
+        context_grad,
+        half_tables,
+    )
+    triple_grad = jnp.stack([query_grad, key_grad, value_grad], axis=1)
+    grad_bias = bias_sums[:3]
     normed_one_grad = lax.psum_scatter(
         jnp.einsum("rch,cdh->rd", triple_grad, qkv_all, preferred_element_type=full_type).astype(
             jnp.bfloat16

time: 1560 us -> 1160 us (0.74)
  matrix products: 324 us -> 142 us
  waiting for transfers between devices: 918 us -> 794 us
  other arithmetic: 132 us -> 56.2 us
  Pallas kernels: 0 us -> 53.9 us
  local copies, waits for them, and re-layouts: 92.9 us -> 43.5 us
    dot_general x29 -> x1, matrix products: 179 us -> 10.1 us  [per_device(): jnp.einsum('rd,cdh->crh', normed_all, qkv_all, preferred_element_type=ful...]
    reduce_scatter x1, waiting for transfers between devices: 164 us -> 88.6 us  [per_device(): lax.psum_scatter(jnp.dot(context_flat, out_all, preferred_element_type=fu...]
    reduce_scatter x1, waiting for transfers between devices: 155 us -> 88.3 us  [per_device(): lax.psum_scatter(jnp.einsum('rcf,cdf->rd', pair_grad, gate_up_all, prefer...]
    pallas_call x0 -> x2, Pallas kernels: none -> 53.9 us  [the longest x1 31.5 us: attention_backward(): pl.pallas_call(backward_kernel, grid_spec=pltpu.PrefetchScalarGridSpec(nu...]
    dynamic_update_slice x8 -> x0, local copies, waits for them, and re-layouts: 46.6 us -> none  [attention_backward(): lax.scan(one_block, (zero_grad, zero_grad), jnp.arange(queries.shape[0] /...]
    convert_element_type x6 -> x3, other arithmetic: 44.9 us -> 4.35 us  [the longest x1 3.78 us: per_device(): key_low = rope_whole(projected[1] + qkv_bias[1], tables).astype(low_type)]
    reduce_scatter x1, waiting for transfers between devices: 87 us -> 47.7 us  [per_device(): lax.psum_scatter(jnp.dot(hidden_low, down_all, preferred_element_type=ful...]
    reduce_scatter x1, waiting for transfers between devices: 7.59 us -> 44.2 us  [per_device(): lax.psum_scatter(grad_qkv.astype(jnp.bfloat16), 'dp', scatter_dimension=1...]
  transfers between devices with their start and end apart: 16 -> 16, of which waited for: 12 -> 14; matrix products, arithmetic and copies ran while one was open for 31% -> 15% of each run, Pallas kernels for 0% -> 5%
where the time goes in v1:
time: 1160 us; the launch traced here: 1150 us
  waiting for transfers between devices  794 us (68%)
  matrix products  142 us (12%)
  other arithmetic  56.2 us (5%)
  Pallas kernels  53.9 us (5%)
  blocking collectives  49.3 us (4%)
  local copies, waits for them, and re-layouts  43.5 us (4%)
  between operations  14.9 us (1%)
    reduce_scatter x1, waiting for transfers between devices, per_device(): lax.psum_scatter(jnp.dot(context_flat, out_all, preferred_element_type=fu...  88.6 us
    reduce_scatter x1, waiting for transfers between devices, per_device(): lax.psum_scatter(jnp.einsum('rcf,cdf->rd', pair_grad, gate_up_all, prefer...  88.3 us
    all_gather x1, waiting for transfers between devices, per_device(): normed_all = lax.all_gather(normed_one, 'tensor', axis=0, tiled=True)  84.3 us
    all_gather x1, waiting for transfers between devices, per_device(): lax.all_gather(normed_two, 'tensor', axis=0, tiled=True)  84.1 us
    all_gather x1, waiting for transfers between devices, per_device(): mlp_grad = lax.all_gather(out_grad, 'tensor', axis=0, tiled=True)  83.7 us
    reduce_scatter x1, waiting for transfers between devices, per_device(): lax.psum_scatter(jnp.einsum('rch,cdh->rd', triple_grad, qkv_all, preferre...  76.3 us
    all_gather x1, waiting for transfers between devices, per_device(): lax.all_gather(w_gate_up.astype(low_type), 'dp', axis=1, tiled=True)  58.9 us
    reduce_scatter x1, waiting for transfers between devices, per_device(): lax.psum_scatter(jnp.dot(hidden_low, down_all, preferred_element_type=ful...  47.7 us
  transfers between devices with their start and end apart: 16, of which 14 were waited for; matrix products, arithmetic and copies ran while one was open for 15% of the time, Pallas kernels for 5%

profile of v1, /device:TPU:0, one launch (start us, length us, event | category | flops | bytes accessed | tf_op | source)
XLA Modules:
  0.0 1154.6 jit_solution(3722311046557709022)
XLA Ops:
  7.2 1.9 copy.66
  9.2 1.0 convert_element_type.112
  12.0 1.4 fusion.34
  16.2 2.1 copy.70
  18.6 1.8 copy.69
  20.7 1.9 copy.68
  22.6 34.4 %all-gather.11.cloned.1.call-done = bf16[3,2048,256]{1,2,0:T(8,128)(2,1)} async-done(((bf16[3,512,256]{1,2,0:T(8,128)(2,1)}), bf16[3,2048,256]{1,2,0:T(8,128)(2,1)}) %all-gather.11.cloned.1.call-update) | async-done | bytes 3145744 | tf_op jit(solution)/shard_map/all_gather | solution.py:350
  57.0 84.3 %all-gather.9.cloned.1.call-done = bf16[2048,2048]{1,0:T(8,128)(2,1)} async-done(((bf16[256,2048]{1,0:T(8,128)(2,1)}), bf16[2048,2048]{1,0:T(8,128)(2,1)}) %all-gather.9.cloned.1.call-update) | async-done | bytes 8388624 | tf_op jit(solution)/shard_map/all_gather | solution.py:360
  141.3 10.1 fusion.11
  151.9 2.3 fusion.79
  154.1 1.4 fusion.80
  157.0 3.8 fusion.56
  160.8 22.4 %attention_forward.1 = (bf16[2048,256]{1,0:T(8,128)(2,1)S(1)}, f32[8,2048]{1,0:T(8,128)S(1)}) custom-call(s32[8]{0:T(128)S(1)} %and_select_fusion.low_ref, bf16[2048,256]{1,0:T(8,128)(2,1)S(1)} %get-tuple-element.143.q_ref, bf16[2048,256]{1,0:T(8,128)(2,1)S(1)} %get-tuple-element.142.k_ref, bf16[2048,256]{1,0:T(8,128)(2,1)S(1)} %get-tuple-element.139.v_ref, ...), custom_call_target="tpu_custom_call" | custom-call | tf_op jit(solution)/shard_map/attention_forward/pallas_call | solution.py:143
  184.1 6.9 convolution_convert_fusion.1
  191.1 3.1 convert_element_type.121
  194.3 88.6 %reduce-scatter.9.cloned.1.call-done = bf16[256,2048]{1,0:T(8,128)(2,1)} async-done(((bf16[2048,2048]{1,0:T(8,128)(2,1)}), bf16[256,2048]{1,0:T(8,128)(2,1)}) %reduce-scatter.9.cloned.1.call-update) | async-done | bytes 1048592 | tf_op jit(solution)/shard_map/reduce_scatter | solution.py:372
  282.9 2.0 fusion.57
  285.6 1.5 add_convert_fusion.1
  287.2 2.3 convert_element_type.123
  290.3 58.9 %all-gather.17.cloned.1.call-done = bf16[2,2048,704]{1,2,0:T(8,128)(2,1)} async-done(((bf16[2,512,704]{1,2,0:T(8,128)(2,1)}), bf16[2,2048,704]{1,2,0:T(8,128)(2,1)}) %all-gather.17.cloned.1.call-update) | async-done | bytes 5767184 | tf_op jit(solution)/shard_map/all_gather | solution.py:351
  349.2 84.1 %all-gather.15.cloned.1.call-done = bf16[2048,2048]{1,0:T(8,128)(2,1)} async-done(((bf16[256,2048]{1,0:T(8,128)(2,1)}), bf16[2048,2048]{1,0:T(8,128)(2,1)}) %all-gather.15.cloned.1.call-update) | async-done | bytes 8388624 | tf_op jit(solution)/shard_map/all_gather | solution.py:382
  433.3 19.4 %fusion.2 = f32[2048,2,704]{0,2,1:T(8,128)} fusion(bf16[2,2048,704]{1,2,0:T(8,128)(2,1)} %all-gather.17.cloned.1.call-done, bf16[2048,2048]{1,0:T(8,128)(2,1)} %all-gather.15.cloned.1.call-done), kind=kOutput, calls=%fused_computation.4 | convolution fusion | flops 11811160064 | bytes 25690112 | tf_op jit(solution)/shard_map/rd,cdf->rcf/dot_general | solution.py:380
  452.7 23.3 %all-gather.19.cloned.1.call-done = bf16[704,2048]{1,0:T(8,128)(2,1)} async-done(((bf16[704,512]{1,0:T(8,128)(2,1)}), bf16[704,2048]{1,0:T(8,128)(2,1)}) %all-gather.19.cloned.1.call-update) | async-done | bytes 2883600 | tf_op jit(solution)/shard_map/all_gather | solution.py:353
  476.0 83.7 %all-gather.21.cloned.1.call-done = bf16[2048,2048]{1,0:T(8,128)(2,1)} async-done(((bf16[256,2048]{1,0:T(8,128)(2,1)}), bf16[2048,2048]{1,0:T(8,128)(2,1)}) %all-gather.21.cloned.1.call-update) | async-done | bytes 8388624 | tf_op jit(solution)/shard_map/all_gather | solution.py:401
  559.6 15.0 %fusion.28 = (bf16[2048,1,704]{0,2,1:T(8,128)(2,1)S(1)}, bf16[2048,1,704]{0,2,1:T(8,128)(2,1)S(1)}, bf16[2048,704]{0,1:T(8,128)(2,1)}) fusion(f32[2048,2,704]{0,2,1:T(8,128)} %fusion.2, bf16[2048,2048]{1,0:T(8,128)(2,1)} %all-gather.21.cloned.1.call-done, bf16[704,2048]{1,0:T(8,128)(2,1)} %all-gather.19.cloned.1.call-done), kind=kOutput, calls=%fused_computation.46 | convolution fusion | flops 5927206912 | bytes 31457280 | tf_op jit(solution)/shard_map/rd,fd->rf/dot_general | solution.py:403
  574.6 1.6 copy-done.57
  577.2 16.1 %bitcast_convert_fusion.1 = bf16[2048,2048]{1,0:T(8,128)(2,1)} fusion(bf16[2,2048,704]{1,2,0:T(8,128)(2,1)S(1)} %copy-done.55, bf16[2048,1,704]{0,2,1:T(8,128)(2,1)S(1)} %get-tuple-element.137, bf16[2048,1,704]{0,2,1:T(8,128)(2,1)S(1)} %get-tuple-element.136), kind=kOutput, calls=%fused_computation.1 | convolution fusion | flops 11818237952 | bytes 19922944 | tf_op jit(solution)/shard_map/rcf,cdf->rd/dot_general | solution.py:408
  593.3 88.3 %reduce-scatter.13.cloned.1.call-done = bf16[256,2048]{1,0:T(8,128)(2,1)} async-done(((bf16[2048,2048]{1,0:T(8,128)(2,1)}), bf16[256,2048]{1,0:T(8,128)(2,1)}) %reduce-scatter.13.cloned.1.call-update) | async-done | bytes 1048592 | tf_op jit(solution)/shard_map/reduce_scatter | solution.py:407
  681.6 3.1 fusion.45
  684.8 3.4 fusion.71
  688.2 10.5 convolution_convert_fusion.2
  698.8 17.9 %convert_bitcast_fusion = bf16[2,2048,704]{1,2,0:T(8,128)(2,1)} fusion(bf16[2048,2048]{1,0:T(8,128)(2,1)} %all-gather.15.cloned.1.call-done, bf16[2048,1,704]{0,2,1:T(8,128)(2,1)} %copy-done.58, bf16[2048,1,704]{0,2,1:T(8,128)(2,1)} %copy-done.57), kind=kOutput, calls=%fused_computation.15 | convolution fusion | flops 11816927232 | bytes 19922944 | tf_op jit(solution)/shard_map/rd,rcf->cdf/dot_general | solution.py:416
  716.8 2.5 slice.134.sin_high_ref
  719.3 1.0 slice.133.sin_low_ref
  720.3 1.0 slice.132.cos_ref
  721.3 47.4 %all-gather.23.cloned.1.call-done = bf16[2048,2048]{1,0:T(8,128)(2,1)} async-done(((bf16[256,2048]{1,0:T(8,128)(2,1)}), bf16[2048,2048]{1,0:T(8,128)(2,1)}) %all-gather.23.cloned.1.call-update) | async-done | bytes 8388624 | tf_op jit(solution)/shard_map/all_gather | solution.py:426
  768.7 6.7 convolution_convert_fusion.3
  775.8 6.6 convolution_convert_fusion.4.grad_ref
  782.5 31.5 %attention_backward.1 = (bf16[2048,256]{1,0:T(8,128)(2,1)S(1)}, bf16[2048,256]{1,0:T(8,128)(2,1)S(1)}, bf16[2048,256]{1,0:T(8,128)(2,1)S(1)}, f32[8,256]{1,0:T(8,128)S(1)}) custom-call(s32[8]{0:T(128)S(1)} %and_select_fusion.low_ref, bf16[2048,256]{1,0:T(8,128)(2,1)S(1)} %copy-done.1, bf16[2048,256]{1,0:T(8,128)(2,1)S(1)} %get-tuple-element.142.k_ref, ...), custom_call_target="tpu_custom_call" | custom-call | tf_op jit(solution)/shard_map/attention_backward/pallas_call | solution.py:282
  815.7 10.5 fusion.17
  826.3 1.1 copy-done.6
  828.1 10.8 bitcast_convert_fusion
  839.3 1.3 copy-done.56
  840.7 11.2 convolution_convert_fusion
  851.9 1.4 copy-done.31
  853.3 1.6 copy.79
  854.9 1.6 copy.80
  856.6 5.6 multiply_subtract_fusion.2
  862.2 19.2 %reduce-scatter.21.cloned.1.call-done = bf16[2,512,704]{1,2,0:T(8,128)(2,1)} async-done(((bf16[2,2048,704]{1,2,0:T(8,128)(2,1)}), bf16[2,512,704]{1,2,0:T(8,128)(2,1)}) %reduce-scatter.21.cloned.1.call-update) | async-done | bytes 1441808 | tf_op jit(solution)/shard_map/reduce_scatter | solution.py:469
  881.4 8.5 multiply_subtract_fusion
  889.9 9.5 psum.21
  900.1 12.6 %reduce-scatter.19.cloned.1.call-done = bf16[256,512]{1,0:T(8,128)(2,1)} async-done(((bf16[256,2048]{1,0:T(8,128)(2,1)}), bf16[256,512]{1,0:T(8,128)(2,1)}) %reduce-scatter.19.cloned.1.call-update) | async-done | bytes 262160 | tf_op jit(solution)/shard_map/reduce_scatter | solution.py:472
  912.7 2.9 multiply_subtract_fusion.3
  915.6 44.2 %reduce-scatter.17.cloned.1.call-done = bf16[3,512,256]{1,2,0:T(8,128)(2,1)} async-done(((bf16[3,2048,256]{1,2,0:T(8,128)(2,1)}), bf16[3,512,256]{1,2,0:T(8,128)(2,1)}) %reduce-scatter.17.cloned.1.call-update) | async-done | bytes 786448 | tf_op jit(solution)/shard_map/reduce_scatter | solution.py:466
  959.8 4.8 multiply_subtract_fusion.1
  964.6 3.0 copy.84
  967.6 3.4 copy.85
  971.0 1.6 copy.86
  972.7 2.7 copy.83
  975.4 76.3 %reduce-scatter.15.cloned.1.call-done = bf16[256,2048]{1,0:T(8,128)(2,1)} async-done(((bf16[2048,2048]{1,0:T(8,128)(2,1)}), bf16[256,2048]{1,0:T(8,128)(2,1)}) %reduce-scatter.15.cloned.1.call-update) | async-done | bytes 1048592 | tf_op jit(solution)/shard_map/reduce_scatter | solution.py:446
  1051.7 2.3 fusion.46
  1054.1 39.8 %all-reduce = (f32[2,2048]{1,0:T(2,128)S(1)}, f32[2,2048]{1,0:T(2,128)S(1)}) all-reduce(f32[2,2048]{1,0:T(2,128)S(1)} %pad_maximum_fusion.6, f32[2,2048]{1,0:T(2,128)S(1)} %pad_maximum_fusion.7), channel_id=1, replica_groups=mesh['dp'=4,'tensor'=8] {'dp','tensor'}, use_global_device_ids=true, to_apply=%region_21.22 | all-reduce | flops 8192 | bytes 65536 | tf_op jit(solution)/shard_map/psum | solution.py:480
  1095.3 47.7 %reduce-scatter.11.cloned.1.call-done = bf16[256,2048]{1,0:T(8,128)(2,1)} async-done(((bf16[2048,2048]{1,0:T(8,128)(2,1)}), bf16[256,2048]{1,0:T(8,128)(2,1)}) %reduce-scatter.11.cloned.1.call-update) | async-done | bytes 1048592 | tf_op jit(solution)/shard_map/reduce_scatter | solution.py:394
  1143.0 4.9 fusion.38
  (191 shorter events, 16.0 us)
Async XLA Ops:
  7.2 49.8 %all-gather.11.cloned.1.call-start = ((), (), s32[]{:S(2)}) async-start(), calls=%async_computation.9 | async-start | bytes 3932160 | tf_op jit(solution)/shard_map/all_gather | solution.py:350
  9.1 2.2 copy-start.18
  9.1 2.0 copy-start.11
  9.2 2.7 copy-start.35
  9.2 2.7 copy-start.37
  10.2 131.1 %all-gather.9.cloned.1.call-start = ((), (), s32[]{:S(2)}) async-start(), calls=%async_computation.8 | async-start | bytes 9437184 | tf_op jit(solution)/shard_map/all_gather | solution.py:360
  11.4 2.0 copy-start.40
  11.4 2.1 copy-start.30
  11.9 2.4 copy-start.42
  11.9 2.4 copy-start.33
  11.9 2.6 copy-start.51
  11.9 2.6 copy-start.39
  13.4 170.7 %all-gather.13.cloned.1.call-start = ((), (), s32[]{:S(2)}) async-start(), calls=%async_computation.10 | async-start | bytes 1310720 | tf_op jit(solution)/shard_map/all_gather | solution.py:352
  14.3 268.7 %reduce-scatter.9.cloned.1.call-start = ((), (), s32[]{:S(2)}) async-start(), calls=%async_computation.11 | async-start | bytes 9437184 | tf_op jit(solution)/shard_map/reduce_scatter | solution.py:372
  154.1 2.2 copy-start.21
  154.1 2.9 copy-start.23
  191.1 158.1 %all-gather.17.cloned.1.call-start = ((), (), s32[]{:S(2)}) async-start(), calls=%async_computation.13 | async-start | bytes 7208960 | tf_op jit(solution)/shard_map/all_gather | solution.py:351
  194.2 239.1 %all-gather.15.cloned.1.call-start = ((), (), s32[]{:S(2)}) async-start(), calls=%async_computation.12 | async-start | bytes 9437184 | tf_op jit(solution)/shard_map/all_gather | solution.py:382
  282.9 2.1 copy-start.12
  282.9 2.2 copy-start.15
  287.2 188.8 %all-gather.19.cloned.1.call-start = ((), (), s32[]{:S(2)}) async-start(), calls=%async_computation.14 | async-start | bytes 3604480 | tf_op jit(solution)/shard_map/all_gather | solution.py:353
  289.5 270.1 %all-gather.21.cloned.1.call-start = ((), (), s32[]{:S(2)}) async-start(), calls=%async_computation.16 | async-start | bytes 9437184 | tf_op jit(solution)/shard_map/all_gather | solution.py:401
  290.3 391.3 %reduce-scatter.13.cloned.1.call-start = ((), (), s32[]{:S(2)}) async-start(), calls=%async_computation.17 | async-start | bytes 9437184 | tf_op jit(solution)/shard_map/reduce_scatter | solution.py:407
  559.6 17.5 %copy-start.55 = (bf16[2,2048,704]{1,2,0:T(8,128)(2,1)S(1)}, bf16[2,2048,704]{1,2,0:T(8,128)(2,1)}, u32[]{:S(2)}) copy-start(bf16[2,2048,704]{1,2,0:T(8,128)(2,1)} %all-gather.17.cloned.1.call-done) | copy-start | bytes 17301508
  574.6 2.5 copy-start.58
  593.3 175.5 %all-gather.23.cloned.1.call-start = ((), (), s32[]{:S(2)}) async-start(), calls=%async_computation.18 | async-start | bytes 9437184 | tf_op jit(solution)/shard_map/all_gather | solution.py:426
  681.6 3.2 copy-start.13
  681.6 3.2 copy-start.16
  681.6 3.2 copy-start.26
  688.2 168.4 %reduce-scatter.23.cloned.1.call-start = ((), (), s32[]{:S(2)}) async-start(), calls=%async_computation.23 | async-start | bytes 3604480 | tf_op jit(solution)/shard_map/reduce_scatter | solution.py:475
  698.7 182.6 %reduce-scatter.21.cloned.1.call-start = ((), (), s32[]{:S(2)}) async-start(), calls=%async_computation.22 | async-start | bytes 7208960 | tf_op jit(solution)/shard_map/reduce_scatter | solution.py:469
  716.7 196.0 %reduce-scatter.19.cloned.1.call-start = ((), (), s32[]{:S(2)}) async-start(), calls=%async_computation.21 | async-start | bytes 1310720 | tf_op jit(solution)/shard_map/reduce_scatter | solution.py:472
  716.8 2.5 copy-start.22
  716.8 3.5 copy-start.24
  775.5 184.4 %reduce-scatter.17.cloned.1.call-start = ((), (), s32[]{:S(2)}) async-start(), calls=%async_computation.20 | async-start | bytes 3932160 | tf_op jit(solution)/shard_map/reduce_scatter | solution.py:466
  775.7 6.7 copy-start.1
  775.8 6.7 copy-start.2
  775.8 6.7 copy-start.3
  775.8 6.7 copy-start.4
  826.2 1.9 copy-start.10
  826.2 225.5 %reduce-scatter.15.cloned.1.call-start = ((), (), s32[]{:S(2)}) async-start(), calls=%async_computation.19 | async-start | bytes 9437184 | tf_op jit(solution)/shard_map/reduce_scatter | solution.py:446
  838.9 304.1 %reduce-scatter.11.cloned.1.call-start = ((), (), s32[]{:S(2)}) async-start(), calls=%async_computation.15 | async-start | bytes 9437184 | tf_op jit(solution)/shard_map/reduce_scatter | solution.py:394
  856.6 24.8 %copy-start.25 = (f32[2,512,704]{1,2,0:T(8,128)S(1)}, f32[2,512,704]{1,2,0:T(8,128)}, u32[]{:S(2)}) copy-start(f32[2,512,704]{1,2,0:T(8,128)} %param.29) | copy-start | bytes 8650756
  862.2 37.3 %copy-start.52 = (f32[3,256]{1,0:T(4,128)S(1)}, f32[3,256]{1,0:T(4,128)}, u32[]{:S(2)}) copy-start(f32[3,256]{1,0:T(4,128)} %param.31) | copy-start | bytes 9220
  862.2 37.3 %copy-start.53 = (f32[3,256]{1,0:T(4,128)S(1)}, f32[3,256]{1,0:T(4,128)}, u32[]{:S(2)}) copy-start(f32[3,256]{1,0:T(4,128)} %param.38) | copy-start | bytes 9220
  862.2 37.3 %copy-start.54 = (f32[3,256]{1,0:T(4,128)S(1)}, f32[3,256]{1,0:T(4,128)}, u32[]{:S(2)}) copy-start(f32[3,256]{1,0:T(4,128)} %param.45) | copy-start | bytes 9220
  889.9 69.9 %copy-start.19 = (f32[3,512,256]{1,2,0:T(8,128)S(1)}, f32[3,512,256]{1,2,0:T(8,128)}, u32[]{:S(2)}) copy-start(f32[3,512,256]{1,2,0:T(8,128)} %copy-done.18) | copy-start | bytes 4718596
  889.9 69.9 %copy-start.28 = (f32[3,512,256]{1,2,0:T(8,128)S(1)}, f32[3,512,256]{1,2,0:T(8,128)}, u32[]{:S(2)}) copy-start(f32[3,512,256]{1,2,0:T(8,128)} %copy.79) | copy-start | bytes 4718596
  899.5 65.1 %copy-start.50 = (f32[3,256]{1,0:T(4,128)}, f32[3,256]{1,0:T(4,128)S(1)}, u32[]{:S(2)}) copy-start(f32[3,256]{1,0:T(4,128)S(1)} %psum.21) | copy-start | bytes 9220
  967.6 3.4 copy-start.29
  971.0 80.7 %copy-start.14 = (bf16[256,2048]{1,0:T(8,128)(2,1)S(1)}, bf16[256,2048]{1,0:T(8,128)(2,1)}, u32[]{:S(2)}) copy-start(bf16[256,2048]{1,0:T(8,128)(2,1)} %param.24) | copy-start | bytes 3145732
  971.0 80.7 %copy-start.34 = (f32[1,2048]{1,0:T(1,128)S(1)}, f32[1,2048]{1,0:T(1,128)}, u32[]{:S(2)}) copy-start(f32[1,2048]{1,0:T(1,128)} %copy-done.33) | copy-start | bytes 24580
  971.0 80.7 %copy-start.41 = (f32[256]{0:T(256)S(1)}, f32[256]{0:T(256)}, u32[]{:S(2)}) copy-start(f32[256]{0:T(256)} %copy-done.40) | copy-start | bytes 3076
  971.0 80.7 %copy-start.43 = (f32[256]{0:T(256)S(1)}, f32[256]{0:T(256)}, u32[]{:S(2)}) copy-start(f32[256]{0:T(256)} %copy-done.42) | copy-start | bytes 3076
  972.7 121.2 %copy-start.36 = (f32[2,2048]{1,0:T(2,128)S(1)}, f32[2,2048]{1,0:T(2,128)}, u32[]{:S(2)}) copy-start(f32[2,2048]{1,0:T(2,128)} %param.32) | copy-start | bytes 49156
  972.7 121.2 %copy-start.44 = (f32[2,2048]{1,0:T(2,128)S(1)}, f32[2,2048]{1,0:T(2,128)}, u32[]{:S(2)}) copy-start(f32[2,2048]{1,0:T(2,128)} %param.39) | copy-start | bytes 49156
  972.7 121.2 %copy-start.45 = (f32[2,2048]{1,0:T(2,128)S(1)}, f32[2,2048]{1,0:T(2,128)}, u32[]{:S(2)}) copy-start(f32[2,2048]{1,0:T(2,128)} %param.46) | copy-start | bytes 49156
  972.7 121.9 %copy-start.38 = (f32[2,2048]{1,0:T(2,128)S(1)}, f32[2,2048]{1,0:T(2,128)}, u32[]{:S(2)}) copy-start(f32[2,2048]{1,0:T(2,128)} %param.33) | copy-start | bytes 49156
  972.7 121.9 %copy-start.46 = (f32[2,2048]{1,0:T(2,128)S(1)}, f32[2,2048]{1,0:T(2,128)}, u32[]{:S(2)}) copy-start(f32[2,2048]{1,0:T(2,128)} %param.40) | copy-start | bytes 49156
  972.7 121.9 %copy-start.47 = (f32[2,2048]{1,0:T(2,128)S(1)}, f32[2,2048]{1,0:T(2,128)}, u32[]{:S(2)}) copy-start(f32[2,2048]{1,0:T(2,128)} %param.47) | copy-start | bytes 49156
  972.7 170.3 %copy-start.17 = (bf16[256,2048]{1,0:T(8,128)(2,1)S(1)}, bf16[256,2048]{1,0:T(8,128)(2,1)}, u32[]{:S(2)}) copy-start(bf16[256,2048]{1,0:T(8,128)(2,1)} %reduce-scatter.9.cloned.1.call-done) | copy-start | bytes 3145732
  972.7 170.3 %copy-start.27 = (bf16[256,2048]{1,0:T(8,128)(2,1)S(1)}, bf16[256,2048]{1,0:T(8,128)(2,1)}, u32[]{:S(2)}) copy-start(bf16[256,2048]{1,0:T(8,128)(2,1)} %param.25) | copy-start | bytes 3145732
  1093.8 54.1 %copy-start.48 = (f32[2,2048]{1,0:T(2,128)}, f32[2,2048]{1,0:T(2,128)S(1)}, u32[]{:S(2)}) copy-start(f32[2,2048]{1,0:T(2,128)S(1)} %get-tuple-element.110) | copy-start | bytes 49156
  1093.9 54.1 %copy-start.49 = (f32[2,2048]{1,0:T(2,128)}, f32[2,2048]{1,0:T(2,128)S(1)}, u32[]{:S(2)}) copy-start(f32[2,2048]{1,0:T(2,128)S(1)} %get-tuple-element.111) | copy-start | bytes 49156
  (11 other events, 15.7 us)
Sparse Core Ops, SparseCore 0:
  10.4 46.5 all-gather.10
  59.2 82.0 all-gather.8
  143.7 25.0 all-gather.12
  191.2 91.6 reduce-scatter.8
  285.2 63.9 all-gather.16
  351.2 82.0 all-gather.14
  435.7 40.1 all-gather.18
  477.5 82.0 all-gather.20
  593.4 88.1 reduce-scatter.12
  688.3 80.4 all-gather.22
  772.4 40.2 reduce-scatter.22
  815.5 65.8 reduce-scatter.20
  884.8 27.8 reduce-scatter.18
  915.8 43.9 reduce-scatter.16
  962.1 89.5 reduce-scatter.14
  1054.0 88.9 reduce-scatter.10

commit v2 on v1

--- a/solution.py
+++ b/solution.py
@@ -1,3 +1,5 @@
+import functools
+
 import jax
 import jax.numpy as jnp
 from jax import lax
@@ -56,13 +58,6 @@
     )
 
 
-def rope_whole(values, tables):
-    cosine, sine_low, sine_high = tables
-    ahead = jnp.roll(values, -(ROT // 2), axis=1)
-    behind = jnp.roll(values, ROT // 2, axis=1)
-    return values * cosine + ahead * sine_low + behind * sine_high
-
-
 NEG = -1e30
 BLK = 256
 NT = (((1,), (1,)), ((), ()))
@@ -87,82 +82,25 @@
     return tile * cosine + sign * (ahead * sine_low + behind * sine_high)
 
 
-def forward_kernel(low_ref, q_ref, k_ref, v_ref, start_ref, ctx_ref, lse_ref, v_turned, acc, stats):
-    block = pl.program_id(0)
-    length, width = k_ref.shape
-    heads = width // HD
-
-    @pl.when(block == 0)
-    def _():
-        for part in range(length // BLK):
-            rows = slice(part * BLK, (part + 1) * BLK)
-            v_turned[:, rows] = v_ref[rows, :].T
-
-    queries = q_ref[pl.ds(pl.multiple_of(block * BLK, BLK), BLK), :] * 0.125
-    queries = queries.astype(jnp.bfloat16)
-    masked = [queries * m for m in head_masks(width, jnp.bfloat16)]
-    start = start_ref[...]
-    query_ids = block * BLK + lax.broadcasted_iota(jnp.int32, (1, BLK), 1)
-    acc[...] = jnp.zeros_like(acc)
-    stats[0:8, :] = jnp.full((8, BLK), NEG, jnp.float32)
-    stats[8:16, :] = jnp.zeros((8, BLK), jnp.float32)
-
-    def step(number, _):
-        base = pl.multiple_of(number * BLK, BLK)
-        keys = k_ref[pl.ds(base, BLK), :]
-        key_ids = base + lax.broadcasted_iota(jnp.int32, (BLK, BLK), 0)
-        visible = (key_ids >= start) & (key_ids <= query_ids)
-        for h in range(heads):
-            scores = jnp.where(visible, dot(keys, masked[h], NT), NEG)
-            peak_old = stats[h : h + 1, :]
-            peak = jnp.maximum(peak_old, jnp.max(scores, axis=0, keepdims=True))
-            fade = jnp.exp(peak_old - peak)
-            prob = jnp.exp(scores - peak)
-            stats[h : h + 1, :] = peak
-            stats[8 + h : 9 + h, :] = stats[8 + h : 9 + h, :] * fade + jnp.sum(
-                prob, axis=0, keepdims=True
-            )
-            rows = slice(h * HD, (h + 1) * HD)
-            acc[rows, :] = acc[rows, :] * fade + dot(
-                v_turned[rows, pl.ds(base, BLK)], prob.astype(jnp.bfloat16)
-            )
-        return 0
-
-    lax.fori_loop(low_ref[block], block + 1, step, 0)
-    for h in range(heads):
-        rows = slice(h * HD, (h + 1) * HD)
-        acc[rows, :] = acc[rows, :] / stats[8 + h : 9 + h, :]
-    ctx_ref[...] = acc[...].T.astype(ctx_ref.dtype)
-    total = jnp.where(stats[8:16, :] > 0, stats[8:16, :], 1.0)
-    lse_ref[...] = stats[0:8, :] + jnp.log(total)
-
-
-def attention_forward(low_blocks, queries, keys, values, start):
-    length, width = queries.shape
-    whole = pl.BlockSpec((length, width), lambda i, low: (0, 0))
-    return pl.pallas_call(
-        forward_kernel,
-        grid_spec=pltpu.PrefetchScalarGridSpec(
-            num_scalar_prefetch=1,
-            grid=(length // BLK,),
-            in_specs=[whole, whole, whole, pl.BlockSpec((1, BLK), lambda i, low: (0, i))],
-            out_specs=[
-                pl.BlockSpec((BLK, width), lambda i, low: (i, 0)),
-                pl.BlockSpec((8, BLK), lambda i, low: (0, i)),
-            ],
-            scratch_shapes=[
-                pltpu.VMEM((width, length), jnp.bfloat16),
-                pltpu.VMEM((width, BLK), jnp.float32),
-                pltpu.VMEM((16, BLK), jnp.float32),
-            ],
-        ),
-        out_shape=[
-            jax.ShapeDtypeStruct((length, width), jnp.bfloat16),
-            jax.ShapeDtypeStruct((8, length), jnp.float32),
-        ],
-        compiler_params=pltpu.CompilerParams(vmem_limit_bytes=32 << 20),
-        name="attention_forward",
-    )(low_blocks, queries, keys, values, start)
+def attend(number, size, k_ref, v_turned, masked, starts, query_ids, acc, stats):
+    base = pl.multiple_of(number * size, size)
+    keys = k_ref[pl.ds(base, size), :]
+    key_ids = base + lax.broadcasted_iota(jnp.int32, (size, size), 0)
+    visible = (key_ids >= starts) & (key_ids <= query_ids)
+    for h, queries in enumerate(masked):
+        scores = jnp.where(visible, dot(keys, queries, NT), NEG)
+        peak_old = stats[h : h + 1, :]
+        peak = jnp.maximum(peak_old, jnp.max(scores, axis=0, keepdims=True))
+        fade = jnp.exp(peak_old - peak)
+        prob = jnp.exp(scores - peak)
+        stats[h : h + 1, :] = peak
+        stats[8 + h : 9 + h, :] = stats[8 + h : 9 + h, :] * fade + jnp.sum(
+            prob, axis=0, keepdims=True
+        )
+        band = slice(h * HD, (h + 1) * HD)
+        acc[band, :] = acc[band, :] * fade + dot(
+            v_turned[band, pl.ds(base, size)], prob.astype(jnp.bfloat16)
+        )
 
 
 def backward_kernel(
@@ -311,6 +249,927 @@
     )(low_blocks, queries, keys, values, start, lse, context, grads, *tables)
 
 
+MESH = pl.DeviceIdType.MESH
+VMEM_BYTES = 62 << 20
+LONGEST = 1024
+TN = (((0,), (0,)), ((), ()))
+LOW = jnp.bfloat16
+
+
+def remote(source, target, send, receive, device):
+    return pltpu.make_async_remote_copy(
+        src_ref=source,
+        dst_ref=target,
+        send_sem=send,
+        recv_sem=receive,
+        device_id=device,
+        device_id_type=MESH,
+    )
+
+
+class Place:
+    def __init__(self, groups, chips):
+        self.groups, self.chips = groups, chips
+        self.group = lax.axis_index("dp")
+        self.spot = lax.axis_index("tensor")
+        self.chip, self.core = self.spot // 2, self.spot % 2
+
+    def at(self, chip, core):
+        return (self.group, chip * 2 + core)
+
+    def peer(self, offset):
+        return (lax.rem(self.group + offset, self.groups), self.spot)
+
+    def partners(self):
+        found = []
+        bit = 1
+        while bit < self.groups:
+            found.append((self.group + bit - 2 * bit * (self.group // bit % 2), self.spot))
+            bit *= 2
+        bit = 1
+        while bit < 2 * self.chips:
+            found.append((self.group, self.spot + bit - 2 * bit * (self.spot // bit % 2)))
+            bit *= 2
+        return found
+
+    def barrier(self, with_groups=False, with_partners=False):
+        semaphore = pltpu.get_barrier_semaphore()
+
+        def greet(target):
+            pl.semaphore_signal(semaphore, inc=1, device_id=target, device_id_type=MESH)
+
+        greet(self.at(self.chip, 1 - self.core))
+        pl.when(self.chip > 0)(lambda: greet(self.at(self.chip - 1, self.core)))
+        pl.when(self.chip < self.chips - 1)(lambda: greet(self.at(self.chip + 1, self.core)))
+        count = 1 + jnp.where(self.chip > 0, 1, 0) + jnp.where(self.chip < self.chips - 1, 1, 0)
+        if with_groups:
+            for offset in range(1, self.groups):
+                greet(self.peer(offset))
+            count = count + self.groups - 1
+        if with_partners:
+            partners = self.partners()
+            for partner in partners:
+                greet(partner)
+            count = count + len(partners)
+        pl.semaphore_wait(semaphore, count)
+
+
+class Gather:
+    SEMS = 5
+
+    def __init__(self, place, full, sems):
+        self.place, self.full = place, full
+        self.line_in, self.core_in, self.right_out, self.left_out, self.core_out = sems
+        self.rows = full.shape[0] // (2 * place.chips)
+
+    @classmethod
+    def scratch(cls, chips):
+        return [pltpu.SemaphoreType.DMA((chips,)) for _ in range(cls.SEMS)]
+
+    def block(self, chip, core):
+        base = pl.multiple_of((chip * 2 + core) * self.rows, self.rows)
+        return self.full.at[pl.ds(base, self.rows), :]
+
+    def own(self):
+        return self.block(self.place.chip, self.place.core)
+
+    def right(self, which):
+        place, part = self.place, self.block(which, self.place.core)
+        target = place.at(jnp.minimum(place.chip + 1, place.chips - 1), place.core)
+        return remote(part, part, self.right_out.at[which], self.line_in.at[which], target)
+
+    def left(self, which):
+        place, part = self.place, self.block(which, self.place.core)
+        target = place.at(jnp.maximum(place.chip - 1, 0), place.core)
+        return remote(part, part, self.left_out.at[which], self.line_in.at[which], target)
+
+    def across(self, which, core):
+        place, part = self.place, self.block(which, core)
+        target = place.at(place.chip, 1 - place.core)
+        return remote(part, part, self.core_out.at[which], self.core_in.at[which], target)
+
+    def begin(self):
+        chip, chips = self.place.chip, self.place.chips
+        pl.when(chip < chips - 1)(lambda: self.right(chip).start())
+        pl.when(chip > 0)(lambda: self.left(chip).start())
+        self.across(chip, self.place.core).start()
+
+    def pass_on(self, step):
+        chip, chips, core = self.place.chip, self.place.chips, self.place.core
+        low, high = chip - 1 - step, chip + 1 + step
+
+        @pl.when(low >= 0)
+        def _():
+            self.right(low).wait_recv()
+            pl.when(chip < chips - 1)(lambda: self.right(low).start())
+            self.across(low, core).start()
+
+        @pl.when(high < chips)
+        def _():
+            self.left(high).wait_recv()
+            pl.when(chip > 0)(lambda: self.left(high).start())
+            self.across(high, core).start()
+
+    def wait_chip(self, which):
+        self.across(which, 1 - self.place.core).wait_recv()
+
+    def each_new(self, step, use):
+        low, high = self.place.chip - 1 - step, self.place.chip + 1 + step
+
+        @pl.when(low >= 0)
+        def _():
+            self.wait_chip(low)
+            use(low)
+
+        @pl.when(high < self.place.chips)
+        def _():
+            self.wait_chip(high)
+            use(high)
+
+    def drain(self):
+        chip, chips, core = self.place.chip, self.place.chips, self.place.core
+
+        def one(which, _):
+            self.across(which, core).wait_send()
+            pl.when((which <= chip) & (chip < chips - 1))(lambda: self.right(which).wait_send())
+            pl.when((which >= chip) & (chip > 0))(lambda: self.left(which).wait_send())
+            return 0
+
+        lax.fori_loop(0, chips, one, 0)
+
+
+class Scatter:
+    def __init__(self, place, work, scratch):
+        self.place, self.work = place, work
+        self.out, self.side, self.line = scratch[:3]
+        self.core_out, self.core_in, self.line_out, self.line_in = scratch[3:]
+        chip, chips = place.chip, place.chips
+        self.near = jnp.minimum(chip, chips - 1 - chip)
+        self.alone = chips - 1 - 2 * self.near
+        self.flip = jnp.where(chip * 2 < chips, 0, 1)
+        self.lag = jnp.where(self.near > 0, 1, 0)
+
+    @staticmethod
+    def scratch(chips, rows, width):
+        return [
+            pltpu.VMEM((chips, rows, width), LOW),
+            pltpu.VMEM((chips, rows, width), LOW),
+            pltpu.VMEM((chips + 1, rows, width), LOW),
+            pltpu.SemaphoreType.DMA((chips,)),
+            pltpu.SemaphoreType.DMA((chips,)),
+            pltpu.SemaphoreType.DMA((chips,)),
+            pltpu.SemaphoreType.DMA((chips + 1,)),
+        ]
+
+    SCRATCH = 7
+
+    def order(self, turn):
+        chips = self.place.chips
+        later = jnp.maximum(turn - self.alone, 0)
+        pair = later // 2
+        far = jnp.where(turn < self.alone, chips - 1 - turn, chips - 1 - self.alone - pair)
+        which = jnp.where((turn >= self.alone) & (later % 2 == 1), pair, far)
+        which = jnp.where(turn == chips - 1, self.near, which)
+        return jnp.where(self.flip == 1, chips - 1 - which, which)
+
+    def across(self, which):
+        place = self.place
+        return remote(
+            self.out.at[which],
+            self.side.at[which],
+            self.core_out.at[which],
+            self.core_in.at[which],
+            place.at(place.chip, 1 - place.core),
+        )
+
+    def right(self, which):
+        place = self.place
+        slot = jnp.where(which == place.chip + 1, place.chips, which)
+        return remote(
+            self.out.at[which],
+            self.line.at[slot],
+            self.line_out.at[which],
+            self.line_in.at[slot],
+            place.at(jnp.minimum(place.chip + 1, place.chips - 1), place.core),
+        )
+
+    def left(self, which):
+        place = self.place
+        return remote(
+            self.out.at[which],
+            self.line.at[which],
+            self.line_out.at[which],
+            self.line_in.at[which],
+            place.at(jnp.maximum(place.chip - 1, 0), place.core),
+        )
+
+    def arrived(self, slot):
+        place = self.place
+        part = self.line.at[slot]
+        other = place.at(place.chip, 1 - place.core)
+        remote(part, part, self.line_out.at[0], self.line_in.at[slot], other).wait_recv()
+
+    def produce(self, turn):
+        which = self.order(turn)
+        self.out[which] = self.work(which, 1 - self.place.core).astype(LOW)
+        self.across(which).start()
+
+    def chip_sum(self, which):
+        mine = self.work(which, self.place.core)
+        self.across(which).wait()
+        return mine + self.side[which].astype(jnp.float32)
+
+    def send(self, which, upstream, copy):
+        total = self.chip_sum(which)
+
+        @pl.when(upstream)
+        def _():
+            self.arrived(which)
+            self.out[which] = (total + self.line[which].astype(jnp.float32)).astype(LOW)
+
+        @pl.when(jnp.logical_not(upstream))
+        def _():
+            self.out[which] = total.astype(LOW)
+
+        copy(which).start()
+
+    def first(self):
+        pl.when(self.lag == 1)(lambda: self.produce(0))
+
+    def slot(self, number):
+        chip, chips = self.place.chip, self.place.chips
+        self.produce(number + self.lag)
+        right = chips - 1 - (number - chip)
+        left = number - (chips - 1 - chip)
+        pl.when((number >= chip) & (right > chip))(
+            lambda: self.send(right, chip > 0, self.right)
+        )
+        pl.when((left >= 0) & (left < chip))(
+            lambda: self.send(left, chip < chips - 1, self.left)
+        )
+
+    def last(self):
+        pl.when(self.lag == 0)(lambda: self.produce(self.place.chips - 1))
+
+    def own(self, total):
+        chip, chips = self.place.chip, self.place.chips
+        total[...] = self.chip_sum(chip)
+
+        @pl.when(chip > 0)
+        def _():
+            self.arrived(chips)
+            total[...] += self.line[chips].astype(jnp.float32)
+
+        @pl.when(chip < chips - 1)
+        def _():
+            self.arrived(chip)
+            total[...] += self.line[chip].astype(jnp.float32)
+
+    def drain(self):
+        chip = self.place.chip
+
+        def one(which, _):
+            pl.when(which > chip)(lambda: self.right(which).wait_send())
+            pl.when(which < chip)(lambda: self.left(which).wait_send())
+            return 0
+
+        lax.fori_loop(0, self.place.chips, one, 0)
+
+
+class Spread:
+    def __init__(self, place, shard, whole, axis, sems):
+        self.place, self.whole, self.sems = place, whole, sems
+        size = shard.shape[axis]
+        here = pl.ds(pl.multiple_of(place.group * size, size), size)
+        index = tuple(here if a == axis else slice(None) for a in range(len(shard.shape)))
+        self.mine = whole.at[index]
+        self.mine[...] = shard[...].astype(LOW)
+
+    @staticmethod
+    def scratch(groups):
+        return [pltpu.SemaphoreType.DMA((groups,)), pltpu.SemaphoreType.DMA((groups,))]
+
+    def copy(self, offset):
+        return remote(
+            self.mine,
+            self.mine,
+            self.sems[0].at[offset],
+            self.sems[1].at[offset],
+            self.place.peer(offset),
+        )
+
+    def start(self):
+        for offset in range(1, self.place.groups):
+            self.copy(offset).start()
+
+    def wait(self):
+        for offset in range(1, self.place.groups):
+            self.copy(offset).wait()
+
+
+class Exchange:
+    def __init__(self, place, staged, landed, sems):
+        self.place, self.staged, self.landed = place, staged, landed
+        self.send, self.receive = sems
+
+    def copy(self, offset):
+        return remote(
+            self.staged.at[offset],
+            self.landed.at[offset],
+            self.send.at[offset],
+            self.receive.at[offset],
+            self.place.peer(offset),
+        )
+
+    def stay(self):
+        return pltpu.make_async_copy(self.staged.at[0], self.landed.at[0], self.send.at[0])
+
+    def wait(self):
+        def one(offset, _):
+            self.copy(offset).wait()
+            return 0
+
+        lax.fori_loop(1, self.place.groups, one, 0)
+        self.stay().wait()
+
+
+def pieces(number, slots, groups, fill):
+    low = 1 + number * (groups - 1) // slots
+    high = 1 + (number + 1) * (groups - 1) // slots
+
+    def one(offset, _):
+        fill(offset)
+        return 0
+
+    lax.fori_loop(low, high, one, 0)
+
+
+def line_call(kernel, name, number, operands, out_shape, scratch, flops, in_hbm=(), from_hbm=()):
+    whole, hbm = pl.BlockSpec(memory_space=pltpu.VMEM), pl.BlockSpec(memory_space=pl.ANY)
+    ins = [hbm if n in from_hbm else whole for n in range(len(operands))]
+    outs = [hbm if n in in_hbm else whole for n in range(len(out_shape))]
+    return pl.pallas_call(
+        kernel,
+        out_shape=out_shape,
+        in_specs=ins,
+        out_specs=outs,
+        scratch_shapes=scratch,
+        compiler_params=pltpu.CompilerParams(
+            collective_id=number, has_side_effects=True, vmem_limit_bytes=VMEM_BYTES
+        ),
+        cost_estimate=pl.CostEstimate(flops=flops, bytes_accessed=0, transcendentals=0),
+        name=name,
+    )(*operands)
+
+
+COST_FLOPS = 80_000_000_000
+
+
+def shape(dims, kind=LOW):
+    return jax.ShapeDtypeStruct(dims, kind)
+
+
+def split_refs(refs, *counts):
+    parts, at = [], 0
+    for count in counts:
+        parts.append(refs[at : at + count])
+        at += count
+    return parts
+
+
+def gather_project(groups, chips, tokens, gain, shift, shards, bias, tables):
+    rows, width = tokens.shape
+    length = rows * 2 * chips
+    qkv_shard, out_shard, gate_shard = shards
+    out_width = qkv_shard.shape[2]
+    hidden = gate_shard.shape[1]
+    tile = tables[0].shape[1]
+
+    def kernel(
+        x_ref, gain_ref, shift_ref, qkv_ref, out_ref, gate_ref, bias_ref,
+        cos_ref, sin_low_ref, sin_high_ref,
+        full, weights, out_whole, gate_whole, q_ref, k_ref, v_ref, *sems
+    ):
+        place = Place(groups, chips)
+        line, one, two, three = split_refs(sems, Gather.SEMS, 2, 2, 2)
+        gather = Gather(place, full, line)
+        normed, _, _ = layer_norm_parts(
+            x_ref[...].astype(jnp.float32), gain_ref[...], shift_ref[...]
+        )
+        gather.own()[...] = normed.astype(LOW)
+        spread_qkv = Spread(place, qkv_ref, weights, 1, one)
+        place.barrier(True)
+        gather.begin()
+        spread_qkv.start()
+        spread_out = Spread(place, out_ref, out_whole, 1, two)
+        spread_out.start()
+        spread_gate = Spread(place, gate_ref, gate_whole, 0, three)
+        spread_gate.start()
+
+        def work(chip):
+            base = pl.multiple_of(chip * 2 * rows, 2 * rows)
+            here = pl.ds(base, 2 * rows)
+            values = full[here, :]
+            for number, ref in enumerate((q_ref, k_ref, v_ref)):
+                result = dot(values, weights[number]) + bias_ref[number : number + 1, :]
+                if number < 2:
+                    parts = [
+                        rope_tile(
+                            result[:, t * tile : (t + 1) * tile],
+                            cos_ref[here, :],
+                            sin_low_ref[here, :],
+                            sin_high_ref[here, :],
+                            1.0,
+                        )
+                        for t in range(out_width // tile)
+                    ]
+                    result = jnp.concatenate(parts, axis=1) if len(parts) > 1 else parts[0]
+                ref[here, :] = result.astype(LOW)
+
+        gather.pass_on(0)
+        spread_qkv.wait()
+        gather.wait_chip(place.chip)
+        work(place.chip)
+
+        def step(number, _):
+            pl.when(number > 0)(lambda: gather.pass_on(number))
+            gather.each_new(number, work)
+            return 0
+
+        lax.fori_loop(0, chips - 1, step, 0)
+        gather.drain()
+        spread_out.wait()
+        spread_gate.wait()
+
+    head_shape = shape((length, out_width))
+    return line_call(
+        kernel,
+        "gather_project",
+        1,
+        (tokens, gain, shift, *shards, bias, *tables),
+        [
+            shape((length, width)),
+            shape((3, width, out_width)),
+            shape((out_width, width)),
+            shape((width, hidden)),
+            head_shape,
+            head_shape,
+            head_shape,
+        ],
+        Gather.scratch(chips) + Spread.scratch(groups) * 3,
+        COST_FLOPS,
+    )
+
+
+def scatter_heads(groups, chips, qkv, start, weight, tokens, grads, shards):
+    rows, width = tokens.shape
+    queries = qkv[0]
+    length, head_width = queries.shape
+    heads = head_width // HD
+    up_shard, down_shard = shards
+
+    def kernel(
+        q_ref, k_ref, v_ref, start_ref, w_ref, x_ref, og_ref, up_ref, down_ref,
+        mid_ref, ctx_ref, lse_ref, full, up_whole, down_whole,
+        v_turned, acc, stats, *rest
+    ):
+        place = Place(groups, chips)
+        for part in range(length // BLK):
+            here = slice(part * BLK, (part + 1) * BLK)
+            v_turned[:, here] = v_ref[here, :].T
+        scratch, line, one, two = split_refs(rest, Scatter.SCRATCH, Gather.SEMS, 2, 2)
+        gather = Gather(place, full, line)
+        gather.own()[...] = og_ref[...]
+        spread_up = Spread(place, up_ref, up_whole, 0, one)
+        spread_down = Spread(place, down_ref, down_whole, 1, two)
+        place.barrier(True)
+        gather.begin()
+        spread_up.start()
+        spread_down.start()
+        masks = head_masks(head_width, LOW)
+
+        def work(chip, core):
+            block = chip * 2 + core
+            base = pl.multiple_of(block * rows, rows)
+            here = pl.ds(base, rows)
+            values = (q_ref[here, :] * 0.125).astype(LOW)
+            masked = [values * m for m in masks]
+            starts = start_ref[:, here]
+            query_ids = base + lax.broadcasted_iota(jnp.int32, (1, rows), 1)
+            acc[...] = jnp.zeros_like(acc)
+            stats[0:8, :] = jnp.full((8, rows), NEG, jnp.float32)
+            stats[8:16, :] = jnp.zeros((8, rows), jnp.float32)
+
+            def step(number, _):
+                attend(number, rows, k_ref, v_turned, masked, starts, query_ids, acc, stats)
+                return 0
+
+            lax.fori_loop(jnp.maximum(block - LONGEST // rows, 0), block + 1, step, 0)
+            for h in range(heads):
+                band = slice(h * HD, (h + 1) * HD)
+                acc[band, :] = acc[band, :] / stats[8 + h : 9 + h, :]
+            context = acc[...].T.astype(LOW)
+            ctx_ref[here, :] = context
+            total = jnp.where(stats[8:16, :] > 0, stats[8:16, :], 1.0)
+            lse_ref[:, here] = stats[0:8, :] + jnp.log(total)
+            return dot(context, w_ref[...])
+
+        scatter = Scatter(place, work, scratch)
+        scatter.first()
+
+        def step(number, _):
+            scatter.slot(number)
+            gather.pass_on(number)
+            return 0
+
+        lax.fori_loop(0, chips - 1, step, 0)
+        scatter.last()
+        scatter.own(mid_ref)
+        mid_ref[...] += x_ref[...].astype(jnp.float32)
+
+        def here_too(which, _):
+            gather.wait_chip(which)
+            return 0
+
+        lax.fori_loop(0, chips, here_too, 0)
+        gather.drain()
+        scatter.drain()
+        spread_up.wait()
+        spread_down.wait()
+
+    return line_call(
+        kernel,
+        "scatter_heads",
+        2,
+        (*qkv, start, weight, tokens, grads, *shards),
+        [
+            shape((rows, width), jnp.float32),
+            shape((length, head_width)),
+            shape((8, length), jnp.float32),
+            shape((length, width)),
+            shape((width, up_shard.shape[1])),
+            shape((down_shard.shape[0], width)),
+        ],
+        [
+            pltpu.VMEM((head_width, length), LOW),
+            pltpu.VMEM((head_width, rows), jnp.float32),
+            pltpu.VMEM((16, rows), jnp.float32),
+        ]
+        + Scatter.scratch(chips, rows, width)
+        + Gather.scratch(chips)
+        + Spread.scratch(groups) * 2,
+        COST_FLOPS,
+    )
+
+
+def gather_hidden(groups, chips, middle, gain, shift, gate_weight, up_weight):
+    rows, width = middle.shape
+    length = rows * 2 * chips
+    hidden = gate_weight.shape[1]
+
+    def kernel(mid_ref, gain_ref, shift_ref, wg_ref, wu_ref, full, hid_ref, one_ref, two_ref, *line):
+        place = Place(groups, chips)
+        gather = Gather(place, full, line)
+        normed, _, _ = layer_norm_parts(mid_ref[...], gain_ref[...], shift_ref[...])
+        gather.own()[...] = normed.astype(LOW)
+        place.barrier()
+        gather.begin()
+
+        def work(chip):
+            for half in range(2):
+                here = pl.ds(pl.multiple_of((chip * 2 + half) * rows, rows), rows)
+                values = full[here, :]
+                gate = dot(values, wg_ref[...])
+                up = dot(values, wu_ref[...])
+                sigmoid = 1.0 / (1.0 + jnp.exp(-gate))
+                activated = gate * sigmoid
+                hid_ref[here, :] = (activated * up).astype(LOW)
+                slope = sigmoid * (1.0 + gate * (1.0 - sigmoid))
+                one_ref[here, :] = (up * slope).astype(LOW)
+                two_ref[here, :] = activated.astype(LOW)
+
+        gather.wait_chip(place.chip)
+        work(place.chip)
+
+        def step(number, _):
+            gather.pass_on(number)
+            gather.each_new(number, work)
+            return 0
+
+        lax.fori_loop(0, chips - 1, step, 0)
+        gather.drain()
+
+    hidden_shape = shape((length, hidden))
+    return line_call(
+        kernel,
+        "gather_hidden",
+        3,
+        (middle, gain, shift, gate_weight, up_weight),
+        [shape((length, width)), hidden_shape, hidden_shape, hidden_shape],
+        Gather.scratch(chips),
+        COST_FLOPS,
+    )
+
+
+def scatter_hidden(groups, chips, grads, hidden_low, factors, down, gate_weight, up_weight):
+    length, width = grads.shape
+    rows = length // (2 * chips)
+    hidden = down.shape[0]
+    part = width // groups
+
+    def kernel(
+        og_ref, hid_ref, one_ref, two_ref, down_ref, wg_ref, wu_ref,
+        gg_ref, ug_ref, sum_ref, landed, staged, *rest
+    ):
+        place = Place(groups, chips)
+        scratch, sems = split_refs(rest, Scatter.SCRATCH, 2)
+        place.barrier(True)
+
+        def work(chip, core):
+            here = pl.ds(pl.multiple_of((chip * 2 + core) * rows, rows), rows)
+            hidden_grad = dot(og_ref[here, :], down_ref[...], NT)
+            gate_grad = (hidden_grad * one_ref[here, :].astype(jnp.float32)).astype(LOW)
+            up_grad = (hidden_grad * two_ref[here, :].astype(jnp.float32)).astype(LOW)
+            gg_ref[here, :] = gate_grad
+            ug_ref[here, :] = up_grad
+            return dot(gate_grad, wg_ref[...], NT) + dot(up_grad, wu_ref[...], NT)
+
+        exchange = Exchange(place, staged, landed, sems)
+
+        def fill(offset):
+            block = lax.rem(place.group + offset, groups)
+            columns = pl.ds(pl.multiple_of(block * part, part), part)
+            staged[offset] = dot(hid_ref[...], og_ref[:, columns], TN).astype(LOW)
+
+        def fill_send(offset):
+            fill(offset)
+            exchange.copy(offset).start()
+
+        scatter = Scatter(place, work, scratch)
+        scatter.first()
+
+        def step(number, _):
+            scatter.slot(number)
+            pieces(number, chips - 1, groups, fill_send)
+            return 0
+
+        lax.fori_loop(0, chips - 1, step, 0)
+        scatter.last()
+        fill(0)
+        exchange.stay().start()
+        scatter.own(sum_ref)
+        scatter.drain()
+        exchange.wait()
+
+    return line_call(
+        kernel,
+        "scatter_hidden",
+        4,
+        (grads, hidden_low, *factors, down, gate_weight, up_weight),
+        [
+            shape((length, hidden)),
+            shape((length, hidden)),
+            shape((rows, width), jnp.float32),
+            shape((groups, hidden, part)),
+        ],
+        [pltpu.VMEM((groups, hidden, part), LOW)]
+        + Scatter.scratch(chips, rows, width)
+        + Spread.scratch(groups),
+        COST_FLOPS,
+        in_hbm=(3,),
+    )
+
+
+def gather_context(
+    groups, chips, middle, normed_grad, out_grad, gain, shift, weight, hidden_low, down, normed, pair
+):
+    rows, width = middle.shape
+    length = rows * 2 * chips
+    out_width = weight.shape[0]
+    hidden = down.shape[0]
+    part = width // groups
+
+    def kernel(
+        mid_ref, ng_ref, og_ref, gain_ref, shift_ref, w_ref, hid_ref, down_ref, a_ref, gg_ref, ug_ref,
+        full, cg_ref, mg_ref, sums_ref, out_ref, landed_gate, landed_up,
+        total, staged_gate, staged_up, columns_in, load, *rest
+    ):
+        place = Place(groups, chips)
+        scratch, line, one, two = split_refs(rest, Scatter.SCRATCH, Gather.SEMS, 2, 2)
+
+        def fetch(offset):
+            block = lax.rem(place.group + offset, groups)
+            columns = pl.ds(pl.multiple_of(block * part, part), part)
+            slot = lax.rem(offset, 2)
+            return pltpu.make_async_copy(a_ref.at[:, columns], columns_in.at[slot], load.at[slot])
+
+        arrive = pltpu.make_async_copy(ng_ref, total, load.at[3])
+        arrive.start()
+        fetch(1).start()
+        gather = Gather(place, full, line)
+        _, plain, inverse = layer_norm_parts(mid_ref[...], gain_ref[...], shift_ref[...])
+        arrive.wait()
+        back, gain_grad, shift_grad = layer_norm_back(total[...], plain, inverse, gain_ref[...])
+        mid_grad = og_ref[...].astype(jnp.float32) + back
+        total[...] = mid_grad
+        keep = pltpu.make_async_copy(total, mg_ref, load.at[2])
+        keep.start()
+        sums_ref[0:1, :] = gain_grad[None, :]
+        sums_ref[1:2, :] = shift_grad[None, :]
+        gather.own()[...] = mid_grad.astype(LOW)
+        place.barrier(True)
+        gather.begin()
+
+        def back_work(chip):
+            here = pl.ds(pl.multiple_of(chip * 2 * rows, 2 * rows), 2 * rows)
+            cg_ref[here, :] = dot(full[here, :], w_ref[...], NT).astype(LOW)
+
+        def out_work(chip, core):
+            here = pl.ds(pl.multiple_of((chip * 2 + core) * rows, rows), rows)
+            return dot(hid_ref[here, :], down_ref[...])
+
+        exchange_gate = Exchange(place, staged_gate, landed_gate, one)
+        exchange_up = Exchange(place, staged_up, landed_up, two)
+
+        def fill(offset):
+            fetch(offset).wait()
+            pl.when(offset > 0)(lambda: fetch(lax.rem(offset + 1, groups)).start())
+            values = columns_in[lax.rem(offset, 2)]
+            staged_gate[offset] = dot(values, gg_ref[...], TN).astype(LOW)
+            staged_up[offset] = dot(values, ug_ref[...], TN).astype(LOW)
+
+        def fill_send(offset):
+            fill(offset)
+            exchange_gate.copy(offset).start()
+            exchange_up.copy(offset).start()
+
+        scatter = Scatter(place, out_work, scratch)
+        scatter.first()
+
+        def step(number, _):
+            scatter.slot(number)
+            pieces(number, chips - 1, groups, fill_send)
+            gather.pass_on(number)
+
+            @pl.when(number == 0)
+            def _():
+                gather.wait_chip(place.chip)
+                back_work(place.chip)
+
+            gather.each_new(number, back_work)
+            return 0
+
+        lax.fori_loop(0, chips - 1, step, 0)
+        scatter.last()
+        fill(jnp.int32(0))
+        exchange_gate.stay().start()
+        exchange_up.stay().start()
+        keep.wait()
+        scatter.own(total)
+        out_ref[...] = (mid_ref[...] + total[...]).astype(LOW)
+        gather.drain()
+        scatter.drain()
+        exchange_gate.wait()
+        exchange_up.wait()
+
+    return line_call(
+        kernel,
+        "gather_context",
+        5,
+        (middle, normed_grad, out_grad, gain, shift, weight, hidden_low, down, normed, *pair),
+        [
+            shape((length, width)),
+            shape((length, out_width)),
+            shape((rows, width), jnp.float32),
+            shape((2, width), jnp.float32),
+            shape((rows, width)),
+            shape((groups, part, hidden)),
+            shape((groups, part, hidden)),
+        ],
+        [
+            pltpu.VMEM((rows, width), jnp.float32),
+            pltpu.VMEM((groups, part, hidden), LOW),
+            pltpu.VMEM((groups, part, hidden), LOW),
+            pltpu.VMEM((2, length, part), LOW),
+            pltpu.SemaphoreType.DMA((4,)),
+        ]
+        + Scatter.scratch(chips, rows, width)
+        + Gather.scratch(chips)
+        + Spread.scratch(groups) * 2,
+        COST_FLOPS,
+        in_hbm=(2, 5, 6),
+        from_hbm=(1, 8),
+    )
+
+
+def scatter_triple(
+    groups, chips, triple, weights, tokens, gain, shift, mid_grad, sums, bias_sums, normed, context, grads
+):
+    length, in_width = triple[0].shape
+    rows = length // (2 * chips)
+    width = weights.shape[1]
+    part = width // groups
+
+    def kernel(
+        q_ref, k_ref, v_ref, w_ref, x_ref, gain_ref, shift_ref, mg_ref, sums_ref, bias_ref,
+        a_ref, ctx_ref, full_ref,
+        in_ref, small_ref, landed_qkv, landed_out,
+        total, staged_qkv, staged_out, small_in, small_out, small_recv, *rest
+    ):
+        place = Place(groups, chips)
+        scratch, one, two = split_refs(rest, Scatter.SCRATCH, 2, 2)
+        place.barrier(True, True)
+
+        def work(chip, core):
+            here = pl.ds(pl.multiple_of((chip * 2 + core) * rows, rows), rows)
+            term = dot(q_ref[here, :], w_ref[0], NT)
+            term = term + dot(k_ref[here, :], w_ref[1], NT)
+            return term + dot(v_ref[here, :], w_ref[2], NT)
+
+        exchange_qkv = Exchange(place, staged_qkv, landed_qkv, one)
+        exchange_out = Exchange(place, staged_out, landed_out, two)
+
+        def fill(offset):
+            block = lax.rem(place.group + offset, groups)
+            columns = pl.ds(pl.multiple_of(block * part, part), part)
+            values = a_ref[:, columns]
+            for number, ref in enumerate((q_ref, k_ref, v_ref)):
+                staged_qkv[offset, number] = dot(values, ref[...], TN).astype(LOW)
+            staged_out[offset] = dot(ctx_ref[...], full_ref[:, columns], TN).astype(LOW)
+
+        def fill_send(offset):
+            fill(offset)
+            exchange_qkv.copy(offset).start()
+            exchange_out.copy(offset).start()
+
+        scatter = Scatter(place, work, scratch)
+        scatter.first()
+
+        def step(number, _):
+            scatter.slot(number)
+            pieces(number, chips - 1, groups, fill_send)
+            return 0
+
+        lax.fori_loop(0, chips - 1, step, 0)
+        scatter.last()
+        fill(0)
+        exchange_qkv.stay().start()
+        exchange_out.stay().start()
+        scatter.own(total)
+        _, plain, inverse = layer_norm_parts(
+            x_ref[...].astype(jnp.float32), gain_ref[...], shift_ref[...]
+        )
+        back, gain_grad, shift_grad = layer_norm_back(total[...], plain, inverse, gain_ref[...])
+        in_ref[...] = (mg_ref[...] + back).astype(LOW)
+        small_ref[...] = jnp.zeros_like(small_ref)
+        small_ref[0:1, :] = gain_grad[None, :]
+        small_ref[1:2, :] = sums_ref[0:1, :]
+        small_ref[2:3, :] = shift_grad[None, :]
+        small_ref[3:4, :] = sums_ref[1:2, :]
+        small_ref[4:7, 0:in_width] = bias_ref[0:3, :]
+        for number, partner in enumerate(place.partners()):
+            swap = remote(
+                small_ref,
+                small_in.at[number],
+                small_out.at[number],
+                small_recv.at[number],
+                partner,
+            )
+            swap.start()
+            swap.wait()
+            kept = 8 if 2**number < groups else 4
+            small_ref[0:kept, :] += small_in[number, 0:kept, :]
+        scatter.drain()
+        exchange_qkv.wait()
+        exchange_out.wait()
+
+    doublings = (groups.bit_length() - 1) + (2 * chips).bit_length() - 1
+    return line_call(
+        kernel,
+        "scatter_triple",
+        6,
+        (*triple, weights, tokens, gain, shift, mid_grad, sums, bias_sums, normed, context, grads),
+        [
+            shape((rows, width)),
+            shape((8, width), jnp.float32),
+            shape((groups, 3, part, in_width)),
+            shape((groups, in_width, part)),
+        ],
+        [
+            pltpu.VMEM((rows, width), jnp.float32),
+            pltpu.VMEM((groups, 3, part, in_width), LOW),
+            pltpu.VMEM((groups, in_width, part), LOW),
+            pltpu.VMEM((doublings, 8, width), jnp.float32),
+            pltpu.SemaphoreType.DMA((doublings,)),
+            pltpu.SemaphoreType.DMA((doublings,)),
+        ]
+        + Scatter.scratch(chips, rows, width)
+        + Spread.scratch(groups) * 2,
+        COST_FLOPS,
+        in_hbm=(2, 3),
+    )
+
+
 def adam_update(master, gradient, moment_one, moment_two, correct_one, correct_two, rate):
     one_new = 0.9 * moment_one + 0.1 * gradient
     two_new = 0.999 * moment_two + 0.001 * gradient * gradient
@@ -319,6 +1178,8 @@
 
 
 def per_device(
+    groups,
+    chips,
     inputs,
     out_grad,
     segments,
@@ -344,143 +1205,80 @@
     second_gain,
     second_shift,
 ):
-    low_type = jnp.bfloat16
-    full_type = jnp.float32
-    qkv_all, gate_up_all, out_all, down_all = (
-        lax.all_gather(w_qkv.astype(low_type), "dp", axis=1, tiled=True),
-        lax.all_gather(w_gate_up.astype(low_type), "dp", axis=1, tiled=True),
-        lax.all_gather(w_out.astype(low_type), "dp", axis=1, tiled=True),
-        lax.all_gather(w_down.astype(low_type), "dp", axis=1, tiled=True),
-    )
     length = segments.shape[1]
     head_width = w_qkv.shape[2]
-    inputs_full = inputs.astype(full_type)
-    normed_one, plain_one, inverse_one = layer_norm_parts(inputs_full, norm_gain[0], norm_bias[0])
-    normed_one = normed_one.astype(low_type)
-    normed_all = lax.all_gather(normed_one, "tensor", axis=0, tiled=True)
-    projected = jnp.einsum("rd,cdh->crh", normed_all, qkv_all, preferred_element_type=full_type)
+    gains = (norm_gain[0:1], norm_gain[1:2])
+    shifts = (norm_bias[0:1], norm_bias[1:2])
     place = positions(segments)[0]
     start = jnp.arange(length, dtype=jnp.int32) - place
     low_blocks = start[::BLK] // BLK
     start = start[None, :]
-    tables = rotary_tables(place, head_width)
-    half_tables = tuple(t[:, : min(head_width, 128)] for t in tables)
-    query_low = rope_whole(projected[0] + qkv_bias[0], tables).astype(low_type)
-    key_low = rope_whole(projected[1] + qkv_bias[1], tables).astype(low_type)
-    value_low = (projected[2] + qkv_bias[2]).astype(low_type)
-    context_flat, lse = attention_forward(low_blocks, query_low, key_low, value_low, start)
-    middle = inputs_full + lax.psum_scatter(
-        jnp.dot(context_flat, out_all, preferred_element_type=full_type).astype(low_type),
-        "tensor",
-        scatter_dimension=0,
-        tiled=True,
-    ).astype(full_type)
-    normed_two, plain_two, inverse_two = layer_norm_parts(middle, norm_gain[1], norm_bias[1])
-    normed_two = normed_two.astype(low_type)
-    gate_pair = jnp.einsum(
-        "rd,cdf->rcf",
-        lax.all_gather(normed_two, "tensor", axis=0, tiled=True),
-        gate_up_all,
-        preferred_element_type=full_type,
-    )
-    gate_parts = (gate_pair,)
-    gate_proj = gate_parts[0][:, 0]
-    up_proj = gate_parts[0][:, 1]
-    sigmoid_gate = jax.nn.sigmoid(gate_proj)
-    activated = gate_proj * sigmoid_gate
-    hidden_low = (activated * up_proj).astype(low_type)
-    outputs = (
-        middle
-        + lax.psum_scatter(
-            jnp.dot(hidden_low, down_all, preferred_element_type=full_type).astype(jnp.bfloat16),
-            "tensor",
-            scatter_dimension=0,
-            tiled=True,
-        ).astype(jnp.float32)
-    ).astype(low_type)
-    mlp_grad = lax.all_gather(out_grad, "tensor", axis=0, tiled=True)
-    grad_down = jnp.einsum("rf,rd->fd", hidden_low, mlp_grad, preferred_element_type=full_type)
-    hidden_grad = jnp.einsum("rd,fd->rf", mlp_grad, down_all, preferred_element_type=full_type)
-    gate_grad = hidden_grad * up_proj * (sigmoid_gate * (1.0 + gate_proj * (1.0 - sigmoid_gate)))
-    up_grad = hidden_grad * activated
-    pair_grad = jnp.stack([gate_grad, up_grad], axis=1).astype(low_type)
-    normed_two_grad = lax.psum_scatter(
-        jnp.einsum("rcf,cdf->rd", pair_grad, gate_up_all, preferred_element_type=full_type).astype(
-            low_type
-        ),
-        "tensor",
-        scatter_dimension=0,
-        tiled=True,
-    ).astype(full_type)
-    rows_grad = pair_grad
-    grad_gate_up = jnp.einsum(
-        "rd,rcf->cdf",
-        lax.all_gather(normed_two, "tensor", axis=0, tiled=True),
-        rows_grad,
-        preferred_element_type=full_type,
-    )
-    middle_ln_grad, gain_two_grad, shift_two_grad = layer_norm_back(
-        normed_two_grad, plain_two, inverse_two, norm_gain[1]
-    )
-    middle_grad = out_grad.astype(full_type) + middle_ln_grad
-    attn_grad_all = lax.all_gather(middle_grad.astype(low_type), "tensor", axis=0, tiled=True)
-    grad_out = jnp.einsum(
-        "rh,rd->hd", context_flat, attn_grad_all, preferred_element_type=full_type
-    )
-    context_grad = jnp.einsum(
-        "rd,hd->rh", attn_grad_all, out_all, preferred_element_type=full_type
-    ).astype(low_type)
-    query_grad, key_grad, value_grad, bias_sums = attention_backward(
-        low_blocks,
-        query_low,
-        key_low,
-        value_low,
-        start,
-        lse,
+    tables = rotary_tables(place, min(head_width, 128))
+
+    normed_one_all, qkv_all, out_all, gate_all, *qkv = gather_project(
+        groups,
+        chips,
+        inputs,
+        gains[0],
+        shifts[0],
+        (w_qkv, w_out, w_gate_up[0]),
+        qkv_bias,
+        tables,
+    )
+    middle, context_flat, lse, mlp_grad, up_all, down_all = scatter_heads(
+        groups, chips, qkv, start, out_all, inputs, out_grad, (w_gate_up[1], w_down)
+    )
+    normed_two_all, hidden_low, *factors = gather_hidden(
+        groups, chips, middle, gains[1], shifts[1], gate_all, up_all
+    )
+    gate_grad, up_grad, normed_two_grad, parts_down = scatter_hidden(
+        groups, chips, mlp_grad, hidden_low, factors, down_all, gate_all, up_all
+    )
+    attn_grad_all, context_grad, middle_grad, sums_two, outputs, parts_gate, parts_up = (
+        gather_context(
+            groups,
+            chips,
+            middle,
+            normed_two_grad,
+            out_grad,
+            gains[1],
+            shifts[1],
+            out_all,
+            hidden_low,
+            down_all,
+            normed_two_all,
+            (gate_grad, up_grad),
+        )
+    )
+    *triple, bias_sums = attention_backward(
+        low_blocks, *qkv, start, lse, context_flat, context_grad, tables
+    )
+    input_grad, small, parts_qkv, parts_out = scatter_triple(
+        groups,
+        chips,
+        triple,
+        qkv_all,
+        inputs,
+        gains[0],
+        shifts[0],
+        middle_grad,
+        sums_two,
+        bias_sums,
+        normed_one_all,
         context_flat,
-        context_grad,
-        half_tables,
-    )
-    triple_grad = jnp.stack([query_grad, key_grad, value_grad], axis=1)
-    grad_bias = bias_sums[:3]
-    normed_one_grad = lax.psum_scatter(
-        jnp.einsum("rch,cdh->rd", triple_grad, qkv_all, preferred_element_type=full_type).astype(
-            jnp.bfloat16
-        ),
-        "tensor",
-        scatter_dimension=0,
-        tiled=True,
-    ).astype(jnp.float32)
-    rows_grad = triple_grad
-    grad_qkv = jnp.einsum(
-        "rd,rch->cdh",
-        lax.all_gather(normed_one, "tensor", axis=0, tiled=True),
-        rows_grad,
-        preferred_element_type=full_type,
-    )
-    input_ln_grad, gain_one_grad, shift_one_grad = layer_norm_back(
-        normed_one_grad, plain_one, inverse_one, norm_gain[0]
-    )
-    input_grad = (middle_grad + input_ln_grad).astype(low_type)
-    grad_qkv, grad_gate_up, grad_out, grad_down = (
-        lax.psum_scatter(
-            grad_qkv.astype(jnp.bfloat16), "dp", scatter_dimension=1, tiled=True
-        ).astype(jnp.float32),
-        lax.psum_scatter(
-            grad_gate_up.astype(jnp.bfloat16), "dp", scatter_dimension=1, tiled=True
-        ).astype(jnp.float32),
-        lax.psum_scatter(
-            grad_out.astype(jnp.bfloat16), "dp", scatter_dimension=1, tiled=True
-        ).astype(jnp.float32),
-        lax.psum_scatter(
-            grad_down.astype(jnp.bfloat16), "dp", scatter_dimension=1, tiled=True
-        ).astype(jnp.float32),
-    )
-    grad_bias = lax.psum(grad_bias, "dp")
-    grad_gain, grad_shift = lax.psum(
-        (jnp.stack([gain_one_grad, gain_two_grad]), jnp.stack([shift_one_grad, shift_two_grad])),
-        ("dp", "tensor"),
-    )
+        attn_grad_all,
+    )
+
+    def add_parts(parts):
+        total = parts[0].astype(jnp.float32)
+        for offset in range(1, groups):
+            total = total + parts[offset].astype(jnp.float32)
+        return total
+
+    grad_qkv, grad_out, grad_down = add_parts(parts_qkv), add_parts(parts_out), add_parts(parts_down)
+    grad_gate_up = jnp.stack([add_parts(parts_gate), add_parts(parts_up)])
+    grad_bias = small[4:7, :head_width]
+    grad_gain, grad_shift = small[0:2], small[2:4]
     correct_one = 1.0 - 0.9**STEP
     correct_two = 1.0 - 0.999**STEP
     rates = (0.02, 0.3, 0.02, 0.02, 0.3, 0.3, 0.3)
@@ -602,5 +1400,6 @@
         P(),
     )
     return jax.shard_map(
-        per_device, mesh=mesh, in_specs=in_specs, out_specs=out_specs, check_vma=False
-    )
+        functools.partial(per_device, mesh.shape["dp"], mesh.shape["tensor"] // 2),
+        mesh=mesh, in_specs=in_specs, out_specs=out_specs, check_vma=False
+    )

time: 1160 us -> 746 us (0.64)
  waiting for transfers between devices: 794 us -> 0 us
  Pallas kernels: 53.9 us -> 664 us
  matrix products: 142 us -> 0 us
  blocking collectives: 49.3 us -> 0 us
  other arithmetic: 56.2 us -> 28.3 us
  between operations: 14.9 us -> 1.62 us
    pallas_call x1 -> x6, Pallas kernels: 22.4 us -> 628 us  [line_call(): pl.pallas_call(kernel, out_shape=out_shape, in_specs=ins, out_specs=outs,...]
    all_gather x8 -> x0, waiting for transfers between devices: 416 us -> none  [the longest x1 84.3 us: per_device(): normed_all = lax.all_gather(normed_one, 'tensor', axis=0, tiled=True)]
    reduce_scatter x8 -> x0, waiting for transfers between devices: 377 us -> none  [the longest x1 88.6 us: per_device(): lax.psum_scatter(jnp.dot(context_flat, out_all, preferred_element_type=fu...]
    dot_general x12 -> x0, matrix products: 142 us -> none  [the longest x1 19.4 us: per_device(): jnp.einsum('rd,cdf->rcf', lax.all_gather(normed_two, 'tensor', axis=0, ti...]
    psum x2 -> x0, blocking collectives: 49.3 us -> none  [the longest x1 39.8 us: per_device(): lax.psum((jnp.stack([gain_one_grad, gain_two_grad]), jnp.stack([shift_one...]
    convert_element_type x11 -> x0, other arithmetic: 22.7 us -> none  [the longest x1 4.88 us: per_device(): input_grad = (middle_grad + input_ln_grad).astype(low_type)]
    unnamed x125 -> x93, local copies, waits for them, and re-layouts: 28.2 us -> 35 us
    sub x7 -> x6, other arithmetic: 23.8 us -> 20.2 us  [adam_update(): return (master - rate * change, one_new, two_new)]
  transfers between devices with their start and end apart: 16 -> 0, of which waited for: 14 -> 0; matrix products, arithmetic and copies ran while one was open for 15% -> 0% of each run, Pallas kernels for 5% -> 0%
where the time goes in v2:
time: 746 us; the launch traced here: 737 us
  Pallas kernels  664 us (89%)
  local copies, waits for them, and re-layouts  43.1 us (6%)
  other arithmetic  28.3 us (4%)
    pallas_call x6, Pallas kernels, line_call(): pl.pallas_call(kernel, out_shape=out_shape, in_specs=ins, out_specs=outs,...  628 us
    pallas_call x1, Pallas kernels, attention_backward(): pl.pallas_call(backward_kernel, grid_spec=pltpu.PrefetchScalarGridSpec(nu...  36.5 us
    unnamed x93, local copies, waits for them, and re-layouts  35 us
    sub x6, other arithmetic, adam_update(): return (master - rate * change, one_new, two_new)  20.2 us

profile of v2, /device:TPU:0, one launch (start us, length us, event | category | flops | bytes accessed | tf_op | source)
XLA Modules:
  0.0 737.4 jit_solution(15509093228484537065)
XLA Ops:
  0.7 0.9 compare_select_fusion
  1.5 0.3 reduce-window.6
  1.8 0.2 slice_reduce_fusion
  2.0 0.2 reduce-window.9
  2.2 0.7 iota_subtract_fusion
  2.9 0.3 multiply_sine_fusion
  3.2 0.1 pad.10.clone
  3.3 0.1 pad.7.clone
  3.4 0.2 maximum_maximum_fusion.2
  3.6 0.1 tile.12
  3.7 1.3 copy.65.cos_ref
  5.0 0.1 tile.14
  5.1 1.3 copy.66.sin_low_ref
  6.4 0.1 tile.31
  6.5 1.3 copy.67.sin_high_ref
  7.8 0.6 fusion.17
  8.4 2.3 copy.64
  10.8 2.1 slice_bitcast_fusion
  12.8 0.6 copy-done.14
  13.4 94.8 %gather_project.1 = (bf16[2048,2048]{1,0:T(8,128)(2,1)}, bf16[3,2048,256]{2,1,0:T(8,128)(2,1)}, bf16[256,2048]{1,0:T(8,128)(2,1)}, bf16[2048,704]{1,0:T(8,128)(2...) custom-call(bf16[256,2048]{1,0:T(8,128)(2,1)} %x_ref.5, ...), custom_call_target="tpu_custom_call" | custom-call | flops 80000000000 | tf_op jit(solution)/shard_map/gather_project/pallas_call | solution.py:611
  108.2 0.1 broadcast.107
  108.3 0.6 subtract_subtract_fusion.start_ref
  108.9 107.1 %scatter_heads.1 = (f32[256,2048]{1,0:T(8,128)}, bf16[2048,256]{1,0:T(8,128)(2,1)}, f32[8,2048]{1,0:T(8,128)}, bf16[2048,2048]{1,0:T(8,128)(2,1)}, bf16[2048,704]{1,0:T(8,128)(2,1)}, /*index=5*/bf16[704,2048]{1,0:T(8,128)(2,1)}) custom-call(bf16[2048,256]{1,0:T(8,128)(2,1)} %get-tuple-element.66.q_ref, bf16[2048,256]{1,0:T(8,128)(2,1)} %get-tuple-element.67.k_ref, ...), custom_call_target="tpu_custom_call" | custom-call | flops 80000000000 | tf_op jit(solution)/shard_map/scatter_heads/pallas_call | solution.py:611
  216.0 86.3 %gather_hidden.1 = (bf16[2048,2048]{1,0:T(8,128)(2,1)}, bf16[2048,704]{1,0:T(8,128)(2,1)}, bf16[2048,704]{1,0:T(8,128)(2,1)}, bf16[2048,704]{1,0:T(8,128)(2,1)}) custom-call(f32[256,2048]{1,0:T(8,128)} %get-tuple-element.70.mid_ref, f32[1,2048]{1,0:T(1,128)} %get-tuple-element.209.gain_ref, f32[1,2048]{1,0:T(1,128)} %get-tuple-element.198.shift_ref, ...), custom_call_target="tpu_custom_call" | custom-call | flops 80000000000 | tf_op jit(solution)/shard_map/gather_hidden/pallas_call | solution.py:611
  302.4 100.6 %scatter_hidden.1 = (bf16[2048,704]{1,0:T(8,128)(2,1)}, bf16[2048,704]{1,0:T(8,128)(2,1)}, f32[256,2048]{1,0:T(8,128)}, bf16[4,704,512]{2,1,0:T(8,128)(2,1)}) custom-call(bf16[2048,2048]{1,0:T(8,128)(2,1)} %get-tuple-element.71.og_ref, bf16[2048,704]{1,0:T(8,128)(2,1)} %get-tuple-element.74.hid_ref, bf16[2048,704]{1,0:T(8,128)(2,1)} %get-tuple-element.75.one_ref, ...), custom_call_target="tpu_custom_call" | custom-call | flops 80000000000 | tf_op jit(solution)/shard_map/scatter_hidden/pallas_call | solution.py:611
  403.0 113.6 %gather_context.1 = (bf16[2048,2048]{1,0:T(8,128)(2,1)}, bf16[2048,256]{1,0:T(8,128)(2,1)}, f32[256,2048]{1,0:T(8,128)}, f32[2,2048]{1,0:T(2,128)}, bf16[256,204...) custom-call(f32[256,2048]{1,0:T(8,128)} %get-tuple-element.70.mid_ref, ...), custom_call_target="tpu_custom_call" | custom-call | flops 80000000000 | tf_op jit(solution)/shard_map/gather_context/pallas_call | solution.py:611
  516.5 3.5 convert_add_fusion
  520.1 1.5 convert_add_fusion.1
  521.6 0.9 copy-done.18
  522.4 2.3 copy.72
  524.7 3.6 copy.73
  528.4 8.0 %multiply_subtract_fusion = (f32[2,512,704]{2,1,0:T(8,128)}, f32[2,512,704]{2,1,0:T(8,128)}, f32[2,512,704]{2,1,0:T(8,128)}, f32[2,512,704]{2,1,0:T(8,128)}) fusion(f32[2,512,704]{2,1,0:T(8,128)S(1)} %copy-done.15, f32[1,512,704]{2,1,0:T(8,128)} %convert_add_fusion, f32[1,512,704]{2,1,0:T(8,128)} %convert_add_fusion.1, f32[2,512,704]{2,1,0:T(8,128)} %copy.72, ...), kind=kLoop, calls=%fused_computation.3 | loop fusion | flops 11534336 | bytes 23068672 | tf_op jit(solution)/shard_map/sub | solution.py:1177
  536.4 3.4 copy.76
  539.8 3.6 copy.77
  543.4 2.2 copy.78
  545.7 0.0 copy-start.9
  545.7 3.6 copy.79
  549.3 0.8 slice.108
  550.1 1.2 copy-done.3
  551.4 1.2 copy-done.4
  552.6 1.2 copy-done.5
  553.8 1.2 copy-done.6
  555.0 1.2 copy-done.7
  556.3 36.5 %attention_backward.1 = (bf16[2048,256]{1,0:T(8,128)(2,1)S(1)}, bf16[2048,256]{1,0:T(8,128)(2,1)S(1)}, bf16[2048,256]{1,0:T(8,128)(2,1)S(1)}, f32[8,256]{1,0:T(8,128)S(1)}) custom-call(s32[8]{0:T(128)S(1)} %and_select_fusion.low_ref, bf16[2048,256]{1,0:T(8,128)(2,1)S(1)} %copy-done.3, bf16[2048,256]{1,0:T(8,128)(2,1)S(1)} %copy-done.4, ...), custom_call_target="tpu_custom_call" | custom-call | tf_op jit(solution)/shard_map/attention_backward/pallas_call | solution.py:220
  592.8 0.0 copy-start.10
  592.8 1.0 copy-done.10
  593.8 1.0 copy-done.11
  594.7 1.0 copy-done.12
  595.7 0.6 copy-done.13
  596.3 125.4 %scatter_triple.1 = (bf16[256,2048]{1,0:T(8,128)(2,1)}, f32[8,2048]{1,0:T(8,128)}, bf16[4,3,512,256]{3,2,1,0:T(8,128)(2,1)}, bf16[4,256,512]{2,1,0:T(8,128)(2,1)}) custom-call(bf16[2048,256]{1,0:T(8,128)(2,1)} %copy-done.10, bf16[2048,256]{1,0:T(8,128)(2,1)} %copy-done.11, bf16[2048,256]{1,0:T(8,128)(2,1)} %copy-done.12, ...), custom_call_target="tpu_custom_call" | custom-call | flops 80000000000 | tf_op jit(solution)/shard_map/scatter_triple/pallas_call | solution.py:611
  721.7 0.0 copy-start.28
  721.7 0.0 copy-start.29
  721.8 6.2 multiply_subtract_fusion.1
  728.0 0.0 copy-start.31
  728.0 0.0 copy-start.35
  728.0 0.0 copy-start.36
  728.1 1.5 multiply_subtract_fusion.3
  729.7 0.7 multiply_subtract_fusion.4
  730.4 0.6 multiply_subtract_fusion.6
  731.1 0.1 copy-done.21
  731.2 3.1 multiply_subtract_fusion.2
  734.3 1.0 copy.82
  735.3 0.6 copy-done.25
  735.9 1.0 copy.83
  (70 shorter events, 0.2 us)
Async XLA Ops:
  6.4 1.4 copy-start.30
  6.4 1.4 copy-start.32
  10.8 2.7 copy-start.14
  516.5 3.5 copy-start.17
  520.0 2.4 copy-start.18
  524.7 3.6 copy-start.15
  539.8 3.6 copy-start.16
  545.7 4.4 copy-start
  545.7 4.4 copy-start.1
  545.7 4.4 copy-start.2
  545.7 4.4 copy-start.8
  545.7 4.4 copy-start.9
  550.1 1.2 copy-start.3
  551.4 1.2 copy-start.4
  552.6 1.2 copy-start.5
  553.8 1.2 copy-start.6
  555.0 1.2 copy-start.7
  592.8 1.0 copy-start.10
  593.8 1.0 copy-start.11
  594.7 1.0 copy-start.12
  595.7 0.6 copy-start.13
  596.3 125.4 %copy-start.20 = (f32[3,512,256]{2,1,0:T(8,128)S(1)}, f32[3,512,256]{2,1,0:T(8,128)}, u32[]{:S(2)}) copy-start(f32[3,512,256]{2,1,0:T(8,128)} %qkv_ref.1) | copy-start | bytes 4718596
  721.7 6.2 copy-start.26
  721.7 6.2 copy-start.27
  721.7 6.2 copy-start.28
  721.7 6.2 copy-start.29
  721.8 9.3 %copy-start.22 = (f32[704,512]{1,0:T(8,128)S(1)}, f32[704,512]{1,0:T(8,128)}, u32[]{:S(2)}) copy-start(f32[704,512]{1,0:T(8,128)} %param.37) | copy-start | bytes 4325380
  721.8 9.3 %copy-start.23 = (f32[704,512]{1,0:T(8,128)S(1)}, f32[704,512]{1,0:T(8,128)}, u32[]{:S(2)}) copy-start(f32[704,512]{1,0:T(8,128)} %param.44) | copy-start | bytes 4325380
  728.0 1.7 copy-start.31
  728.0 1.7 copy-start.33
  728.0 1.7 copy-start.34
  728.0 1.6 copy-start.35
  728.0 1.6 copy-start.36
  728.0 1.6 copy-start.37
  728.0 1.6 copy-start.38
  728.1 2.4 copy-start.39
  728.1 2.4 copy-start.40
  728.1 2.4 copy-start.41
  728.1 3.0 copy-start.19
  728.1 3.1 copy-start.21
  731.2 3.1 copy-start.24
  734.3 1.6 copy-start.25

commit v3 on v2

--- a/solution.py
+++ b/solution.py
@@ -280,98 +280,125 @@
     def peer(self, offset):
         return (lax.rem(self.group + offset, self.groups), self.spot)
 
-    def partners(self):
-        found = []
-        bit = 1
-        while bit < self.groups:
-            found.append((self.group + bit - 2 * bit * (self.group // bit % 2), self.spot))
-            bit *= 2
-        bit = 1
-        while bit < 2 * self.chips:
-            found.append((self.group, self.spot + bit - 2 * bit * (self.spot // bit % 2)))
-            bit *= 2
-        return found
-
-    def barrier(self, with_groups=False, with_partners=False):
+    def fellow(self, offset):
+        return (self.group, lax.rem(self.spot + offset, 2 * self.chips))
+
+    def barrier(self, with_groups=False, with_all_spots=False):
         semaphore = pltpu.get_barrier_semaphore()
 
         def greet(target):
             pl.semaphore_signal(semaphore, inc=1, device_id=target, device_id_type=MESH)
 
-        greet(self.at(self.chip, 1 - self.core))
-        pl.when(self.chip > 0)(lambda: greet(self.at(self.chip - 1, self.core)))
-        pl.when(self.chip < self.chips - 1)(lambda: greet(self.at(self.chip + 1, self.core)))
-        count = 1 + jnp.where(self.chip > 0, 1, 0) + jnp.where(self.chip < self.chips - 1, 1, 0)
+        if with_all_spots:
+            for offset in range(1, 2 * self.chips):
+                greet(self.fellow(offset))
+            count = 2 * self.chips - 1
+        else:
+            greet(self.at(self.chip, 1 - self.core))
+            pl.when(self.chip > 0)(lambda: greet(self.at(self.chip - 1, self.core)))
+            pl.when(self.chip < self.chips - 1)(lambda: greet(self.at(self.chip + 1, self.core)))
+            count = 1 + jnp.where(self.chip > 0, 1, 0) + jnp.where(self.chip < self.chips - 1, 1, 0)
         if with_groups:
             for offset in range(1, self.groups):
                 greet(self.peer(offset))
             count = count + self.groups - 1
-        if with_partners:
-            partners = self.partners()
-            for partner in partners:
-                greet(partner)
-            count = count + len(partners)
         pl.semaphore_wait(semaphore, count)
+
+
+def each(count, use):
+    def one(index, _):
+        use(index)
+        return 0
+
+    lax.fori_loop(0, count, one, 0)
+
+
+def block_of(ref, index, size):
+    return ref.at[pl.ds(pl.multiple_of(index * size, size), size)]
+
+
+def fetch_all(pairs, sems):
+    copies = [pltpu.make_async_copy(a, b, sems.at[n]) for n, (a, b) in enumerate(pairs)]
+    for copy in copies:
+        copy.start()
+    return copies
+
+
+HALVES = 2
 
 
 class Gather:
     SEMS = 5
 
-    def __init__(self, place, full, sems):
-        self.place, self.full = place, full
+    def __init__(self, place, full, sems, kept=None, keep_sem=None):
+        self.place, self.full, self.kept, self.keep_sem = place, full, kept, keep_sem
         self.line_in, self.core_in, self.right_out, self.left_out, self.core_out = sems
         self.rows = full.shape[0] // (2 * place.chips)
 
     @classmethod
     def scratch(cls, chips):
-        return [pltpu.SemaphoreType.DMA((chips,)) for _ in range(cls.SEMS)]
-
-    def block(self, chip, core):
-        base = pl.multiple_of((chip * 2 + core) * self.rows, self.rows)
-        return self.full.at[pl.ds(base, self.rows), :]
+        return [pltpu.SemaphoreType.DMA((chips * HALVES,)) for _ in range(cls.SEMS)]
 
     def own(self):
-        return self.block(self.place.chip, self.place.core)
-
-    def right(self, which):
-        place, part = self.place, self.block(which, self.place.core)
+        return block_of(self.full, self.place.spot, self.rows)
+
+    def block(self, chip, core, half):
+        return block_of(self.full, (chip * 2 + core) * HALVES + half, self.rows // HALVES)
+
+    def right(self, which, half):
+        place, part = self.place, self.block(which, self.place.core, half)
         target = place.at(jnp.minimum(place.chip + 1, place.chips - 1), place.core)
-        return remote(part, part, self.right_out.at[which], self.line_in.at[which], target)
-
-    def left(self, which):
-        place, part = self.place, self.block(which, self.place.core)
+        index = which * HALVES + half
+        return remote(part, part, self.right_out.at[index], self.line_in.at[index], target)
+
+    def left(self, which, half):
+        place, part = self.place, self.block(which, self.place.core, half)
         target = place.at(jnp.maximum(place.chip - 1, 0), place.core)
-        return remote(part, part, self.left_out.at[which], self.line_in.at[which], target)
-
-    def across(self, which, core):
-        place, part = self.place, self.block(which, core)
+        index = which * HALVES + half
+        return remote(part, part, self.left_out.at[index], self.line_in.at[index], target)
+
+    def across(self, which, core, half):
+        place, part = self.place, self.block(which, core, half)
         target = place.at(place.chip, 1 - place.core)
-        return remote(part, part, self.core_out.at[which], self.core_in.at[which], target)
+        index = which * HALVES + half
+        return remote(part, part, self.core_out.at[index], self.core_in.at[index], target)
 
     def begin(self):
         chip, chips = self.place.chip, self.place.chips
-        pl.when(chip < chips - 1)(lambda: self.right(chip).start())
-        pl.when(chip > 0)(lambda: self.left(chip).start())
-        self.across(chip, self.place.core).start()
+        for half in range(HALVES):
+            pl.when(chip < chips - 1)(lambda: self.right(chip, half).start())
+            pl.when(chip > 0)(lambda: self.left(chip, half).start())
+        for half in range(HALVES):
+            self.across(chip, self.place.core, half).start()
 
     def pass_on(self, step):
         chip, chips, core = self.place.chip, self.place.chips, self.place.core
         low, high = chip - 1 - step, chip + 1 + step
-
-        @pl.when(low >= 0)
-        def _():
-            self.right(low).wait_recv()
-            pl.when(chip < chips - 1)(lambda: self.right(low).start())
-            self.across(low, core).start()
-
-        @pl.when(high < chips)
-        def _():
-            self.left(high).wait_recv()
-            pl.when(chip > 0)(lambda: self.left(high).start())
-            self.across(high, core).start()
+        for half in range(HALVES):
+
+            @pl.when(low >= 0)
+            def _():
+                self.right(low, half).wait_recv()
+                pl.when(chip < chips - 1)(lambda: self.right(low, half).start())
+                self.across(low, core, half).start()
+
+            @pl.when(high < chips)
+            def _():
+                self.left(high, half).wait_recv()
+                pl.when(chip > 0)(lambda: self.left(high, half).start())
+                self.across(high, core, half).start()
+
+    def keep(self, which):
+        part = block_of(self.full, which, 2 * self.rows)
+        return pltpu.make_async_copy(
+            part, block_of(self.kept, which, 2 * self.rows), self.keep_sem.at[which]
+        )
 
     def wait_chip(self, which):
-        self.across(which, 1 - self.place.core).wait_recv()
+        for half in range(HALVES):
+            self.across(which, 1 - self.place.core, half).wait_recv()
+        if self.kept is not None:
+            self.keep(which).start()
 
     def each_new(self, step, use):
         low, high = self.place.chip - 1 - step, self.place.chip + 1 + step
@@ -389,13 +416,17 @@
     def drain(self):
         chip, chips, core = self.place.chip, self.place.chips, self.place.core
 
-        def one(which, _):
-            self.across(which, core).wait_send()
-            pl.when((which <= chip) & (chip < chips - 1))(lambda: self.right(which).wait_send())
-            pl.when((which >= chip) & (chip > 0))(lambda: self.left(which).wait_send())
-            return 0
-
-        lax.fori_loop(0, chips, one, 0)
+        def one(which):
+            for half in range(HALVES):
+                self.across(which, core, half).wait_send()
+                pl.when((which <= chip) & (chip < chips - 1))(
+                    lambda: self.right(which, half).wait_send()
+                )
+                pl.when((which >= chip) & (chip > 0))(lambda: self.left(which, half).wait_send())
+            if self.kept is not None:
+                self.keep(which).wait()
+
+        each(chips, one)
 
 
 class Scatter:
@@ -403,6 +434,7 @@
         self.place, self.work = place, work
         self.out, self.side, self.line = scratch[:3]
         self.core_out, self.core_in, self.line_out, self.line_in = scratch[3:]
+        self.part = self.out.shape[1] // HALVES
         chip, chips = place.chip, place.chips
         self.near = jnp.minimum(chip, chips - 1 - chip)
         self.alone = chips - 1 - 2 * self.near
@@ -417,8 +449,8 @@
             pltpu.VMEM((chips + 1, rows, width), LOW),
             pltpu.SemaphoreType.DMA((chips,)),
             pltpu.SemaphoreType.DMA((chips,)),
-            pltpu.SemaphoreType.DMA((chips,)),
-            pltpu.SemaphoreType.DMA((chips + 1,)),
+            pltpu.SemaphoreType.DMA((chips * HALVES,)),
+            pltpu.SemaphoreType.DMA(((chips + 1) * HALVES,)),
         ]
 
     SCRATCH = 7
@@ -442,32 +474,33 @@
             place.at(place.chip, 1 - place.core),
         )
 
-    def right(self, which):
+    def hop(self, which, slot, half, target):
+        rows = slice(half * self.part, (half + 1) * self.part)
+        return remote(
+            self.out.at[which, rows],
+            self.line.at[slot, rows],
+            self.line_out.at[which * HALVES + half],
+            self.line_in.at[slot * HALVES + half],
+            self.place.at(target, self.place.core),
+        )
+
+    def right(self, which, half):
         place = self.place
         slot = jnp.where(which == place.chip + 1, place.chips, which)
-        return remote(
-            self.out.at[which],
-            self.line.at[slot],
-            self.line_out.at[which],
-            self.line_in.at[slot],
-            place.at(jnp.minimum(place.chip + 1, place.chips - 1), place.core),
-        )
-
-    def left(self, which):
+        return self.hop(which, slot, half, jnp.minimum(place.chip + 1, place.chips - 1))
+
+    def left(self, which, half):
+        return self.hop(which, which, half, jnp.maximum(self.place.chip - 1, 0))
+
+    def arrived(self, slot, half):
         place = self.place
-        return remote(
-            self.out.at[which],
-            self.line.at[which],
-            self.line_out.at[which],
-            self.line_in.at[which],
-            place.at(jnp.maximum(place.chip - 1, 0), place.core),
-        )
-
-    def arrived(self, slot):
-        place = self.place
-        part = self.line.at[slot]
+        rows = slice(half * self.part, (half + 1) * self.part)
+        part = self.line.at[slot, rows]
         other = place.at(place.chip, 1 - place.core)
-        remote(part, part, self.line_out.at[0], self.line_in.at[slot], other).wait_recv()
+        remote(
+            part, part, self.line_out.at[0], self.line_in.at[slot * HALVES + half], other
+        ).wait_recv()
+        return self.line[slot, rows].astype(jnp.float32)
 
     def produce(self, turn):
         which = self.order(turn)
@@ -484,14 +517,17 @@
 
         @pl.when(upstream)
         def _():
-            self.arrived(which)
-            self.out[which] = (total + self.line[which].astype(jnp.float32)).astype(LOW)
+            for half in range(HALVES):
+                rows = slice(half * self.part, (half + 1) * self.part)
+                self.out[which, rows] = (total[rows] + self.arrived(which, half)).astype(LOW)
+                copy(which, half).start()
 
         @pl.when(jnp.logical_not(upstream))
         def _():
-            self.out[which] = total.astype(LOW)
-
-        copy(which).start()
+            for half in range(HALVES):
+                rows = slice(half * self.part, (half + 1) * self.part)
+                self.out[which, rows] = total[rows].astype(LOW)
+                copy(which, half).start()
 
     def first(self):
         pl.when(self.lag == 1)(lambda: self.produce(0))
@@ -514,36 +550,35 @@
     def own(self, total):
         chip, chips = self.place.chip, self.place.chips
         total[...] = self.chip_sum(chip)
-
-        @pl.when(chip > 0)
-        def _():
-            self.arrived(chips)
-            total[...] += self.line[chips].astype(jnp.float32)
-
-        @pl.when(chip < chips - 1)
-        def _():
-            self.arrived(chip)
-            total[...] += self.line[chip].astype(jnp.float32)
+        for half in range(HALVES):
+            rows = slice(half * self.part, (half + 1) * self.part)
+
+            @pl.when(chip > 0)
+            def _():
+                total[rows] += self.arrived(chips, half)
+
+            @pl.when(chip < chips - 1)
+            def _():
+                total[rows] += self.arrived(chip, half)
 
     def drain(self):
         chip = self.place.chip
 
-        def one(which, _):
-            pl.when(which > chip)(lambda: self.right(which).wait_send())
-            pl.when(which < chip)(lambda: self.left(which).wait_send())
-            return 0
-
-        lax.fori_loop(0, self.place.chips, one, 0)
+        def one(which):
+            for half in range(HALVES):
+                pl.when(which > chip)(lambda: self.right(which, half).wait_send())
+                pl.when(which < chip)(lambda: self.left(which, half).wait_send())
+
+        each(self.place.chips, one)
 
 
 class Spread:
-    def __init__(self, place, shard, whole, axis, sems):
-        self.place, self.whole, self.sems = place, whole, sems
+    def __init__(self, place, shard, staged, whole, axis, sems):
+        self.place, self.staged, self.whole, self.sems = place, staged, whole, sems
         size = shard.shape[axis]
         here = pl.ds(pl.multiple_of(place.group * size, size), size)
-        index = tuple(here if a == axis else slice(None) for a in range(len(shard.shape)))
-        self.mine = whole.at[index]
-        self.mine[...] = shard[...].astype(LOW)
+        self.mine = whole.at[tuple(here if a == axis else slice(None) for a in range(len(shard.shape)))]
+        staged[...] = shard[...].astype(LOW)
 
     @staticmethod
     def scratch(groups):
@@ -551,20 +586,25 @@
 
     def copy(self, offset):
         return remote(
-            self.mine,
+            self.staged,
             self.mine,
             self.sems[0].at[offset],
             self.sems[1].at[offset],
             self.place.peer(offset),
         )
 
+    def stay(self):
+        return pltpu.make_async_copy(self.staged, self.mine, self.sems[0].at[0])
+
     def start(self):
         for offset in range(1, self.place.groups):
             self.copy(offset).start()
+        self.stay().start()
 
     def wait(self):
         for offset in range(1, self.place.groups):
             self.copy(offset).wait()
+        self.stay().wait()
 
 
 class Exchange:
@@ -593,15 +633,41 @@
         self.stay().wait()
 
 
-def pieces(number, slots, groups, fill):
-    low = 1 + number * (groups - 1) // slots
-    high = 1 + (number + 1) * (groups - 1) // slots
-
-    def one(offset, _):
-        fill(offset)
-        return 0
-
-    lax.fori_loop(low, high, one, 0)
+class SmallSum:
+    def __init__(self, slots, me, count, target, sems):
+        self.slots, self.me, self.count, self.target = slots, me, count, target
+        self.send, self.receive = sems
+
+    def copy(self, offset):
+        part = self.slots.at[self.me]
+        return remote(
+            part, part, self.send.at[offset], self.receive.at[self.me], self.target(offset)
+        )
+
+    def begin(self, rows):
+        self.slots[self.me] = rows
+        for offset in range(1, self.count):
+            self.copy(offset).start()
+
+    def result(self):
+        for offset in range(1, self.count):
+            source = lax.rem(self.me + offset, self.count)
+            part = self.slots.at[source]
+            remote(
+                part, part, self.send.at[offset], self.receive.at[source], self.target(offset)
+            ).wait_recv()
+        total = self.slots[0]
+        for index in range(1, self.count):
+            total = total + self.slots[index]
+        for offset in range(1, self.count):
+            self.copy(offset).wait_send()
+        return total
+
+
+def pieces(number, groups, fill):
+    @pl.when(number == 0)
+    def _():
+        each(groups - 1, lambda index: fill(index + 1))
 
 
 def line_call(kernel, name, number, operands, out_shape, scratch, flops, in_hbm=(), from_hbm=()):
@@ -640,31 +706,32 @@
 def gather_project(groups, chips, tokens, gain, shift, shards, bias, tables):
     rows, width = tokens.shape
     length = rows * 2 * chips
-    qkv_shard, out_shard, gate_shard = shards
-    out_width = qkv_shard.shape[2]
-    hidden = gate_shard.shape[1]
+    qkv_shard, out_shard = shards
+    part, out_width = qkv_shard.shape[1:]
     tile = tables[0].shape[1]
 
     def kernel(
-        x_ref, gain_ref, shift_ref, qkv_ref, out_ref, gate_ref, bias_ref,
-        cos_ref, sin_low_ref, sin_high_ref,
-        full, weights, out_whole, gate_whole, q_ref, k_ref, v_ref, *sems
+        x_ref, gain_ref, shift_ref, qkv_ref, out_ref, bias_ref, cos_hbm, sin_low_hbm, sin_high_hbm,
+        kept, weights_kept, out_whole, q_ref, k_ref, v_ref,
+        full, weights, qkv_staged, out_staged, cos_ref, sin_low_ref, sin_high_ref,
+        load, keep_sem, *sems
     ):
         place = Place(groups, chips)
-        line, one, two, three = split_refs(sems, Gather.SEMS, 2, 2, 2)
-        gather = Gather(place, full, line)
+        fetches = fetch_all(
+            [(cos_hbm, cos_ref), (sin_low_hbm, sin_low_ref), (sin_high_hbm, sin_high_ref)], load
+        )
+        line, one, two = split_refs(sems, Gather.SEMS, 2, 2)
+        gather = Gather(place, full, line, kept, keep_sem)
         normed, _, _ = layer_norm_parts(
             x_ref[...].astype(jnp.float32), gain_ref[...], shift_ref[...]
         )
         gather.own()[...] = normed.astype(LOW)
-        spread_qkv = Spread(place, qkv_ref, weights, 1, one)
+        spread_qkv = Spread(place, qkv_ref, qkv_staged, weights, 1, one)
         place.barrier(True)
         gather.begin()
         spread_qkv.start()
-        spread_out = Spread(place, out_ref, out_whole, 1, two)
+        spread_out = Spread(place, out_ref, out_staged, out_whole, 1, two)
         spread_out.start()
-        spread_gate = Spread(place, gate_ref, gate_whole, 0, three)
-        spread_gate.start()
 
         def work(chip):
             base = pl.multiple_of(chip * 2 * rows, 2 * rows)
@@ -687,19 +754,22 @@
                 ref[here, :] = result.astype(LOW)
 
         gather.pass_on(0)
+        for copy in fetches:
+            copy.wait()
         spread_qkv.wait()
+        weights_keep = pltpu.make_async_copy(weights, weights_kept, load.at[3])
+        weights_keep.start()
         gather.wait_chip(place.chip)
         work(place.chip)
 
-        def step(number, _):
+        def step(number):
             pl.when(number > 0)(lambda: gather.pass_on(number))
             gather.each_new(number, work)
-            return 0
-
-        lax.fori_loop(0, chips - 1, step, 0)
+
+        each(chips - 1, step)
+        weights_keep.wait()
+        spread_out.wait()
         gather.drain()
-        spread_out.wait()
-        spread_gate.wait()
 
     head_shape = shape((length, out_width))
     return line_call(
@@ -711,41 +781,63 @@
             shape((length, width)),
             shape((3, width, out_width)),
             shape((out_width, width)),
-            shape((width, hidden)),
             head_shape,
             head_shape,
             head_shape,
         ],
-        Gather.scratch(chips) + Spread.scratch(groups) * 3,
+        [
+            pltpu.VMEM((length, width), LOW),
+            pltpu.VMEM((3, width, out_width), LOW),
+            pltpu.VMEM(qkv_shard.shape, LOW),
+            pltpu.VMEM(out_shard.shape, LOW),
+            *(pltpu.VMEM((length, tile), jnp.float32) for _ in range(3)),
+            pltpu.SemaphoreType.DMA((4,)),
+            pltpu.SemaphoreType.DMA((chips,)),
+        ]
+        + Gather.scratch(chips)
+        + Spread.scratch(groups) * 2,
         COST_FLOPS,
+        in_hbm=(0, 1, 2),
+        from_hbm=(6, 7, 8),
     )
 
 
 def scatter_heads(groups, chips, qkv, start, weight, tokens, grads, shards):
     rows, width = tokens.shape
-    queries = qkv[0]
-    length, head_width = queries.shape
+    length, head_width = qkv[0].shape
     heads = head_width // HD
-    up_shard, down_shard = shards
+    (pair_shard,) = shards
 
     def kernel(
-        q_ref, k_ref, v_ref, start_ref, w_ref, x_ref, og_ref, up_ref, down_ref,
-        mid_ref, ctx_ref, lse_ref, full, up_whole, down_whole,
-        v_turned, acc, stats, *rest
+        q_hbm, k_hbm, v_hbm, w_hbm, x_hbm, og_hbm, start_ref, pair_ref,
+        mid_ref, ctx_ref, lse_ref, kept, pair_whole,
+        full, q_ref, k_ref, v_ref, w_ref, x_ref, pair_staged,
+        load, keep_sem, v_turned, acc, stats, *rest
     ):
         place = Place(groups, chips)
+        scratch, line, one = split_refs(rest, Scatter.SCRATCH, Gather.SEMS, 2)
+        gather = Gather(place, full, line, kept, keep_sem)
+        fetches = fetch_all(
+            [
+                (og_hbm, gather.own()),
+                (k_hbm, k_ref),
+                (v_hbm, v_ref),
+                (q_hbm, q_ref),
+                (w_hbm, w_ref),
+                (x_hbm, x_ref),
+            ],
+            load,
+        )
+        place.barrier(True)
+        fetches[0].wait()
+        gather.begin()
+        spread_pair = Spread(place, pair_ref, pair_staged, pair_whole, 2, one)
+        spread_pair.start()
+        for copy in fetches[1:5]:
+            copy.wait()
         for part in range(length // BLK):
             here = slice(part * BLK, (part + 1) * BLK)
             v_turned[:, here] = v_ref[here, :].T
-        scratch, line, one, two = split_refs(rest, Scatter.SCRATCH, Gather.SEMS, 2, 2)
-        gather = Gather(place, full, line)
-        gather.own()[...] = og_ref[...]
-        spread_up = Spread(place, up_ref, up_whole, 0, one)
-        spread_down = Spread(place, down_ref, down_whole, 1, two)
-        place.barrier(True)
-        gather.begin()
-        spread_up.start()
-        spread_down.start()
         masks = head_masks(head_width, LOW)
 
         def work(chip, core):
@@ -777,124 +869,206 @@
         scatter = Scatter(place, work, scratch)
         scatter.first()
 
-        def step(number, _):
+        def seen(chip):
+            pass
+
+        def step(number):
             scatter.slot(number)
             gather.pass_on(number)
-            return 0
-
-        lax.fori_loop(0, chips - 1, step, 0)
+            pl.when(number > 0)(lambda: gather.each_new(number - 1, seen))
+
+        each(chips - 1, step)
         scatter.last()
+        fetches[5].wait()
+        gather.wait_chip(place.chip)
+        gather.each_new(chips - 2, seen)
         scatter.own(mid_ref)
         mid_ref[...] += x_ref[...].astype(jnp.float32)
-
-        def here_too(which, _):
-            gather.wait_chip(which)
-            return 0
-
-        lax.fori_loop(0, chips, here_too, 0)
         gather.drain()
         scatter.drain()
-        spread_up.wait()
-        spread_down.wait()
+        spread_pair.wait()
 
     return line_call(
         kernel,
         "scatter_heads",
         2,
-        (*qkv, start, weight, tokens, grads, *shards),
+        (*qkv, weight, tokens, grads, start, *shards),
         [
             shape((rows, width), jnp.float32),
             shape((length, head_width)),
             shape((8, length), jnp.float32),
             shape((length, width)),
-            shape((width, up_shard.shape[1])),
-            shape((down_shard.shape[0], width)),
+            shape((2, pair_shard.shape[1], width)),
         ],
         [
+            pltpu.VMEM((length, width), LOW),
+            *(pltpu.VMEM((length, head_width), LOW) for _ in range(3)),
+            pltpu.VMEM((head_width, width), LOW),
+            pltpu.VMEM((rows, width), LOW),
+            pltpu.VMEM(pair_shard.shape, LOW),
+            pltpu.SemaphoreType.DMA((6,)),
+            pltpu.SemaphoreType.DMA((chips,)),
             pltpu.VMEM((head_width, length), LOW),
             pltpu.VMEM((head_width, rows), jnp.float32),
             pltpu.VMEM((16, rows), jnp.float32),
         ]
         + Scatter.scratch(chips, rows, width)
         + Gather.scratch(chips)
-        + Spread.scratch(groups) * 2,
+        + Spread.scratch(groups),
         COST_FLOPS,
-    )
-
-
-def gather_hidden(groups, chips, middle, gain, shift, gate_weight, up_weight):
+        in_hbm=(3, 4),
+        from_hbm=(0, 1, 2, 3, 4, 5),
+    )
+
+
+def gather_hidden(groups, chips, middle, gain, shift, pair_weight, down_shard):
     rows, width = middle.shape
     length = rows * 2 * chips
-    hidden = gate_weight.shape[1]
-
-    def kernel(mid_ref, gain_ref, shift_ref, wg_ref, wu_ref, full, hid_ref, one_ref, two_ref, *line):
+    hidden = pair_weight.shape[1]
+
+    def kernel(
+        mid_ref, gain_ref, shift_ref, pair_hbm, down_ref,
+        kept, hid_kept, one_kept, two_kept, down_whole,
+        full, hid_ref, one_ref, two_ref, pair_ref, down_staged, load, keep_sem, *rest
+    ):
         place = Place(groups, chips)
-        gather = Gather(place, full, line)
+        fetches = fetch_all([(pair_hbm, pair_ref)], load)
+        line, keeps, sems = split_refs(rest, Gather.SEMS, 3, 2)
+        gather = Gather(place, full, line, kept, keep_sem)
         normed, _, _ = layer_norm_parts(mid_ref[...], gain_ref[...], shift_ref[...])
         gather.own()[...] = normed.astype(LOW)
-        place.barrier()
+        place.barrier(True)
         gather.begin()
+        spread_down = Spread(place, down_ref, down_staged, down_whole, 1, sems)
+        spread_down.start()
+        results = list(zip((hid_ref, one_ref, two_ref), (hid_kept, one_kept, two_kept), keeps))
+
+        def store(chip):
+            return [
+                pltpu.make_async_copy(
+                    block_of(a, chip, 2 * rows), block_of(b, chip, 2 * rows), sem.at[chip]
+                )
+                for a, b, sem in results
+            ]
 
         def work(chip):
             for half in range(2):
                 here = pl.ds(pl.multiple_of((chip * 2 + half) * rows, rows), rows)
                 values = full[here, :]
-                gate = dot(values, wg_ref[...])
-                up = dot(values, wu_ref[...])
+                gate = dot(values, pair_ref[0], NT)
+                up = dot(values, pair_ref[1], NT)
                 sigmoid = 1.0 / (1.0 + jnp.exp(-gate))
                 activated = gate * sigmoid
                 hid_ref[here, :] = (activated * up).astype(LOW)
                 slope = sigmoid * (1.0 + gate * (1.0 - sigmoid))
                 one_ref[here, :] = (up * slope).astype(LOW)
                 two_ref[here, :] = activated.astype(LOW)
-
+            for copy in store(chip):
+                copy.start()
+
+        for copy in fetches:
+            copy.wait()
         gather.wait_chip(place.chip)
         work(place.chip)
 
-        def step(number, _):
+        def step(number):
             gather.pass_on(number)
             gather.each_new(number, work)
-            return 0
-
-        lax.fori_loop(0, chips - 1, step, 0)
+
+        each(chips - 1, step)
         gather.drain()
+
+        def stored(chip):
+            for copy in store(chip):
+                copy.wait()
+
+        each(chips, stored)
+        spread_down.wait()
 
     hidden_shape = shape((length, hidden))
     return line_call(
         kernel,
         "gather_hidden",
         3,
-        (middle, gain, shift, gate_weight, up_weight),
-        [shape((length, width)), hidden_shape, hidden_shape, hidden_shape],
-        Gather.scratch(chips),
+        (middle, gain, shift, pair_weight, down_shard),
+        [
+            shape((length, width)),
+            hidden_shape,
+            hidden_shape,
+            hidden_shape,
+            shape((down_shard.shape[0], width)),
+        ],
+        [
+            pltpu.VMEM((length, width), LOW),
+            *(pltpu.VMEM((length, hidden), LOW) for _ in range(3)),
+            pltpu.VMEM(pair_weight.shape, LOW),
+            pltpu.VMEM(down_shard.shape, LOW),
+            pltpu.SemaphoreType.DMA((1,)),
+            pltpu.SemaphoreType.DMA((chips,)),
+        ]
+        + Gather.scratch(chips)
+        + [pltpu.SemaphoreType.DMA((chips,)) for _ in range(3)]
+        + Spread.scratch(groups),
         COST_FLOPS,
-    )
-
-
-def scatter_hidden(groups, chips, grads, hidden_low, factors, down, gate_weight, up_weight):
+        in_hbm=(0, 1, 2, 3, 4),
+        from_hbm=(3,),
+    )
+
+
+def scatter_hidden(groups, chips, grads, hidden_low, factors, down, pair_weight):
     length, width = grads.shape
     rows = length // (2 * chips)
     hidden = down.shape[0]
     part = width // groups
 
     def kernel(
-        og_ref, hid_ref, one_ref, two_ref, down_ref, wg_ref, wu_ref,
-        gg_ref, ug_ref, sum_ref, landed, staged, *rest
+        og_hbm, hid_hbm, one_hbm, two_hbm, down_hbm, pair_hbm,
+        gg_kept, ug_kept, sum_ref, landed,
+        og_ref, hid_ref, one_ref, two_ref, down_ref, pair_ref, gg_ref, ug_ref, staged,
+        load, load_og, load_one, load_two, keep_gg, keep_ug, *rest
     ):
         place = Place(groups, chips)
         scratch, sems = split_refs(rest, Scatter.SCRATCH, 2)
-        place.barrier(True)
+        chunked = ((og_hbm, og_ref, load_og), (one_hbm, one_ref, load_one), (two_hbm, two_ref, load_two))
+
+        def bring(chip):
+            return [
+                pltpu.make_async_copy(
+                    block_of(a, chip, 2 * rows), block_of(b, chip, 2 * rows), sem.at[chip]
+                )
+                for a, b, sem in chunked
+            ]
+
+        def store(block):
+            return [
+                pltpu.make_async_copy(block_of(a, block, rows), block_of(b, block, rows), sem.at[block])
+                for a, b, sem in ((gg_ref, gg_kept, keep_gg), (ug_ref, ug_kept, keep_ug))
+            ]
 
         def work(chip, core):
-            here = pl.ds(pl.multiple_of((chip * 2 + core) * rows, rows), rows)
+            block = chip * 2 + core
+            here = pl.ds(pl.multiple_of(block * rows, rows), rows)
             hidden_grad = dot(og_ref[here, :], down_ref[...], NT)
             gate_grad = (hidden_grad * one_ref[here, :].astype(jnp.float32)).astype(LOW)
             up_grad = (hidden_grad * two_ref[here, :].astype(jnp.float32)).astype(LOW)
             gg_ref[here, :] = gate_grad
             ug_ref[here, :] = up_grad
-            return dot(gate_grad, wg_ref[...], NT) + dot(up_grad, wu_ref[...], NT)
+            for copy in store(block):
+                copy.start()
+            return dot(gate_grad, pair_ref[0]) + dot(up_grad, pair_ref[1])
 
         exchange = Exchange(place, staged, landed, sems)
+        scatter = Scatter(place, work, scratch)
+        fetches = fetch_all([(down_hbm, down_ref), (pair_hbm, pair_ref)], load)
+
+        def begin(turn):
+            for copy in bring(scatter.order(turn)):
+                copy.start()
+
+        each(chips, begin)
+        late = pltpu.make_async_copy(hid_hbm, hid_ref, load.at[2])
+        late.start()
+        place.barrier(True)
 
         def fill(offset):
             block = lax.rem(place.group + offset, groups)
@@ -905,15 +1079,31 @@
             fill(offset)
             exchange.copy(offset).start()
 
-        scatter = Scatter(place, work, scratch)
+        def brought(turn, _=0):
+            for copy in bring(scatter.order(turn)):
+                copy.wait()
+            return 0
+
+        def brought_once(turn):
+            brought(turn)
+
+        for copy in fetches:
+            copy.wait()
+        brought_once(0)
         scatter.first()
-
-        def step(number, _):
+        pl.when(scatter.lag == 1)(functools.partial(brought_once, 1))
+
+        def step(number):
             scatter.slot(number)
-            pieces(number, chips - 1, groups, fill_send)
-            return 0
-
-        lax.fori_loop(0, chips - 1, step, 0)
+
+            @pl.when(number == 0)
+            def _():
+                lax.fori_loop(1 + scatter.lag, chips, brought, 0)
+                late.wait()
+
+            pieces(number, groups, fill_send)
+
+        each(chips - 1, step)
         scatter.last()
         fill(0)
         exchange.stay().start()
@@ -921,22 +1111,40 @@
         scatter.drain()
         exchange.wait()
 
+        def stored(block):
+            for copy in store(block):
+                copy.wait()
+
+        each(2 * chips, stored)
+
+    hidden_shape = shape((length, hidden))
     return line_call(
         kernel,
         "scatter_hidden",
         4,
-        (grads, hidden_low, *factors, down, gate_weight, up_weight),
+        (grads, hidden_low, *factors, down, pair_weight),
         [
-            shape((length, hidden)),
-            shape((length, hidden)),
+            hidden_shape,
+            hidden_shape,
             shape((rows, width), jnp.float32),
             shape((groups, hidden, part)),
         ],
-        [pltpu.VMEM((groups, hidden, part), LOW)]
+        [
+            pltpu.VMEM((length, width), LOW),
+            *(pltpu.VMEM((length, hidden), LOW) for _ in range(3)),
+            pltpu.VMEM(down.shape, LOW),
+            pltpu.VMEM(pair_weight.shape, LOW),
+            *(pltpu.VMEM((length, hidden), LOW) for _ in range(2)),
+            pltpu.VMEM((groups, hidden, part), LOW),
+            pltpu.SemaphoreType.DMA((3,)),
+            *(pltpu.SemaphoreType.DMA((chips,)) for _ in range(3)),
+            *(pltpu.SemaphoreType.DMA((2 * chips,)) for _ in range(2)),
+        ]
         + Scatter.scratch(chips, rows, width)
         + Spread.scratch(groups),
         COST_FLOPS,
-        in_hbm=(3,),
+        in_hbm=(0, 1, 3),
+        from_hbm=(0, 1, 2, 3, 4, 5),
     )
 
 
@@ -950,12 +1158,12 @@
     part = width // groups
 
     def kernel(
-        mid_ref, ng_ref, og_ref, gain_ref, shift_ref, w_ref, hid_ref, down_ref, a_ref, gg_ref, ug_ref,
-        full, cg_ref, mg_ref, sums_ref, out_ref, landed_gate, landed_up,
-        total, staged_gate, staged_up, columns_in, load, *rest
+        mid_ref, ng_hbm, og_ref, gain_ref, shift_ref, w_hbm, hid_hbm, down_hbm, a_ref, gg_hbm, ug_hbm,
+        kept, cg_ref, mg_ref, sums_ref, out_ref, landed,
+        full, total, w_ref, hid_ref, down_ref, gg_ref, ug_ref, staged, columns_in, load, keep_sem, *rest
     ):
         place = Place(groups, chips)
-        scratch, line, one, two = split_refs(rest, Scatter.SCRATCH, Gather.SEMS, 2, 2)
+        scratch, line, sems = split_refs(rest, Scatter.SCRATCH, Gather.SEMS, 2)
 
         def fetch(offset):
             block = lax.rem(place.group + offset, groups)
@@ -963,10 +1171,24 @@
             slot = lax.rem(offset, 2)
             return pltpu.make_async_copy(a_ref.at[:, columns], columns_in.at[slot], load.at[slot])
 
-        arrive = pltpu.make_async_copy(ng_ref, total, load.at[3])
+        arrive = pltpu.make_async_copy(ng_hbm, total, load.at[3])
         arrive.start()
+        late = [
+            pltpu.make_async_copy(a, b, load.at[4 + n])
+            for n, (a, b) in enumerate(
+                (
+                    (down_hbm, down_ref),
+                    (hid_hbm, hid_ref),
+                    (w_hbm, w_ref),
+                    (gg_hbm, gg_ref),
+                    (ug_hbm, ug_ref),
+                )
+            )
+        ]
+        for copy in late:
+            copy.start()
         fetch(1).start()
-        gather = Gather(place, full, line)
+        gather = Gather(place, full, line, kept, keep_sem)
         _, plain, inverse = layer_norm_parts(mid_ref[...], gain_ref[...], shift_ref[...])
         arrive.wait()
         back, gain_grad, shift_grad = layer_norm_back(total[...], plain, inverse, gain_ref[...])
@@ -974,11 +1196,11 @@
         total[...] = mid_grad
         keep = pltpu.make_async_copy(total, mg_ref, load.at[2])
         keep.start()
-        sums_ref[0:1, :] = gain_grad[None, :]
-        sums_ref[1:2, :] = shift_grad[None, :]
         gather.own()[...] = mid_grad.astype(LOW)
         place.barrier(True)
         gather.begin()
+        sums_ref[0:1, :] = gain_grad[None, :]
+        sums_ref[1:2, :] = shift_grad[None, :]
 
         def back_work(chip):
             here = pl.ds(pl.multiple_of(chip * 2 * rows, 2 * rows), 2 * rows)
@@ -988,27 +1210,29 @@
             here = pl.ds(pl.multiple_of((chip * 2 + core) * rows, rows), rows)
             return dot(hid_ref[here, :], down_ref[...])
 
-        exchange_gate = Exchange(place, staged_gate, landed_gate, one)
-        exchange_up = Exchange(place, staged_up, landed_up, two)
+        exchange = Exchange(place, staged, landed, sems)
 
         def fill(offset):
             fetch(offset).wait()
             pl.when(offset > 0)(lambda: fetch(lax.rem(offset + 1, groups)).start())
             values = columns_in[lax.rem(offset, 2)]
-            staged_gate[offset] = dot(values, gg_ref[...], TN).astype(LOW)
-            staged_up[offset] = dot(values, ug_ref[...], TN).astype(LOW)
+            staged[offset, 0] = dot(gg_ref[...], values, TN).astype(LOW)
+            staged[offset, 1] = dot(ug_ref[...], values, TN).astype(LOW)
 
         def fill_send(offset):
             fill(offset)
-            exchange_gate.copy(offset).start()
-            exchange_up.copy(offset).start()
+            exchange.copy(offset).start()
 
         scatter = Scatter(place, out_work, scratch)
+        late[0].wait()
+        late[1].wait()
         scatter.first()
-
-        def step(number, _):
+        for copy in late[2:]:
+            copy.wait()
+
+        def step(number):
             scatter.slot(number)
-            pieces(number, chips - 1, groups, fill_send)
+            pieces(number, groups, fill_send)
             gather.pass_on(number)
 
             @pl.when(number == 0)
@@ -1017,20 +1241,17 @@
                 back_work(place.chip)
 
             gather.each_new(number, back_work)
-            return 0
-
-        lax.fori_loop(0, chips - 1, step, 0)
+
+        each(chips - 1, step)
         scatter.last()
         fill(jnp.int32(0))
-        exchange_gate.stay().start()
-        exchange_up.stay().start()
+        exchange.stay().start()
         keep.wait()
         scatter.own(total)
         out_ref[...] = (mid_ref[...] + total[...]).astype(LOW)
         gather.drain()
         scatter.drain()
-        exchange_gate.wait()
-        exchange_up.wait()
+        exchange.wait()
 
     return line_call(
         kernel,
@@ -1043,22 +1264,27 @@
             shape((rows, width), jnp.float32),
             shape((2, width), jnp.float32),
             shape((rows, width)),
-            shape((groups, part, hidden)),
-            shape((groups, part, hidden)),
+            shape((groups, 2, hidden, part)),
         ],
         [
+            pltpu.VMEM((length, width), LOW),
             pltpu.VMEM((rows, width), jnp.float32),
-            pltpu.VMEM((groups, part, hidden), LOW),
-            pltpu.VMEM((groups, part, hidden), LOW),
+            pltpu.VMEM(weight.shape, LOW),
+            pltpu.VMEM((length, hidden), LOW),
+            pltpu.VMEM(down.shape, LOW),
+            pltpu.VMEM((length, hidden), LOW),
+            pltpu.VMEM((length, hidden), LOW),
+            pltpu.VMEM((groups, 2, hidden, part), LOW),
             pltpu.VMEM((2, length, part), LOW),
-            pltpu.SemaphoreType.DMA((4,)),
+            pltpu.SemaphoreType.DMA((9,)),
+            pltpu.SemaphoreType.DMA((chips,)),
         ]
         + Scatter.scratch(chips, rows, width)
         + Gather.scratch(chips)
-        + Spread.scratch(groups) * 2,
+        + Spread.scratch(groups),
         COST_FLOPS,
-        in_hbm=(2, 5, 6),
-        from_hbm=(1, 8),
+        in_hbm=(0, 2, 5),
+        from_hbm=(1, 5, 6, 7, 8, 9, 10),
     )
 
 
@@ -1071,14 +1297,30 @@
     part = width // groups
 
     def kernel(
-        q_ref, k_ref, v_ref, w_ref, x_ref, gain_ref, shift_ref, mg_ref, sums_ref, bias_ref,
-        a_ref, ctx_ref, full_ref,
+        q_ref, k_ref, v_ref, w_ref, gain_ref, shift_ref, sums_ref, bias_ref,
+        x_hbm, mg_hbm, a_hbm, ctx_hbm, full_hbm,
         in_ref, small_ref, landed_qkv, landed_out,
-        total, staged_qkv, staged_out, small_in, small_out, small_recv, *rest
+        x_ref, mg_ref, a_ref, ctx_ref, full_ref, load,
+        total, staged_qkv, staged_out, early_spots, early_groups, late_spots, late_groups, *rest
     ):
         place = Place(groups, chips)
-        scratch, one, two = split_refs(rest, Scatter.SCRATCH, 2, 2)
+        scratch, one, two, sums_sems = split_refs(rest, Scatter.SCRATCH, 2, 2, 8)
+        fetches = fetch_all(
+            [
+                (a_hbm, a_ref),
+                (ctx_hbm, ctx_ref),
+                (full_hbm, full_ref),
+                (x_hbm, x_ref),
+                (mg_hbm, mg_ref),
+            ],
+            load,
+        )
         place.barrier(True, True)
+        spots, count = place.spot, 2 * chips
+        early_a = SmallSum(early_spots, spots, count, place.fellow, sums_sems[0:2])
+        early_b = SmallSum(early_groups, place.group, groups, place.peer, sums_sems[2:4])
+        late_a = SmallSum(late_spots, spots, count, place.fellow, sums_sems[4:6])
+        late_b = SmallSum(late_groups, place.group, groups, place.peer, sums_sems[6:8])
 
         def work(chip, core):
             here = pl.ds(pl.multiple_of((chip * 2 + core) * rows, rows), rows)
@@ -1105,50 +1347,54 @@
         scatter = Scatter(place, work, scratch)
         scatter.first()
 
-        def step(number, _):
+        def step(number):
             scatter.slot(number)
-            pieces(number, chips - 1, groups, fill_send)
-            return 0
-
-        lax.fori_loop(0, chips - 1, step, 0)
+
+            @pl.when(number == 0)
+            def _():
+                early_a.begin(sums_ref[...])
+                for copy in fetches:
+                    copy.wait()
+
+            pieces(number, groups, fill_send)
+
+            @pl.when(number == chips - 2)
+            def _():
+                early_groups[place.group] = jnp.zeros(early_groups.shape[1:], jnp.float32)
+                early_groups[place.group, 4:7, 0:in_width] = bias_ref[0:3, :]
+                early_groups[place.group, 0:2, :] = early_a.result()
+                early_b.begin(early_groups[place.group])
+
+        each(chips - 1, step)
         scatter.last()
         fill(0)
         exchange_qkv.stay().start()
         exchange_out.stay().start()
-        scatter.own(total)
         _, plain, inverse = layer_norm_parts(
             x_ref[...].astype(jnp.float32), gain_ref[...], shift_ref[...]
         )
+        scatter.own(total)
         back, gain_grad, shift_grad = layer_norm_back(total[...], plain, inverse, gain_ref[...])
+        late_a.begin(jnp.concatenate([gain_grad[None, :], shift_grad[None, :]], axis=0))
         in_ref[...] = (mg_ref[...] + back).astype(LOW)
-        small_ref[...] = jnp.zeros_like(small_ref)
-        small_ref[0:1, :] = gain_grad[None, :]
-        small_ref[1:2, :] = sums_ref[0:1, :]
-        small_ref[2:3, :] = shift_grad[None, :]
-        small_ref[3:4, :] = sums_ref[1:2, :]
-        small_ref[4:7, 0:in_width] = bias_ref[0:3, :]
-        for number, partner in enumerate(place.partners()):
-            swap = remote(
-                small_ref,
-                small_in.at[number],
-                small_out.at[number],
-                small_recv.at[number],
-                partner,
-            )
-            swap.start()
-            swap.wait()
-            kept = 8 if 2**number < groups else 4
-            small_ref[0:kept, :] += small_in[number, 0:kept, :]
         scatter.drain()
         exchange_qkv.wait()
         exchange_out.wait()
-
-    doublings = (groups.bit_length() - 1) + (2 * chips).bit_length() - 1
+        late_b.begin(late_a.result())
+        first = early_b.result()
+        last = late_b.result()
+        small_ref[...] = first
+        small_ref[1:2, :] = first[0:1, :]
+        small_ref[3:4, :] = first[1:2, :]
+        small_ref[0:1, :] = last[0:1, :]
+        small_ref[2:3, :] = last[1:2, :]
+
+    devices = 2 * chips
     return line_call(
         kernel,
         "scatter_triple",
         6,
-        (*triple, weights, tokens, gain, shift, mid_grad, sums, bias_sums, normed, context, grads),
+        (*triple, weights, gain, shift, sums, bias_sums, tokens, mid_grad, normed, context, grads),
         [
             shape((rows, width)),
             shape((8, width), jnp.float32),
@@ -1156,17 +1402,26 @@
             shape((groups, in_width, part)),
         ],
         [
+            pltpu.VMEM((rows, width), LOW),
+            pltpu.VMEM((rows, width), jnp.float32),
+            pltpu.VMEM((length, width), LOW),
+            pltpu.VMEM((length, in_width), LOW),
+            pltpu.VMEM((length, width), LOW),
+            pltpu.SemaphoreType.DMA((5,)),
             pltpu.VMEM((rows, width), jnp.float32),
             pltpu.VMEM((groups, 3, part, in_width), LOW),
             pltpu.VMEM((groups, in_width, part), LOW),
-            pltpu.VMEM((doublings, 8, width), jnp.float32),
-            pltpu.SemaphoreType.DMA((doublings,)),
-            pltpu.SemaphoreType.DMA((doublings,)),
+            pltpu.VMEM((devices, 2, width), jnp.float32),
+            pltpu.VMEM((groups, 8, width), jnp.float32),
+            pltpu.VMEM((devices, 2, width), jnp.float32),
+            pltpu.VMEM((groups, 2, width), jnp.float32),
         ]
         + Scatter.scratch(chips, rows, width)
-        + Spread.scratch(groups) * 2,
+        + Spread.scratch(groups) * 2
+        + [pltpu.SemaphoreType.DMA((n,)) for n in (devices, devices, groups, groups) * 2],
         COST_FLOPS,
         in_hbm=(2, 3),
+        from_hbm=(8, 9, 10, 11, 12),
     )
 
 
@@ -1215,26 +1470,27 @@
     start = start[None, :]
     tables = rotary_tables(place, min(head_width, 128))
 
-    normed_one_all, qkv_all, out_all, gate_all, *qkv = gather_project(
+    gate_up_turned = jnp.swapaxes(w_gate_up, 1, 2)
+    normed_one_all, qkv_all, out_all, *qkv = gather_project(
         groups,
         chips,
         inputs,
         gains[0],
         shifts[0],
-        (w_qkv, w_out, w_gate_up[0]),
+        (w_qkv, w_out),
         qkv_bias,
         tables,
     )
-    middle, context_flat, lse, mlp_grad, up_all, down_all = scatter_heads(
-        groups, chips, qkv, start, out_all, inputs, out_grad, (w_gate_up[1], w_down)
-    )
-    normed_two_all, hidden_low, *factors = gather_hidden(
-        groups, chips, middle, gains[1], shifts[1], gate_all, up_all
+    middle, context_flat, lse, mlp_grad, pair_all = scatter_heads(
+        groups, chips, qkv, start, out_all, inputs, out_grad, (gate_up_turned,)
+    )
+    normed_two_all, hidden_low, *factors, down_all = gather_hidden(
+        groups, chips, middle, gains[1], shifts[1], pair_all, w_down
     )
     gate_grad, up_grad, normed_two_grad, parts_down = scatter_hidden(
-        groups, chips, mlp_grad, hidden_low, factors, down_all, gate_all, up_all
-    )
-    attn_grad_all, context_grad, middle_grad, sums_two, outputs, parts_gate, parts_up = (
+        groups, chips, mlp_grad, hidden_low, factors, down_all, pair_all
+    )
+    attn_grad_all, context_grad, middle_grad, sums_two, outputs, parts_pair = (
         gather_context(
             groups,
             chips,
@@ -1276,7 +1532,7 @@
         return total
 
     grad_qkv, grad_out, grad_down = add_parts(parts_qkv), add_parts(parts_out), add_parts(parts_down)
-    grad_gate_up = jnp.stack([add_parts(parts_gate), add_parts(parts_up)])
+    grad_gate_up = jnp.swapaxes(add_parts(parts_pair), 1, 2)
     grad_bias = small[4:7, :head_width]
     grad_gain, grad_shift = small[0:2], small[2:4]
     correct_one = 1.0 - 0.9**STEP

time: 746 us -> 640 us (0.86)
  Pallas kernels: 664 us -> 584 us
  local copies, waits for them, and re-layouts: 43.1 us -> 24.3 us
    pallas_call x6, Pallas kernels: 628 us -> 553 us  [line_call(): pl.pallas_call(kernel, out_shape=out_shape, in_specs=ins, out_specs=outs,...]
    unnamed x93 -> x68, local copies, waits for them, and re-layouts: 35 us -> 18.1 us
where the time goes in v3:
time: 640 us; the launch traced here: 633 us
  Pallas kernels  584 us (91%)
  local copies, waits for them, and re-layouts  24.3 us (4%)
  other arithmetic  22.8 us (4%)
    pallas_call x6, Pallas kernels, line_call(): pl.pallas_call(kernel, out_shape=out_shape, in_specs=ins, out_specs=outs,...  553 us
    pallas_call x1, Pallas kernels, attention_backward(): pl.pallas_call(backward_kernel, grid_spec=pltpu.PrefetchScalarGridSpec(nu...  31.4 us
    sub x6, other arithmetic, adam_update(): return (master - rate * change, one_new, two_new)  20.3 us
    unnamed x68, local copies, waits for them, and re-layouts  18.1 us

profile of v3, /device:TPU:0, one launch (start us, length us, event | category | flops | bytes accessed | tf_op | source)
XLA Modules:
  0.0 632.6 jit_solution(838468135387233493)
XLA Ops:
  0.7 0.1 pad.8.clone
  0.8 0.1 pad.5.clone
  0.8 0.9 compare_select_fusion
  1.7 0.3 reduce-window.6
  2.0 0.2 slice_reduce_fusion
  2.2 0.2 reduce-window.9
  2.4 0.1 broadcast.107
  2.5 0.6 subtract_subtract_fusion.start_ref
  3.1 0.1 iota_subtract_fusion
  3.1 0.1 slice.88
  3.2 1.4 fusion.17
  4.7 0.3 multiply_sine_fusion
  5.0 0.2 maximum_maximum_fusion.2
  5.2 0.1 tile.31
  5.3 1.3 copy.56.sin_high_hbm.sin_high_ref
  6.6 0.1 tile.14
  6.7 1.3 copy.55.sin_low_hbm.sin_low_ref
  8.0 0.1 tile.12
  8.1 1.3 copy.54.cos_hbm.cos_ref
  9.4 80.7 %gather_project.1 = (bf16[2048,2048]{1,0:T(8,128)(2,1)}, bf16[3,2048,256]{2,1,0:T(8,128)(2,1)}, bf16[256,2048]{1,0:T(8,128)(2,1)}, bf16[2048,256]{1,0:T(8,128)(2...) custom-call(bf16[256,2048]{1,0:T(8,128)(2,1)} %x_hbm.3, f32[1,2048]{1,0:T(1,128)} %get-tuple-element.142.gain_ref, ...), custom_call_target="tpu_custom_call" | custom-call | flops 80000000000 | tf_op jit(solution)/shard_map/gather_project/pallas_call | solution.py:677
  90.2 100.9 %scatter_heads.1 = (f32[256,2048]{1,0:T(8,128)}, bf16[2048,256]{1,0:T(8,128)(2,1)}, f32[8,2048]{1,0:T(8,128)}, bf16[2048,2048]{1,0:T(8,128)(2,1)}, bf16[2,704,2048]{2,1,0:T(8,128)(2,1)}) custom-call(bf16[2048,256]{1,0:T(8,128)(2,1)} %get-tuple-element.64.q_hbm.q_ref, bf16[2048,256]{1,0:T(8,128)(2,1)} %get-tuple-element.65.k_hbm.k_ref, ...), custom_call_target="tpu_custom_call" | custom-call | flops 80000000000 | tf_op jit(solution)/shard_map/scatter_heads/pallas_call | solution.py:677
  191.1 82.7 %gather_hidden.1 = (bf16[2048,2048]{1,0:T(8,128)(2,1)}, bf16[2048,704]{1,0:T(8,128)(2,1)}, bf16[2048,704]{1,0:T(8,128)(2,1)}, bf16[2048,704]{1,0:T(8,128)(2,1)}, bf16[704,2048]{1,0:T(8,128)(2,1)}) custom-call(f32[256,2048]{1,0:T(8,128)} %get-tuple-element.68.mid_ref, f32[1,2048]{1,0:T(1,128)} %get-tuple-element.143.gain_ref, ...), custom_call_target="tpu_custom_call" | custom-call | flops 80000000000 | tf_op jit(solution)/shard_map/gather_hidden/pallas_call | solution.py:677
  273.8 88.9 %scatter_hidden.1 = (bf16[2048,704]{1,0:T(8,128)(2,1)}, bf16[2048,704]{1,0:T(8,128)(2,1)}, f32[256,2048]{1,0:T(8,128)}, bf16[4,704,512]{2,1,0:T(8,128)(2,1)}) custom-call(bf16[2048,2048]{1,0:T(8,128)(2,1)} %get-tuple-element.69.og_hbm, bf16[2048,704]{1,0:T(8,128)(2,1)} %get-tuple-element.71.hid_hbm, bf16[2048,704]{1,0:T(8,128)(2,1)} %get-tuple-element.72.one_hbm, ...), custom_call_target="tpu_custom_call" | custom-call | flops 80000000000 | tf_op jit(solution)/shard_map/scatter_hidden/pallas_call | solution.py:677
  362.8 0.0 copy-start
  362.8 0.0 copy-start.9
  362.8 102.2 %gather_context.1 = (bf16[2048,2048]{1,0:T(8,128)(2,1)}, bf16[2048,256]{1,0:T(8,128)(2,1)}, f32[256,2048]{1,0:T(8,128)}, f32[2,2048]{1,0:T(2,128)}, bf16[256,204...) custom-call(f32[256,2048]{1,0:T(8,128)} %get-tuple-element.68.mid_ref, f32[256,2048]{1,0:T(8,128)} %get-tuple-element.75.ng_hbm, ...), custom_call_target="tpu_custom_call" | custom-call | flops 80000000000 | tf_op jit(solution)/shard_map/gather_context/pallas_call | solution.py:677
  465.1 0.0 copy-start.1
  465.1 1.2 copy-done.1
  466.3 1.2 copy-done.2
  467.5 1.2 copy-done.3
  468.8 1.2 copy-done.4
  470.0 1.2 copy-done.5
  471.2 1.2 copy-done.6
  472.4 1.2 copy-done.7
  473.7 31.4 %attention_backward.1 = (bf16[2048,256]{1,0:T(8,128)(2,1)S(1)}, bf16[2048,256]{1,0:T(8,128)(2,1)S(1)}, bf16[2048,256]{1,0:T(8,128)(2,1)S(1)}, f32[8,256]{1,0:T(8,128)S(1)}) custom-call(s32[8]{0:T(128)S(1)} %and_select_fusion.low_ref, bf16[2048,256]{1,0:T(8,128)(2,1)S(1)} %copy-done.4, bf16[2048,256]{1,0:T(8,128)(2,1)S(1)} %copy-done.5, ...), custom_call_target="tpu_custom_call" | custom-call | tf_op jit(solution)/shard_map/attention_backward/pallas_call | solution.py:220
  505.1 0.0 copy-start.10
  505.1 1.0 copy-done.10
  506.1 1.0 copy-done.11
  507.0 1.0 copy-done.12
  508.0 0.6 copy-done.13
  508.6 0.0 copy-start.26
  508.6 0.0 copy-start.23
  508.6 97.1 %scatter_triple.1 = (bf16[256,2048]{1,0:T(8,128)(2,1)}, f32[8,2048]{1,0:T(8,128)}, bf16[4,3,512,256]{3,2,1,0:T(8,128)(2,1)}, bf16[4,256,512]{2,1,0:T(8,128)(2,1)}) custom-call(bf16[2048,256]{1,0:T(8,128)(2,1)} %copy-done.10, bf16[2048,256]{1,0:T(8,128)(2,1)} %copy-done.11, bf16[2048,256]{1,0:T(8,128)(2,1)} %copy-done.12, ...), custom_call_target="tpu_custom_call" | custom-call | flops 80000000000 | tf_op jit(solution)/shard_map/scatter_triple/pallas_call | solution.py:677
  605.7 1.4 multiply_subtract_fusion.6
  607.1 1.7 multiply_subtract_fusion.4
  608.8 0.0 copy-start.22
  608.8 3.2 multiply_subtract_fusion.3
  612.0 0.0 copy-start.19
  612.0 0.0 copy-start.20
  612.0 0.0 copy-start.21
  612.0 0.0 copy-start.17
  612.1 5.0 multiply_subtract_fusion.2
  617.1 0.0 slice-start.1
  617.1 0.0 copy-start.15
  617.1 0.0 copy-start.16
  617.2 3.7 multiply_subtract_fusion.1
  620.8 1.3 slice-done
  622.1 0.4 slice-done.1
  622.5 0.9 copy-done.15
  623.4 0.8 copy-done.16
  624.2 5.3 multiply_subtract_fusion
  629.6 1.0 copy.62
  630.5 0.6 copy-done.25
  631.2 1.0 copy.63
  (43 shorter events, 0.1 us)
Async XLA Ops:
  362.8 102.3 %copy-start = (f32[2048,128]{1,0:T(8,128)S(1)}, f32[2048,128]{1,0:T(8,128)}, u32[]{:S(2)}) copy-start(f32[2048,128]{1,0:T(8,128)} %copy.56.sin_high_hbm.sin_high_ref) | copy-start | bytes 3145732
  362.8 102.3 %copy-start.8 = (f32[8,2048]{1,0:T(8,128)S(1)}, f32[8,2048]{1,0:T(8,128)}, u32[]{:S(2)}) copy-start(f32[8,2048]{1,0:T(8,128)} %get-tuple-element.80.lse_ref) | copy-start | bytes 196612
  362.8 102.3 %copy-start.9 = (s32[1,2048]{1,0:T(1,128)S(1)}, s32[1,2048]{1,0:T(1,128)}, u32[]{:S(2)}) copy-start(s32[1,2048]{1,0:T(1,128)} %subtract_subtract_fusion.start_ref) | copy-start | bytes 24580
  465.1 1.2 copy-start.1
  466.3 1.2 copy-start.2
  467.5 1.2 copy-start.3
  468.8 1.2 copy-start.4
  470.0 1.2 copy-start.5
  471.2 1.2 copy-start.6
  472.4 1.2 copy-start.7
  505.1 1.0 copy-start.10
  506.1 1.0 copy-start.11
  507.0 1.0 copy-start.12
  508.0 0.6 copy-start.13
  508.6 98.5 %copy-start.27 = (f32[2,2048]{1,0:T(2,128)S(1)}, f32[2,2048]{1,0:T(2,128)}, u32[]{:S(2)}) copy-start(f32[2,2048]{1,0:T(2,128)} %param.33) | copy-start | bytes 49156
  508.6 98.5 %copy-start.28 = (f32[2,2048]{1,0:T(2,128)S(1)}, f32[2,2048]{1,0:T(2,128)}, u32[]{:S(2)}) copy-start(f32[2,2048]{1,0:T(2,128)} %param.32) | copy-start | bytes 49156
  508.6 98.5 %copy-start.29 = (f32[2,2048]{1,0:T(2,128)S(1)}, f32[2,2048]{1,0:T(2,128)}, u32[]{:S(2)}) copy-start(f32[2,2048]{1,0:T(2,128)} %param.40) | copy-start | bytes 49156
  508.6 98.5 %copy-start.30 = (f32[2,2048]{1,0:T(2,128)S(1)}, f32[2,2048]{1,0:T(2,128)}, u32[]{:S(2)}) copy-start(f32[2,2048]{1,0:T(2,128)} %param.47) | copy-start | bytes 49156
  508.6 100.2 %copy-start.26 = (f32[256,512]{1,0:T(8,128)S(1)}, f32[256,512]{1,0:T(8,128)}, u32[]{:S(2)}) copy-start(f32[256,512]{1,0:T(8,128)} %out_ref.1) | copy-start | bytes 1572868
  508.6 103.4 %copy-start.23 = (f32[704,512]{1,0:T(8,128)S(1)}, f32[704,512]{1,0:T(8,128)}, u32[]{:S(2)}) copy-start(f32[704,512]{1,0:T(8,128)} %param.37) | copy-start | bytes 4325380
  608.8 3.2 copy-start.18
  608.8 3.2 copy-start.22
  612.0 5.1 copy-start.14
  612.0 5.1 copy-start.19
  612.0 5.1 copy-start.20
  612.0 5.1 copy-start.21
  612.0 8.8 %copy-start.17 = (f32[2,512,704]{1,2,0:T(8,128)S(1)}, f32[2,512,704]{1,2,0:T(8,128)}, u32[]{:S(2)}) copy-start(f32[2,512,704]{1,2,0:T(8,128)} %param.43) | copy-start | bytes 8650756
  617.1 5.0 slice-start
  617.1 5.4 slice-start.1
  617.1 6.2 copy-start.15
  617.1 7.1 %copy-start.16 = (f32[2,512,704]{1,2,0:T(8,128)S(1)}, f32[2,512,704]{1,2,0:T(8,128)}, u32[]{:S(2)}) copy-start(f32[2,512,704]{1,2,0:T(8,128)} %param.36) | copy-start | bytes 8650756
  624.2 5.4 copy-start.24
  629.5 1.6 copy-start.25

commit v4 on v3

--- a/solution.py
+++ b/solution.py
@@ -363,18 +363,18 @@
         index = which * HALVES + half
         return remote(part, part, self.core_out.at[index], self.core_in.at[index], target)
 
-    def begin(self):
+    def begin(self, halves=range(HALVES)):
         chip, chips = self.place.chip, self.place.chips
-        for half in range(HALVES):
+        for half in halves:
             pl.when(chip < chips - 1)(lambda: self.right(chip, half).start())
             pl.when(chip > 0)(lambda: self.left(chip, half).start())
-        for half in range(HALVES):
+        for half in halves:
             self.across(chip, self.place.core, half).start()
 
-    def pass_on(self, step):
+    def pass_on(self, step, halves=range(HALVES)):
         chip, chips, core = self.place.chip, self.place.chips, self.place.core
         low, high = chip - 1 - step, chip + 1 + step
-        for half in range(HALVES):
+        for half in halves:
 
             @pl.when(low >= 0)
             def _():
@@ -394,23 +394,23 @@
             part, block_of(self.kept, which, 2 * self.rows), self.keep_sem.at[which]
         )
 
-    def wait_chip(self, which):
-        for half in range(HALVES):
+    def wait_chip(self, which, halves=range(HALVES)):
+        for half in halves:
             self.across(which, 1 - self.place.core, half).wait_recv()
-        if self.kept is not None:
+        if self.kept is not None and HALVES - 1 in halves:
             self.keep(which).start()
 
-    def each_new(self, step, use):
+    def each_new(self, step, use, halves=range(HALVES)):
         low, high = self.place.chip - 1 - step, self.place.chip + 1 + step
 
         @pl.when(low >= 0)
         def _():
-            self.wait_chip(low)
+            self.wait_chip(low, halves)
             use(low)
 
         @pl.when(high < self.place.chips)
         def _():
-            self.wait_chip(high)
+            self.wait_chip(high, halves)
             use(high)
 
     def drain(self):
@@ -430,11 +430,11 @@
 
 
 class Scatter:
-    def __init__(self, place, work, scratch):
-        self.place, self.work = place, work
+    def __init__(self, place, work, scratch, halves=HALVES):
+        self.place, self.work, self.halves = place, work, halves
         self.out, self.side, self.line = scratch[:3]
         self.core_out, self.core_in, self.line_out, self.line_in = scratch[3:]
-        self.part = self.out.shape[1] // HALVES
+        self.part = self.out.shape[1] // halves
         chip, chips = place.chip, place.chips
         self.near = jnp.minimum(chip, chips - 1 - chip)
         self.alone = chips - 1 - 2 * self.near
@@ -479,8 +479,8 @@
         return remote(
             self.out.at[which, rows],
             self.line.at[slot, rows],
-            self.line_out.at[which * HALVES + half],
-            self.line_in.at[slot * HALVES + half],
+            self.line_out.at[which * self.halves + half],
+            self.line_in.at[slot * self.halves + half],
             self.place.at(target, self.place.core),
         )
 
@@ -498,7 +498,7 @@
         part = self.line.at[slot, rows]
         other = place.at(place.chip, 1 - place.core)
         remote(
-            part, part, self.line_out.at[0], self.line_in.at[slot * HALVES + half], other
+            part, part, self.line_out.at[0], self.line_in.at[slot * self.halves + half], other
         ).wait_recv()
         return self.line[slot, rows].astype(jnp.float32)
 
@@ -517,14 +517,14 @@
 
         @pl.when(upstream)
         def _():
-            for half in range(HALVES):
+            for half in range(self.halves):
                 rows = slice(half * self.part, (half + 1) * self.part)
                 self.out[which, rows] = (total[rows] + self.arrived(which, half)).astype(LOW)
                 copy(which, half).start()
 
         @pl.when(jnp.logical_not(upstream))
         def _():
-            for half in range(HALVES):
+            for half in range(self.halves):
                 rows = slice(half * self.part, (half + 1) * self.part)
                 self.out[which, rows] = total[rows].astype(LOW)
                 copy(which, half).start()
@@ -550,7 +550,7 @@
     def own(self, total):
         chip, chips = self.place.chip, self.place.chips
         total[...] = self.chip_sum(chip)
-        for half in range(HALVES):
+        for half in range(self.halves):
             rows = slice(half * self.part, (half + 1) * self.part)
 
             @pl.when(chip > 0)
@@ -565,11 +565,29 @@
         chip = self.place.chip
 
         def one(which):
-            for half in range(HALVES):
+            for half in range(self.halves):
                 pl.when(which > chip)(lambda: self.right(which, half).wait_send())
                 pl.when(which < chip)(lambda: self.left(which, half).wait_send())
 
         each(self.place.chips, one)
+
+
+class StoredScatter(Scatter):
+    def __init__(self, place, scratch, mine):
+        super().__init__(place, None, scratch, 1)
+        self.mine = mine
+
+    def put(self, which, other, own):
+        self.out[which] = other.astype(LOW)
+        self.across(which).start()
+        self.mine[which] = own.astype(LOW)
+
+    def produce(self, turn):
+        pass
+
+    def chip_sum(self, which):
+        self.across(which).wait()
+        return self.mine[which].astype(jnp.float32) + self.side[which].astype(jnp.float32)
 
 
 class Spread:
@@ -706,21 +724,23 @@
 def gather_project(groups, chips, tokens, gain, shift, shards, bias, tables):
     rows, width = tokens.shape
     length = rows * 2 * chips
-    qkv_shard, out_shard = shards
+    qkv_shard, out_shard, down_shard = shards
     part, out_width = qkv_shard.shape[1:]
+    upper = down_shard.shape[0] // 2
     tile = tables[0].shape[1]
 
     def kernel(
-        x_ref, gain_ref, shift_ref, qkv_ref, out_ref, bias_ref, cos_hbm, sin_low_hbm, sin_high_hbm,
-        kept, weights_kept, out_whole, q_ref, k_ref, v_ref,
-        full, weights, qkv_staged, out_staged, cos_ref, sin_low_ref, sin_high_ref,
+        x_ref, gain_ref, shift_ref, qkv_ref, out_ref, down_ref, bias_ref,
+        cos_hbm, sin_low_hbm, sin_high_hbm,
+        kept, weights_kept, out_whole, down_whole, q_ref, k_ref, v_ref,
+        full, weights, qkv_staged, out_staged, down_staged, cos_ref, sin_low_ref, sin_high_ref,
         load, keep_sem, *sems
     ):
         place = Place(groups, chips)
         fetches = fetch_all(
             [(cos_hbm, cos_ref), (sin_low_hbm, sin_low_ref), (sin_high_hbm, sin_high_ref)], load
         )
-        line, one, two = split_refs(sems, Gather.SEMS, 2, 2)
+        line, one, two, three = split_refs(sems, Gather.SEMS, 2, 2, 2)
         gather = Gather(place, full, line, kept, keep_sem)
         normed, _, _ = layer_norm_parts(
             x_ref[...].astype(jnp.float32), gain_ref[...], shift_ref[...]
@@ -732,6 +752,8 @@
         spread_qkv.start()
         spread_out = Spread(place, out_ref, out_staged, out_whole, 1, two)
         spread_out.start()
+        spread_down = Spread(place, down_ref.at[0:upper], down_staged, down_whole, 1, three)
+        spread_down.start()
 
         def work(chip):
             base = pl.multiple_of(chip * 2 * rows, 2 * rows)
@@ -769,6 +791,7 @@
         each(chips - 1, step)
         weights_keep.wait()
         spread_out.wait()
+        spread_down.wait()
         gather.drain()
 
     head_shape = shape((length, out_width))
@@ -781,6 +804,7 @@
             shape((length, width)),
             shape((3, width, out_width)),
             shape((out_width, width)),
+            shape((upper, width)),
             head_shape,
             head_shape,
             head_shape,
@@ -790,15 +814,16 @@
             pltpu.VMEM((3, width, out_width), LOW),
             pltpu.VMEM(qkv_shard.shape, LOW),
             pltpu.VMEM(out_shard.shape, LOW),
+            pltpu.VMEM((upper, down_shard.shape[1]), LOW),
             *(pltpu.VMEM((length, tile), jnp.float32) for _ in range(3)),
             pltpu.SemaphoreType.DMA((4,)),
             pltpu.SemaphoreType.DMA((chips,)),
         ]
         + Gather.scratch(chips)
-        + Spread.scratch(groups) * 2,
+        + Spread.scratch(groups) * 3,
         COST_FLOPS,
-        in_hbm=(0, 1, 2),
-        from_hbm=(6, 7, 8),
+        in_hbm=(0, 1, 2, 3),
+        from_hbm=(7, 8, 9),
     )
 
 
@@ -806,16 +831,17 @@
     rows, width = tokens.shape
     length, head_width = qkv[0].shape
     heads = head_width // HD
-    (pair_shard,) = shards
+    pair_shard, down_shard = shards
+    upper = down_shard.shape[0] // 2
 
     def kernel(
-        q_hbm, k_hbm, v_hbm, w_hbm, x_hbm, og_hbm, start_ref, pair_ref,
-        mid_ref, ctx_ref, lse_ref, kept, pair_whole,
-        full, q_ref, k_ref, v_ref, w_ref, x_ref, pair_staged,
+        q_hbm, k_hbm, v_hbm, w_hbm, x_hbm, og_hbm, start_ref, pair_ref, down_ref,
+        mid_ref, ctx_ref, lse_ref, kept, pair_whole, down_whole,
+        full, q_ref, k_ref, v_ref, w_ref, x_ref, pair_staged, down_staged,
         load, keep_sem, v_turned, acc, stats, *rest
     ):
         place = Place(groups, chips)
-        scratch, line, one = split_refs(rest, Scatter.SCRATCH, Gather.SEMS, 2)
+        scratch, line, one, two = split_refs(rest, Scatter.SCRATCH, Gather.SEMS, 2, 2)
         gather = Gather(place, full, line, kept, keep_sem)
         fetches = fetch_all(
             [
@@ -833,6 +859,8 @@
         gather.begin()
         spread_pair = Spread(place, pair_ref, pair_staged, pair_whole, 2, one)
         spread_pair.start()
+        spread_down = Spread(place, down_ref.at[upper:], down_staged, down_whole, 1, two)
+        spread_down.start()
         for copy in fetches[1:5]:
             copy.wait()
         for part in range(length // BLK):
@@ -887,6 +915,7 @@
         gather.drain()
         scatter.drain()
         spread_pair.wait()
+        spread_down.wait()
 
     return line_call(
         kernel,
@@ -899,6 +928,7 @@
             shape((8, length), jnp.float32),
             shape((length, width)),
             shape((2, pair_shard.shape[1], width)),
+            shape((down_shard.shape[0] - upper, width)),
         ],
         [
             pltpu.VMEM((length, width), LOW),
@@ -906,6 +936,7 @@
             pltpu.VMEM((head_width, width), LOW),
             pltpu.VMEM((rows, width), LOW),
             pltpu.VMEM(pair_shard.shape, LOW),
+            pltpu.VMEM((down_shard.shape[0] - upper, down_shard.shape[1]), LOW),
             pltpu.SemaphoreType.DMA((6,)),
             pltpu.SemaphoreType.DMA((chips,)),
             pltpu.VMEM((head_width, length), LOW),
@@ -914,216 +945,153 @@
         ]
         + Scatter.scratch(chips, rows, width)
         + Gather.scratch(chips)
-        + Spread.scratch(groups),
+        + Spread.scratch(groups) * 2,
         COST_FLOPS,
-        in_hbm=(3, 4),
+        in_hbm=(3, 4, 5),
         from_hbm=(0, 1, 2, 3, 4, 5),
     )
 
 
-def gather_hidden(groups, chips, middle, gain, shift, pair_weight, down_shard):
+def hidden_layers(groups, chips, middle, gain, shift, pair_weight, down_parts, grads):
     rows, width = middle.shape
     length = rows * 2 * chips
     hidden = pair_weight.shape[1]
+    upper = down_parts[0].shape[0]
+    part = width // groups
+    size = rows // HALVES
 
     def kernel(
-        mid_ref, gain_ref, shift_ref, pair_hbm, down_ref,
-        kept, hid_kept, one_kept, two_kept, down_whole,
-        full, hid_ref, one_ref, two_ref, pair_ref, down_staged, load, keep_sem, *rest
+        gain_ref, shift_ref, mid_hbm, pair_hbm, down_one, down_two, og_hbm,
+        kept, hid_kept, gg_kept, ug_kept, sum_ref, landed,
+        full, og_ref, pair_ref, down_ref, hid_ref, held, staged, mine, load, keep_sem, store_sem, *rest
     ):
         place = Place(groups, chips)
-        fetches = fetch_all([(pair_hbm, pair_ref)], load)
-        line, keeps, sems = split_refs(rest, Gather.SEMS, 3, 2)
+        first, second, line, sems = split_refs(rest, Scatter.SCRATCH, Scatter.SCRATCH, Gather.SEMS, 2)
+        fetches = fetch_all(
+            [
+                (mid_hbm, sum_ref),
+                (pair_hbm, pair_ref),
+                (down_one, down_ref.at[0:upper]),
+                (down_two, down_ref.at[upper:hidden]),
+                (og_hbm, og_ref),
+            ],
+            load,
+        )
         gather = Gather(place, full, line, kept, keep_sem)
-        normed, _, _ = layer_norm_parts(mid_ref[...], gain_ref[...], shift_ref[...])
+        scatters = [
+            StoredScatter(place, scratch, mine.at[half])
+            for half, scratch in enumerate((first, second))
+        ]
+        exchange = Exchange(place, staged, landed, sems)
+        fetches[0].wait()
+        normed, _, _ = layer_norm_parts(sum_ref[...], gain_ref[...], shift_ref[...])
         gather.own()[...] = normed.astype(LOW)
         place.barrier(True)
-        gather.begin()
-        spread_down = Spread(place, down_ref, down_staged, down_whole, 1, sems)
-        spread_down.start()
-        results = list(zip((hid_ref, one_ref, two_ref), (hid_kept, one_kept, two_kept), keeps))
-
-        def store(chip):
-            return [
-                pltpu.make_async_copy(
-                    block_of(a, chip, 2 * rows), block_of(b, chip, 2 * rows), sem.at[chip]
-                )
-                for a, b, sem in results
+        at_end = (place.chip == 0) | (place.chip == chips - 1)
+        gather.begin((0,))
+        pl.when(at_end)(lambda: gather.begin((1,)))
+        for copy in fetches[1:]:
+            copy.wait()
+
+        def work(chip, half):
+            pieces_of = [
+                pl.ds(pl.multiple_of((chip * 2 + core) * rows + half * size, size), size)
+                for core in range(2)
             ]
-
-        def work(chip):
-            for half in range(2):
-                here = pl.ds(pl.multiple_of((chip * 2 + half) * rows, rows), rows)
-                values = full[here, :]
-                gate = dot(values, pair_ref[0], NT)
-                up = dot(values, pair_ref[1], NT)
-                sigmoid = 1.0 / (1.0 + jnp.exp(-gate))
-                activated = gate * sigmoid
-                hid_ref[here, :] = (activated * up).astype(LOW)
-                slope = sigmoid * (1.0 + gate * (1.0 - sigmoid))
-                one_ref[here, :] = (up * slope).astype(LOW)
-                two_ref[here, :] = activated.astype(LOW)
-            for copy in store(chip):
+            values = jnp.concatenate([full[here, :] for here in pieces_of], axis=0)
+            gate = dot(values, pair_ref[0], NT)
+            up = dot(values, pair_ref[1], NT)
+            sigmoid = 1.0 / (1.0 + jnp.exp(-gate))
+            activated = gate * sigmoid
+            hidden_low = (activated * up).astype(LOW)
+            hidden_grad = dot(
+                jnp.concatenate([og_ref[here, :] for here in pieces_of], axis=0), down_ref[...], NT
+            )
+            slope = sigmoid * (1.0 + gate * (1.0 - sigmoid))
+            gate_grad = (hidden_grad * (up * slope)).astype(LOW)
+            up_grad = (hidden_grad * activated).astype(LOW)
+            held[0] = gate_grad
+            held[1] = up_grad
+            copies = []
+            for core, here in enumerate(pieces_of):
+                hid_ref[here, :] = hidden_low[core * size : (core + 1) * size]
+                from_held = pl.ds(core * size, size)
+                copies += [
+                    pltpu.make_async_copy(hid_ref.at[here], hid_kept.at[here], store_sem.at[core]),
+                    pltpu.make_async_copy(
+                        held.at[0, from_held], gg_kept.at[here], store_sem.at[2 + core]
+                    ),
+                    pltpu.make_async_copy(
+                        held.at[1, from_held], ug_kept.at[here], store_sem.at[4 + core]
+                    ),
+                ]
+            for copy in copies:
                 copy.start()
-
-        for copy in fetches:
-            copy.wait()
-        gather.wait_chip(place.chip)
-        work(place.chip)
-
-        def step(number):
-            gather.pass_on(number)
-            gather.each_new(number, work)
-
-        each(chips - 1, step)
+            term = dot(gate_grad, pair_ref[0]) + dot(up_grad, pair_ref[1])
+            low, high = term[0:size], term[size : 2 * size]
+            scatters[half].put(
+                chip,
+                jnp.where(place.core == 0, high, low),
+                jnp.where(place.core == 0, low, high),
+            )
+            for copy in copies:
+                copy.wait()
+
+        def fill(offset):
+            block = lax.rem(place.group + offset, groups)
+            columns = pl.ds(pl.multiple_of(block * part, part), part)
+            staged[offset] = dot(hid_ref[...], og_ref[:, columns], TN).astype(LOW)
+
+        def fill_send(offset):
+            fill(offset)
+            exchange.copy(offset).start()
+
+        gather.wait_chip(place.chip, (0,))
+        work(place.chip, 0)
+
+        def gather_first(step):
+            gather.pass_on(step, (0,))
+            gather.each_new(step, lambda chip: work(chip, 0), (0,))
+
+        each(chips - 1, gather_first)
+        pl.when(jnp.logical_not(at_end))(lambda: gather.begin((1,)))
+
+        def both(step):
+            scatters[0].slot(step)
+
+            @pl.when(step == 0)
+            def _():
+                gather.wait_chip(place.chip, (1,))
+                work(place.chip, 1)
+
+            gather.pass_on(step, (1,))
+            gather.each_new(step, lambda chip: work(chip, 1), (1,))
+
+        each(chips - 1, both)
+
+        def scatter_second(step):
+            scatters[1].slot(step)
+            pieces(step, groups, fill_send)
+            pl.when(step == 0)(lambda: scatters[0].own(sum_ref.at[0:size]))
+
+        each(chips - 1, scatter_second)
+        fill(0)
+        exchange.stay().start()
+        scatters[1].own(sum_ref.at[size:rows])
         gather.drain()
-
-        def stored(chip):
-            for copy in store(chip):
-                copy.wait()
-
-        each(chips, stored)
-        spread_down.wait()
+        scatters[0].drain()
+        scatters[1].drain()
+        exchange.wait()
 
     hidden_shape = shape((length, hidden))
     return line_call(
         kernel,
         "gather_hidden",
         3,
-        (middle, gain, shift, pair_weight, down_shard),
+        (gain, shift, middle, pair_weight, *down_parts, grads),
         [
             shape((length, width)),
             hidden_shape,
-            hidden_shape,
-            hidden_shape,
-            shape((down_shard.shape[0], width)),
-        ],
-        [
-            pltpu.VMEM((length, width), LOW),
-            *(pltpu.VMEM((length, hidden), LOW) for _ in range(3)),
-            pltpu.VMEM(pair_weight.shape, LOW),
-            pltpu.VMEM(down_shard.shape, LOW),
-            pltpu.SemaphoreType.DMA((1,)),
-            pltpu.SemaphoreType.DMA((chips,)),
-        ]
-        + Gather.scratch(chips)
-        + [pltpu.SemaphoreType.DMA((chips,)) for _ in range(3)]
-        + Spread.scratch(groups),
-        COST_FLOPS,
-        in_hbm=(0, 1, 2, 3, 4),
-        from_hbm=(3,),
-    )
-
-
-def scatter_hidden(groups, chips, grads, hidden_low, factors, down, pair_weight):
-    length, width = grads.shape
-    rows = length // (2 * chips)
-    hidden = down.shape[0]
-    part = width // groups
-
-    def kernel(
-        og_hbm, hid_hbm, one_hbm, two_hbm, down_hbm, pair_hbm,
-        gg_kept, ug_kept, sum_ref, landed,
-        og_ref, hid_ref, one_ref, two_ref, down_ref, pair_ref, gg_ref, ug_ref, staged,
-        load, load_og, load_one, load_two, keep_gg, keep_ug, *rest
-    ):
-        place = Place(groups, chips)
-        scratch, sems = split_refs(rest, Scatter.SCRATCH, 2)
-        chunked = ((og_hbm, og_ref, load_og), (one_hbm, one_ref, load_one), (two_hbm, two_ref, load_two))
-
-        def bring(chip):
-            return [
-                pltpu.make_async_copy(
-                    block_of(a, chip, 2 * rows), block_of(b, chip, 2 * rows), sem.at[chip]
-                )
-                for a, b, sem in chunked
-            ]
-
-        def store(block):
-            return [
-                pltpu.make_async_copy(block_of(a, block, rows), block_of(b, block, rows), sem.at[block])
-                for a, b, sem in ((gg_ref, gg_kept, keep_gg), (ug_ref, ug_kept, keep_ug))
-            ]
-
-        def work(chip, core):
-            block = chip * 2 + core
-            here = pl.ds(pl.multiple_of(block * rows, rows), rows)
-            hidden_grad = dot(og_ref[here, :], down_ref[...], NT)
-            gate_grad = (hidden_grad * one_ref[here, :].astype(jnp.float32)).astype(LOW)
-            up_grad = (hidden_grad * two_ref[here, :].astype(jnp.float32)).astype(LOW)
-            gg_ref[here, :] = gate_grad
-            ug_ref[here, :] = up_grad
-            for copy in store(block):
-                copy.start()
-            return dot(gate_grad, pair_ref[0]) + dot(up_grad, pair_ref[1])
-
-        exchange = Exchange(place, staged, landed, sems)
-        scatter = Scatter(place, work, scratch)
-        fetches = fetch_all([(down_hbm, down_ref), (pair_hbm, pair_ref)], load)
-
-        def begin(turn):
-            for copy in bring(scatter.order(turn)):
-                copy.start()
-
-        each(chips, begin)
-        late = pltpu.make_async_copy(hid_hbm, hid_ref, load.at[2])
-        late.start()
-        place.barrier(True)
-
-        def fill(offset):
-            block = lax.rem(place.group + offset, groups)
-            columns = pl.ds(pl.multiple_of(block * part, part), part)
-            staged[offset] = dot(hid_ref[...], og_ref[:, columns], TN).astype(LOW)
-
-        def fill_send(offset):
-            fill(offset)
-            exchange.copy(offset).start()
-
-        def brought(turn, _=0):
-            for copy in bring(scatter.order(turn)):
-                copy.wait()
-            return 0
-
-        def brought_once(turn):
-            brought(turn)
-
-        for copy in fetches:
-            copy.wait()
-        brought_once(0)
-        scatter.first()
-        pl.when(scatter.lag == 1)(functools.partial(brought_once, 1))
-
-        def step(number):
-            scatter.slot(number)
-
-            @pl.when(number == 0)
-            def _():
-                lax.fori_loop(1 + scatter.lag, chips, brought, 0)
-                late.wait()
-
-            pieces(number, groups, fill_send)
-
-        each(chips - 1, step)
-        scatter.last()
-        fill(0)
-        exchange.stay().start()
-        scatter.own(sum_ref)
-        scatter.drain()
-        exchange.wait()
-
-        def stored(block):
-            for copy in store(block):
-                copy.wait()
-
-        each(2 * chips, stored)
-
-    hidden_shape = shape((length, hidden))
-    return line_call(
-        kernel,
-        "scatter_hidden",
-        4,
-        (grads, hidden_low, *factors, down, pair_weight),
-        [
             hidden_shape,
             hidden_shape,
             shape((rows, width), jnp.float32),
@@ -1131,34 +1099,39 @@
         ],
         [
             pltpu.VMEM((length, width), LOW),
-            *(pltpu.VMEM((length, hidden), LOW) for _ in range(3)),
-            pltpu.VMEM(down.shape, LOW),
+            pltpu.VMEM((length, width), LOW),
             pltpu.VMEM(pair_weight.shape, LOW),
-            *(pltpu.VMEM((length, hidden), LOW) for _ in range(2)),
+            pltpu.VMEM((hidden, width), LOW),
+            pltpu.VMEM((length, hidden), LOW),
+            pltpu.VMEM((2, rows, hidden), LOW),
             pltpu.VMEM((groups, hidden, part), LOW),
-            pltpu.SemaphoreType.DMA((3,)),
-            *(pltpu.SemaphoreType.DMA((chips,)) for _ in range(3)),
-            *(pltpu.SemaphoreType.DMA((2 * chips,)) for _ in range(2)),
+            pltpu.VMEM((HALVES, chips, size, width), LOW),
+            pltpu.SemaphoreType.DMA((5,)),
+            pltpu.SemaphoreType.DMA((chips,)),
+            pltpu.SemaphoreType.DMA((6,)),
         ]
-        + Scatter.scratch(chips, rows, width)
+        + Scatter.scratch(chips, size, width) * 2
+        + Gather.scratch(chips)
         + Spread.scratch(groups),
         COST_FLOPS,
-        in_hbm=(0, 1, 3),
-        from_hbm=(0, 1, 2, 3, 4, 5),
+        in_hbm=(0, 1, 2, 3, 5),
+        from_hbm=(2, 3, 4, 5, 6),
     )
 
 
 def gather_context(
-    groups, chips, middle, normed_grad, out_grad, gain, shift, weight, hidden_low, down, normed, pair
+    groups, chips, middle, normed_grad, out_grad, gain, shift, weight, hidden_low, down_parts, normed, pair
 ):
     rows, width = middle.shape
     length = rows * 2 * chips
     out_width = weight.shape[0]
-    hidden = down.shape[0]
+    hidden = hidden_low.shape[1]
+    upper = down_parts[0].shape[0]
     part = width // groups
 
     def kernel(
-        mid_ref, ng_hbm, og_ref, gain_ref, shift_ref, w_hbm, hid_hbm, down_hbm, a_ref, gg_hbm, ug_hbm,
+        mid_ref, ng_hbm, og_ref, gain_ref, shift_ref, w_hbm, hid_hbm, down_one, down_two,
+        a_ref, gg_hbm, ug_hbm,
         kept, cg_ref, mg_ref, sums_ref, out_ref, landed,
         full, total, w_ref, hid_ref, down_ref, gg_ref, ug_ref, staged, columns_in, load, keep_sem, *rest
     ):
@@ -1177,7 +1150,8 @@
             pltpu.make_async_copy(a, b, load.at[4 + n])
             for n, (a, b) in enumerate(
                 (
-                    (down_hbm, down_ref),
+                    (down_one, down_ref.at[0:upper]),
+                    (down_two, down_ref.at[upper:hidden]),
                     (hid_hbm, hid_ref),
                     (w_hbm, w_ref),
                     (gg_hbm, gg_ref),
@@ -1224,10 +1198,10 @@
             exchange.copy(offset).start()
 
         scatter = Scatter(place, out_work, scratch)
-        late[0].wait()
-        late[1].wait()
+        for copy in late[:3]:
+            copy.wait()
         scatter.first()
-        for copy in late[2:]:
+        for copy in late[3:]:
             copy.wait()
 
         def step(number):
@@ -1257,7 +1231,7 @@
         kernel,
         "gather_context",
         5,
-        (middle, normed_grad, out_grad, gain, shift, weight, hidden_low, down, normed, *pair),
+        (middle, normed_grad, out_grad, gain, shift, weight, hidden_low, *down_parts, normed, *pair),
         [
             shape((length, width)),
             shape((length, out_width)),
@@ -1271,12 +1245,12 @@
             pltpu.VMEM((rows, width), jnp.float32),
             pltpu.VMEM(weight.shape, LOW),
             pltpu.VMEM((length, hidden), LOW),
-            pltpu.VMEM(down.shape, LOW),
+            pltpu.VMEM((hidden, width), LOW),
             pltpu.VMEM((length, hidden), LOW),
             pltpu.VMEM((length, hidden), LOW),
             pltpu.VMEM((groups, 2, hidden, part), LOW),
             pltpu.VMEM((2, length, part), LOW),
-            pltpu.SemaphoreType.DMA((9,)),
+            pltpu.SemaphoreType.DMA((10,)),
             pltpu.SemaphoreType.DMA((chips,)),
         ]
         + Scatter.scratch(chips, rows, width)
@@ -1284,7 +1258,7 @@
         + Spread.scratch(groups),
         COST_FLOPS,
         in_hbm=(0, 2, 5),
-        from_hbm=(1, 5, 6, 7, 8, 9, 10),
+        from_hbm=(1, 5, 6, 7, 8, 9, 10, 11),
     )
 
 
@@ -1471,24 +1445,22 @@
     tables = rotary_tables(place, min(head_width, 128))
 
     gate_up_turned = jnp.swapaxes(w_gate_up, 1, 2)
-    normed_one_all, qkv_all, out_all, *qkv = gather_project(
+    normed_one_all, qkv_all, out_all, down_one, *qkv = gather_project(
         groups,
         chips,
         inputs,
         gains[0],
         shifts[0],
-        (w_qkv, w_out),
+        (w_qkv, w_out, w_down),
         qkv_bias,
         tables,
     )
-    middle, context_flat, lse, mlp_grad, pair_all = scatter_heads(
-        groups, chips, qkv, start, out_all, inputs, out_grad, (gate_up_turned,)
-    )
-    normed_two_all, hidden_low, *factors, down_all = gather_hidden(
-        groups, chips, middle, gains[1], shifts[1], pair_all, w_down
-    )
-    gate_grad, up_grad, normed_two_grad, parts_down = scatter_hidden(
-        groups, chips, mlp_grad, hidden_low, factors, down_all, pair_all
+    middle, context_flat, lse, mlp_grad, pair_all, down_two = scatter_heads(
+        groups, chips, qkv, start, out_all, inputs, out_grad, (gate_up_turned, w_down)
+    )
+    down_parts = (down_one, down_two)
+    normed_two_all, hidden_low, gate_grad, up_grad, normed_two_grad, parts_down = hidden_layers(
+        groups, chips, middle, gains[1], shifts[1], pair_all, down_parts, mlp_grad
     )
     attn_grad_all, context_grad, middle_grad, sums_two, outputs, parts_pair = (
         gather_context(
@@ -1501,7 +1473,7 @@
             shifts[1],
             out_all,
             hidden_low,
-            down_all,
+            down_parts,
             normed_two_all,
             (gate_grad, up_grad),
         )

time: 640 us -> 601 us (0.939)
  Pallas kernels: 584 us -> 545 us
    pallas_call x6 -> x5, Pallas kernels: 553 us -> 510 us  [line_call(): pl.pallas_call(kernel, out_shape=out_shape, in_specs=ins, out_specs=outs,...]
where the time goes in v4:
time: 601 us; the launch traced here: 593 us
  Pallas kernels  545 us (91%)
  local copies, waits for them, and re-layouts  24.3 us (4%)
  other arithmetic  22.8 us (4%)
    pallas_call x5, Pallas kernels, line_call(): pl.pallas_call(kernel, out_shape=out_shape, in_specs=ins, out_specs=outs,...  510 us
    pallas_call x1, Pallas kernels, attention_backward(): pl.pallas_call(backward_kernel, grid_spec=pltpu.PrefetchScalarGridSpec(nu...  35.2 us
    sub x6, other arithmetic, adam_update(): return (master - rate * change, one_new, two_new)  20.3 us
    unnamed x68, local copies, waits for them, and re-layouts  18.1 us

profile of v4, /device:TPU:0, one launch (start us, length us, event | category | flops | bytes accessed | tf_op | source)
XLA Modules:
  0.0 593.5 jit_solution(14783856166101185738)
XLA Ops:
  0.7 0.1 pad.8.clone
  0.8 0.1 pad.5.clone
  0.8 0.9 compare_select_fusion
  1.7 0.3 reduce-window.6
  2.0 0.2 slice_reduce_fusion
  2.2 0.2 reduce-window.9
  2.4 0.1 broadcast.107
  2.5 0.6 subtract_subtract_fusion.start_ref
  3.1 0.1 iota_subtract_fusion
  3.1 0.1 slice.88
  3.2 1.4 fusion.17
  4.7 0.3 multiply_sine_fusion
  5.0 0.2 maximum_maximum_fusion.2
  5.2 0.1 tile.31
  5.3 1.3 copy.56.sin_high_hbm.sin_high_ref
  6.6 0.1 tile.14
  6.7 1.3 copy.55.sin_low_hbm.sin_low_ref
  8.0 0.1 tile.12
  8.1 1.3 copy.54.cos_hbm.cos_ref
  9.4 81.2 %gather_project.1 = (bf16[2048,2048]{1,0:T(8,128)(2,1)}, bf16[3,2048,256]{2,1,0:T(8,128)(2,1)}, bf16[256,2048]{1,0:T(8,128)(2,1)}, bf16[352,2048]{1,0:T(8,128)(2...) custom-call(bf16[256,2048]{1,0:T(8,128)(2,1)} %x_hbm.3, ...), custom_call_target="tpu_custom_call" | custom-call | flops 80000000000 | tf_op jit(solution)/shard_map/gather_project/pallas_call | solution.py:695
  90.7 101.4 %scatter_heads.1 = (f32[256,2048]{1,0:T(8,128)}, bf16[2048,256]{1,0:T(8,128)(2,1)}, f32[8,2048]{1,0:T(8,128)}, bf16[2048,2048]{1,0:T(8,128)(2,1)}, bf16[2,704,20...) custom-call(bf16[2048,256]{1,0:T(8,128)(2,1)} %get-tuple-element.63.q_hbm.q_ref, ...), custom_call_target="tpu_custom_call" | custom-call | flops 80000000000 | tf_op jit(solution)/shard_map/scatter_heads/pallas_call | solution.py:695
  192.1 131.6 %gather_hidden.1 = (bf16[2048,2048]{1,0:T(8,128)(2,1)}, bf16[2048,704]{1,0:T(8,128)(2,1)}, bf16[2048,704]{1,0:T(8,128)(2,1)}, bf16[2048,704]{1,0:T(8,128)(2,1)},...) custom-call(f32[1,2048]{1,0:T(1,128)} %get-tuple-element.141.gain_ref, f32[1,2048]{1,0:T(1,128)} %get-tuple-element.130.shift_ref, ...), custom_call_target="tpu_custom_call" | custom-call | flops 80000000000 | tf_op jit(solution)/shard_map/gather_hidden/pallas_call | solution.py:695
  323.6 0.0 copy-start
  323.6 0.0 copy-start.9
  323.7 101.5 %gather_context.1 = (bf16[2048,2048]{1,0:T(8,128)(2,1)}, bf16[2048,256]{1,0:T(8,128)(2,1)}, f32[256,2048]{1,0:T(8,128)}, f32[2,2048]{1,0:T(2,128)}, bf16[256,204...) custom-call(f32[256,2048]{1,0:T(8,128)} %get-tuple-element.67.mid_hbm.mid_ref, f32[256,2048]{1,0:T(8,128)} %get-tuple-element.72.ng_hbm, ...), custom_call_target="tpu_custom_call" | custom-call | flops 80000000000 | tf_op jit(solution)/shard_map/gather_context/pallas_call | solution.py:695
  425.2 0.0 copy-start.1
  425.2 1.2 copy-done.1
  426.4 1.2 copy-done.2
  427.7 1.2 copy-done.3
  428.9 1.2 copy-done.4
  430.1 1.2 copy-done.5
  431.4 1.2 copy-done.6
  432.6 1.2 copy-done.7
  433.8 35.2 %attention_backward.1 = (bf16[2048,256]{1,0:T(8,128)(2,1)S(1)}, bf16[2048,256]{1,0:T(8,128)(2,1)S(1)}, bf16[2048,256]{1,0:T(8,128)(2,1)S(1)}, f32[8,256]{1,0:T(8,128)S(1)}) custom-call(s32[8]{0:T(128)S(1)} %and_select_fusion.low_ref, bf16[2048,256]{1,0:T(8,128)(2,1)S(1)} %copy-done.4, bf16[2048,256]{1,0:T(8,128)(2,1)S(1)} %copy-done.5, ...), custom_call_target="tpu_custom_call" | custom-call | tf_op jit(solution)/shard_map/attention_backward/pallas_call | solution.py:220
  469.0 0.0 copy-start.10
  469.0 1.0 copy-done.10
  470.0 1.0 copy-done.11
  471.0 1.0 copy-done.12
  471.9 0.6 copy-done.13
  472.5 0.0 copy-start.26
  472.6 0.0 copy-start.23
  472.6 94.1 %scatter_triple.1 = (bf16[256,2048]{1,0:T(8,128)(2,1)}, f32[8,2048]{1,0:T(8,128)}, bf16[4,3,512,256]{3,2,1,0:T(8,128)(2,1)}, bf16[4,256,512]{2,1,0:T(8,128)(2,1)}) custom-call(bf16[2048,256]{1,0:T(8,128)(2,1)} %copy-done.10, bf16[2048,256]{1,0:T(8,128)(2,1)} %copy-done.11, bf16[2048,256]{1,0:T(8,128)(2,1)} %copy-done.12, ...), custom_call_target="tpu_custom_call" | custom-call | flops 80000000000 | tf_op jit(solution)/shard_map/scatter_triple/pallas_call | solution.py:695
  566.6 1.4 multiply_subtract_fusion.6
  568.0 0.0 copy-done.28
  568.0 1.7 multiply_subtract_fusion.4
  569.7 0.0 copy-start.22
  569.7 3.2 multiply_subtract_fusion.3
  572.9 0.0 copy-start.19
  572.9 0.0 copy-start.20
  573.0 0.0 copy-start.21
  573.0 0.0 copy-start.17
  573.0 5.0 multiply_subtract_fusion.2
  578.0 0.0 slice-start.1
  578.1 0.0 copy-start.15
  578.1 0.0 copy-start.16
  578.1 3.7 multiply_subtract_fusion.1
  581.8 1.3 slice-done
  583.0 0.4 slice-done.1
  583.4 0.9 copy-done.15
  584.3 0.8 copy-done.16
  585.1 5.3 multiply_subtract_fusion
  590.5 1.0 copy.62
  591.4 0.6 copy-done.25
  592.1 1.0 copy.63
  (42 shorter events, 0.1 us)
Async XLA Ops:
  323.6 101.6 %copy-start = (f32[2048,128]{1,0:T(8,128)S(1)}, f32[2048,128]{1,0:T(8,128)}, u32[]{:S(2)}) copy-start(f32[2048,128]{1,0:T(8,128)} %copy.56.sin_high_hbm.sin_high_ref) | copy-start | bytes 3145732
  323.6 101.6 %copy-start.8 = (f32[8,2048]{1,0:T(8,128)S(1)}, f32[8,2048]{1,0:T(8,128)}, u32[]{:S(2)}) copy-start(f32[8,2048]{1,0:T(8,128)} %get-tuple-element.78.lse_ref) | copy-start | bytes 196612
  323.6 101.6 %copy-start.9 = (s32[1,2048]{1,0:T(1,128)S(1)}, s32[1,2048]{1,0:T(1,128)}, u32[]{:S(2)}) copy-start(s32[1,2048]{1,0:T(1,128)} %subtract_subtract_fusion.start_ref) | copy-start | bytes 24580
  425.2 1.2 copy-start.1
  426.4 1.2 copy-start.2
  427.7 1.2 copy-start.3
  428.9 1.2 copy-start.4
  430.1 1.2 copy-start.5
  431.3 1.2 copy-start.6
  432.6 1.2 copy-start.7
  469.0 1.0 copy-start.10
  470.0 1.0 copy-start.11
  471.0 1.0 copy-start.12
  471.9 0.6 copy-start.13
  472.5 95.5 %copy-start.27 = (f32[2,2048]{1,0:T(2,128)S(1)}, f32[2,2048]{1,0:T(2,128)}, u32[]{:S(2)}) copy-start(f32[2,2048]{1,0:T(2,128)} %param.33) | copy-start | bytes 49156
  472.5 95.5 %copy-start.28 = (f32[2,2048]{1,0:T(2,128)S(1)}, f32[2,2048]{1,0:T(2,128)}, u32[]{:S(2)}) copy-start(f32[2,2048]{1,0:T(2,128)} %param.32) | copy-start | bytes 49156
  472.5 95.5 %copy-start.29 = (f32[2,2048]{1,0:T(2,128)S(1)}, f32[2,2048]{1,0:T(2,128)}, u32[]{:S(2)}) copy-start(f32[2,2048]{1,0:T(2,128)} %param.40) | copy-start | bytes 49156
  472.5 95.5 %copy-start.30 = (f32[2,2048]{1,0:T(2,128)S(1)}, f32[2,2048]{1,0:T(2,128)}, u32[]{:S(2)}) copy-start(f32[2,2048]{1,0:T(2,128)} %param.47) | copy-start | bytes 49156
  472.5 97.2 %copy-start.26 = (f32[256,512]{1,0:T(8,128)S(1)}, f32[256,512]{1,0:T(8,128)}, u32[]{:S(2)}) copy-start(f32[256,512]{1,0:T(8,128)} %out_ref.1) | copy-start | bytes 1572868
  472.6 100.3 %copy-start.23 = (f32[704,512]{1,0:T(8,128)S(1)}, f32[704,512]{1,0:T(8,128)}, u32[]{:S(2)}) copy-start(f32[704,512]{1,0:T(8,128)} %param.37) | copy-start | bytes 4325380
  569.7 3.2 copy-start.18
  569.7 3.2 copy-start.22
  572.9 5.1 copy-start.14
  572.9 5.1 copy-start.19
  572.9 5.1 copy-start.20
  573.0 5.1 copy-start.21
  573.0 8.8 %copy-start.17 = (f32[2,512,704]{1,2,0:T(8,128)S(1)}, f32[2,512,704]{1,2,0:T(8,128)}, u32[]{:S(2)}) copy-start(f32[2,512,704]{1,2,0:T(8,128)} %param.43) | copy-start | bytes 8650756
  578.0 5.0 slice-start
  578.0 5.4 slice-start.1
  578.1 6.2 %copy-start.15 = (f32[2,512,704]{1,2,0:T(8,128)S(1)}, f32[2,512,704]{1,2,0:T(8,128)}, u32[]{:S(2)}) copy-start(f32[2,512,704]{1,2,0:T(8,128)} %param.29) | copy-start | bytes 8650756
  578.1 7.1 %copy-start.16 = (f32[2,512,704]{1,2,0:T(8,128)S(1)}, f32[2,512,704]{1,2,0:T(8,128)}, u32[]{:S(2)}) copy-start(f32[2,512,704]{1,2,0:T(8,128)} %param.36) | copy-start | bytes 8650756
  585.1 5.4 copy-start.24
  590.5 1.6 copy-start.25

commit v5 on v4

--- a/solution.py
+++ b/solution.py
@@ -101,152 +101,6 @@
         acc[band, :] = acc[band, :] * fade + dot(
             v_turned[band, pl.ds(base, size)], prob.astype(jnp.bfloat16)
         )
-
-
-def backward_kernel(
-    low_ref,
-    q_ref,
-    k_ref,
-    v_ref,
-    start_ref,
-    lse_ref,
-    ctx_ref,
-    grad_ref,
-    cos_ref,
-    sin_low_ref,
-    sin_high_ref,
-    dq_ref,
-    dk_ref,
-    dv_ref,
-    bias_ref,
-    k_turned,
-    dq_acc,
-    dk_acc,
-    dv_acc,
-):
-    block = pl.program_id(0)
-    last = pl.num_programs(0) - 1
-    length, width = k_ref.shape
-    heads = width // HD
-    tile = min(width, 128)
-
-    @pl.when(block == 0)
-    def _():
-        for part in range(length // BLK):
-            rows = slice(part * BLK, (part + 1) * BLK)
-            k_turned[:, rows] = k_ref[rows, :].T
-        dk_acc[...] = jnp.zeros_like(dk_acc)
-        dv_acc[...] = jnp.zeros_like(dv_acc)
-        bias_ref[...] = jnp.zeros_like(bias_ref)
-
-    here = pl.ds(pl.multiple_of(block * BLK, BLK), BLK)
-    masks = head_masks(width, jnp.bfloat16)
-    queries = (q_ref[here, :] * 0.125).astype(jnp.bfloat16)
-    masked = [queries * m for m in masks]
-    grads = grad_ref[...]
-    grads_masked = [grads * m for m in masks]
-    product = grads.astype(jnp.float32) * ctx_ref[...].astype(jnp.float32)
-    select = (
-        lax.broadcasted_iota(jnp.int32, (8, width), 1) // HD
-        == lax.broadcasted_iota(jnp.int32, (8, width), 0)
-    ).astype(jnp.float32)
-    delta = dot(select, product, NT, lax.Precision.HIGHEST)
-    start = start_ref[...]
-    query_ids = block * BLK + lax.broadcasted_iota(jnp.int32, (1, BLK), 1)
-    dq_acc[...] = jnp.zeros_like(dq_acc)
-
-    def step(number, _):
-        base = pl.multiple_of(number * BLK, BLK)
-        rows_k = pl.ds(base, BLK)
-        keys = k_ref[rows_k, :]
-        vals = v_ref[rows_k, :]
-        key_ids = base + lax.broadcasted_iota(jnp.int32, (BLK, BLK), 0)
-        visible = (key_ids >= start) & (key_ids <= query_ids)
-        dk = dk_acc[rows_k, :]
-        dv = dv_acc[rows_k, :]
-        for h in range(heads):
-            scores = dot(keys, masked[h], NT)
-            prob = jnp.where(visible, jnp.exp(scores - lse_ref[h : h + 1, :]), 0.0)
-            dprob = dot(vals, grads_masked[h], NT)
-            dscore = (prob * (dprob - delta[h : h + 1, :])).astype(jnp.bfloat16)
-            dv = dv + dot(prob.astype(jnp.bfloat16), grads_masked[h])
-            dk = dk + dot(dscore, masked[h])
-            rows = slice(h * HD, (h + 1) * HD)
-            dq_acc[rows, :] += dot(k_turned[rows, rows_k], dscore)
-        dk_acc[rows_k, :] = dk
-        dv_acc[rows_k, :] = dv
-        return 0
-
-    lax.fori_loop(low_ref[block], block + 1, step, 0)
-
-    def turn_back(values, rows):
-        parts = []
-        for t in range(width // tile):
-            parts.append(
-                rope_tile(
-                    values[:, t * tile : (t + 1) * tile],
-                    cos_ref[rows, :],
-                    sin_low_ref[rows, :],
-                    sin_high_ref[rows, :],
-                    -1.0,
-                )
-            )
-        return jnp.concatenate(parts, axis=1) if len(parts) > 1 else parts[0]
-
-    dq = turn_back(dq_acc[...].T * 0.125, here).astype(jnp.bfloat16)
-    dq_ref[...] = dq
-    bias_ref[0:1, :] += jnp.sum(dq.astype(jnp.float32), axis=0, keepdims=True)
-
-    @pl.when(block == last)
-    def _():
-        def finish(part, _):
-            rows = pl.ds(pl.multiple_of(part * BLK, BLK), BLK)
-            dk = turn_back(dk_acc[rows, :], rows).astype(jnp.bfloat16)
-            dv = dv_acc[rows, :].astype(jnp.bfloat16)
-            dk_ref[rows, :] = dk
-            dv_ref[rows, :] = dv
-            bias_ref[1:2, :] += jnp.sum(dk.astype(jnp.float32), axis=0, keepdims=True)
-            bias_ref[2:3, :] += jnp.sum(dv.astype(jnp.float32), axis=0, keepdims=True)
-            return 0
-
-        lax.fori_loop(0, length // BLK, finish, 0)
-
-
-def attention_backward(low_blocks, queries, keys, values, start, lse, context, grads, tables):
-    length, width = queries.shape
-    whole = pl.BlockSpec((length, width), lambda i, low: (0, 0))
-    rows = pl.BlockSpec((BLK, width), lambda i, low: (i, 0))
-    table = pl.BlockSpec(tables[0].shape, lambda i, low: (0, 0))
-    return pl.pallas_call(
-        backward_kernel,
-        grid_spec=pltpu.PrefetchScalarGridSpec(
-            num_scalar_prefetch=1,
-            grid=(length // BLK,),
-            in_specs=[
-                whole,
-                whole,
-                whole,
-                pl.BlockSpec((1, BLK), lambda i, low: (0, i)),
-                pl.BlockSpec((8, BLK), lambda i, low: (0, i)),
-                rows,
-                rows,
-                table,
-                table,
-                table,
-            ],
-            out_specs=[rows, whole, whole, pl.BlockSpec((8, width), lambda i, low: (0, 0))],
-            scratch_shapes=[
-                pltpu.VMEM((width, length), jnp.bfloat16),
-                pltpu.VMEM((width, BLK), jnp.float32),
-                pltpu.VMEM((length, width), jnp.float32),
-                pltpu.VMEM((length, width), jnp.float32),
-            ],
-        ),
-        out_shape=[jax.ShapeDtypeStruct((length, width), jnp.bfloat16)] * 3
-        + [jax.ShapeDtypeStruct((8, width), jnp.float32)],
-        compiler_params=pltpu.CompilerParams(vmem_limit_bytes=40 << 20),
-        name="attention_backward",
-    )(low_blocks, queries, keys, values, start, lse, context, grads, *tables)
 
 
 MESH = pl.DeviceIdType.MESH
@@ -1262,63 +1116,196 @@
     )
 
 
+class PreparedScatter(Scatter):
+    def __init__(self, place, work, scratch, prepare):
+        super().__init__(place, work, scratch)
+        self.prepare = prepare
+
+    def produce(self, turn):
+        self.prepare(turn, self.order(turn))
+        super().produce(turn)
+
+
 def scatter_triple(
-    groups, chips, triple, weights, tokens, gain, shift, mid_grad, sums, bias_sums, normed, context, grads
+    groups, chips, qkv, start, lse, context, context_grad, tables, weights, tokens, gain, shift,
+    mid_grad, sums, normed, grads
 ):
-    length, in_width = triple[0].shape
+    length, in_width = qkv[0].shape
     rows = length // (2 * chips)
     width = weights.shape[1]
     part = width // groups
+    heads = in_width // HD
+    tile = tables[0].shape[1]
+    reach = LONGEST // rows
 
     def kernel(
-        q_ref, k_ref, v_ref, w_ref, gain_ref, shift_ref, sums_ref, bias_ref,
-        x_hbm, mg_hbm, a_hbm, ctx_hbm, full_hbm,
+        start_ref, lse_ref, gain_ref, shift_ref, sums_ref,
+        q_hbm, k_hbm, v_hbm, cg_hbm, ctx_hbm, cos_hbm, sin_low_hbm, sin_high_hbm,
+        w_hbm, x_hbm, mg_hbm, a_hbm, full_hbm,
         in_ref, small_ref, landed_qkv, landed_out,
-        x_ref, mg_ref, a_ref, ctx_ref, full_ref, load,
+        q_ref, k_ref, v_ref, cg_ref, ctx_ref, cos_ref, sin_low_ref, sin_high_ref,
+        w_ref, x_ref, mg_ref, columns_in, load, load_columns,
+        k_turned, dq_acc, dk_acc, dv_acc, delta, dq_ref, dk_ref, dv_ref, bias,
         total, staged_qkv, staged_out, early_spots, early_groups, late_spots, late_groups, *rest
     ):
         place = Place(groups, chips)
         scratch, one, two, sums_sems = split_refs(rest, Scatter.SCRATCH, 2, 2, 8)
         fetches = fetch_all(
             [
-                (a_hbm, a_ref),
+                (k_hbm, k_ref),
+                (q_hbm, q_ref),
+                (v_hbm, v_ref),
+                (cg_hbm, cg_ref),
                 (ctx_hbm, ctx_ref),
-                (full_hbm, full_ref),
+                (cos_hbm, cos_ref),
+                (sin_low_hbm, sin_low_ref),
+                (sin_high_hbm, sin_high_ref),
+                (w_hbm, w_ref),
                 (x_hbm, x_ref),
                 (mg_hbm, mg_ref),
             ],
             load,
         )
+        dq_acc[...] = jnp.zeros_like(dq_acc)
+        dk_acc[...] = jnp.zeros_like(dk_acc)
+        dv_acc[...] = jnp.zeros_like(dv_acc)
+        bias[...] = jnp.zeros_like(bias)
         place.barrier(True, True)
         spots, count = place.spot, 2 * chips
         early_a = SmallSum(early_spots, spots, count, place.fellow, sums_sems[0:2])
         early_b = SmallSum(early_groups, place.group, groups, place.peer, sums_sems[2:4])
         late_a = SmallSum(late_spots, spots, count, place.fellow, sums_sems[4:6])
         late_b = SmallSum(late_groups, place.group, groups, place.peer, sums_sems[6:8])
+        for copy in fetches[:9]:
+            copy.wait()
+        masks = head_masks(in_width, LOW)
+        select = (
+            lax.broadcasted_iota(jnp.int32, (8, in_width), 1) // HD
+            == lax.broadcasted_iota(jnp.int32, (8, in_width), 0)
+        ).astype(jnp.float32)
+
+        def set_up(block):
+            here = pl.ds(pl.multiple_of(block * rows, rows), rows)
+            k_turned[:, here] = k_ref[here, :].T
+            product = cg_ref[here, :].astype(jnp.float32) * ctx_ref[here, :].astype(jnp.float32)
+            delta[:, here] = dot(select, product, NT, lax.Precision.HIGHEST)
+
+        each(2 * chips, set_up)
+
+        def attend_back(query_block, key_block):
+            base_q = pl.multiple_of(query_block * rows, rows)
+            base_k = pl.multiple_of(key_block * rows, rows)
+            rows_q, rows_k = pl.ds(base_q, rows), pl.ds(base_k, rows)
+            queries = (q_ref[rows_q, :] * 0.125).astype(LOW)
+            incoming = cg_ref[rows_q, :]
+            keys, vals = k_ref[rows_k, :], v_ref[rows_k, :]
+            key_ids = base_k + lax.broadcasted_iota(jnp.int32, (rows, rows), 0)
+            query_ids = base_q + lax.broadcasted_iota(jnp.int32, (1, rows), 1)
+            visible = (key_ids >= start_ref[:, rows_q]) & (key_ids <= query_ids)
+            dk, dv = dk_acc[rows_k, :], dv_acc[rows_k, :]
+            for h in range(heads):
+                masked, incoming_masked = queries * masks[h], incoming * masks[h]
+                scores = dot(keys, masked, NT)
+                prob = jnp.where(visible, jnp.exp(scores - lse_ref[h : h + 1, rows_q]), 0.0)
+                dprob = dot(vals, incoming_masked, NT)
+                dscore = (prob * (dprob - delta[h : h + 1, rows_q])).astype(LOW)
+                dv = dv + dot(prob.astype(LOW), incoming_masked)
+                dk = dk + dot(dscore, masked)
+                band = slice(h * HD, (h + 1) * HD)
+                dq_acc[band, rows_q] += dot(k_turned[band, rows_k], dscore)
+            dk_acc[rows_k, :] = dk
+            dv_acc[rows_k, :] = dv
+
+        def turn_back(values, here):
+            parts = [
+                rope_tile(
+                    values[:, t * tile : (t + 1) * tile],
+                    cos_ref[here, :],
+                    sin_low_ref[here, :],
+                    sin_high_ref[here, :],
+                    -1.0,
+                )
+                for t in range(in_width // tile)
+            ]
+            return jnp.concatenate(parts, axis=1) if len(parts) > 1 else parts[0]
+
+        def prepare(turn, chip):
+            def with_chip(other):
+                done = 0
+                for earlier in range(chips):
+                    done = done + jnp.where(
+                        (scatter.order(earlier) == other) & (earlier < turn), 1, 0
+                    )
+                upper, lower = jnp.maximum(chip, other), jnp.minimum(chip, other)
+
+                @pl.when(done == 0)
+                def _():
+                    def one(number):
+                        query_block = upper * 2 + number // 2
+                        key_block = lower * 2 + number % 2
+                        pl.when(
+                            (key_block <= query_block) & (query_block - key_block <= reach)
+                        )(lambda: attend_back(query_block, key_block))
+
+                    each(4, one)
+
+            each(chips, with_chip)
+
+            def finish(core):
+                here = pl.ds(pl.multiple_of((chip * 2 + core) * rows, rows), rows)
+                dq = turn_back(dq_acc[:, here].T * 0.125, here).astype(LOW)
+                dk = turn_back(dk_acc[here, :], here).astype(LOW)
+                dv = dv_acc[here, :].astype(LOW)
+                for number, (ref, values) in enumerate(((dq_ref, dq), (dk_ref, dk), (dv_ref, dv))):
+                    ref[here, :] = values
+                    bias[number : number + 1, :] += jnp.sum(
+                        values.astype(jnp.float32), axis=0, keepdims=True
+                    )
+
+            each(2, finish)
 
         def work(chip, core):
             here = pl.ds(pl.multiple_of((chip * 2 + core) * rows, rows), rows)
-            term = dot(q_ref[here, :], w_ref[0], NT)
-            term = term + dot(k_ref[here, :], w_ref[1], NT)
-            return term + dot(v_ref[here, :], w_ref[2], NT)
+            term = dot(dq_ref[here, :], w_ref[0], NT)
+            term = term + dot(dk_ref[here, :], w_ref[1], NT)
+            return term + dot(dv_ref[here, :], w_ref[2], NT)
 
         exchange_qkv = Exchange(place, staged_qkv, landed_qkv, one)
         exchange_out = Exchange(place, staged_out, landed_out, two)
 
-        def fill(offset):
+        def columns_of(offset):
             block = lax.rem(place.group + offset, groups)
-            columns = pl.ds(pl.multiple_of(block * part, part), part)
-            values = a_ref[:, columns]
-            for number, ref in enumerate((q_ref, k_ref, v_ref)):
+            return pl.ds(pl.multiple_of(block * part, part), part)
+
+        def fetch(source, index):
+            columns = columns_of(lax.rem(index + 1, groups))
+            slot = lax.rem(index, 2)
+            return pltpu.make_async_copy(
+                source.at[:, columns], columns_in.at[slot], load_columns.at[slot]
+            )
+
+        def fill_out(index):
+            fetch(full_hbm, index).wait()
+            offset = lax.rem(index + 1, groups)
+            staged_out[offset] = dot(ctx_ref[...], columns_in[lax.rem(index, 2)], TN).astype(LOW)
+            pl.when(offset > 0)(lambda: exchange_out.copy(offset).start())
+            pl.when(offset == 0)(lambda: exchange_out.stay().start())
+            pl.when(index + 2 < groups)(lambda: fetch(full_hbm, index + 2).start())
+            pl.when(index + 2 >= groups)(lambda: fetch(a_hbm, index + 2 - groups).start())
+
+        def fill_qkv(index):
+            fetch(a_hbm, index).wait()
+            offset = lax.rem(index + 1, groups)
+            values = columns_in[lax.rem(index, 2)]
+            for number, ref in enumerate((dq_ref, dk_ref, dv_ref)):
                 staged_qkv[offset, number] = dot(values, ref[...], TN).astype(LOW)
-            staged_out[offset] = dot(ctx_ref[...], full_ref[:, columns], TN).astype(LOW)
-
-        def fill_send(offset):
-            fill(offset)
-            exchange_qkv.copy(offset).start()
-            exchange_out.copy(offset).start()
-
-        scatter = Scatter(place, work, scratch)
+            pl.when(offset > 0)(lambda: exchange_qkv.copy(offset).start())
+            pl.when(offset == 0)(lambda: exchange_qkv.stay().start())
+            pl.when(index + 2 < groups)(lambda: fetch(a_hbm, index + 2).start())
+
+        fetch(full_hbm, 0).start()
+        fetch(full_hbm, 1).start()
+        scatter = PreparedScatter(place, work, scratch, prepare)
         scatter.first()
 
         def step(number):
@@ -1327,23 +1314,17 @@
             @pl.when(number == 0)
             def _():
                 early_a.begin(sums_ref[...])
-                for copy in fetches:
+                for copy in fetches[9:]:
                     copy.wait()
-
-            pieces(number, groups, fill_send)
-
-            @pl.when(number == chips - 2)
-            def _():
-                early_groups[place.group] = jnp.zeros(early_groups.shape[1:], jnp.float32)
-                early_groups[place.group, 4:7, 0:in_width] = bias_ref[0:3, :]
-                early_groups[place.group, 0:2, :] = early_a.result()
-                early_b.begin(early_groups[place.group])
+                each(groups, fill_out)
 
         each(chips - 1, step)
         scatter.last()
-        fill(0)
-        exchange_qkv.stay().start()
-        exchange_out.stay().start()
+        each(groups, fill_qkv)
+        early_groups[place.group] = jnp.zeros(early_groups.shape[1:], jnp.float32)
+        early_groups[place.group, 4:7, 0:in_width] = bias[0:3, :]
+        early_groups[place.group, 0:2, :] = early_a.result()
+        early_b.begin(early_groups[place.group])
         _, plain, inverse = layer_norm_parts(
             x_ref[...].astype(jnp.float32), gain_ref[...], shift_ref[...]
         )
@@ -1352,8 +1333,6 @@
         late_a.begin(jnp.concatenate([gain_grad[None, :], shift_grad[None, :]], axis=0))
         in_ref[...] = (mg_ref[...] + back).astype(LOW)
         scatter.drain()
-        exchange_qkv.wait()
-        exchange_out.wait()
         late_b.begin(late_a.result())
         first = early_b.result()
         last = late_b.result()
@@ -1362,13 +1341,20 @@
         small_ref[3:4, :] = first[1:2, :]
         small_ref[0:1, :] = last[0:1, :]
         small_ref[2:3, :] = last[1:2, :]
+        exchange_qkv.wait()
+        exchange_out.wait()
 
     devices = 2 * chips
+    heads_kind = pltpu.VMEM((length, in_width), LOW)
+    heads_sum = pltpu.VMEM((length, in_width), jnp.float32)
     return line_call(
         kernel,
         "scatter_triple",
         6,
-        (*triple, weights, gain, shift, sums, bias_sums, tokens, mid_grad, normed, context, grads),
+        (
+            start, lse, gain, shift, sums,
+            *qkv, context_grad, context, *tables, weights, tokens, mid_grad, normed, grads,
+        ),
         [
             shape((rows, width)),
             shape((8, width), jnp.float32),
@@ -1376,12 +1362,23 @@
             shape((groups, in_width, part)),
         ],
         [
+            *(heads_kind for _ in range(5)),
+            *(pltpu.VMEM((length, tile), jnp.float32) for _ in range(3)),
+            pltpu.VMEM(weights.shape, LOW),
             pltpu.VMEM((rows, width), LOW),
             pltpu.VMEM((rows, width), jnp.float32),
-            pltpu.VMEM((length, width), LOW),
-            pltpu.VMEM((length, in_width), LOW),
-            pltpu.VMEM((length, width), LOW),
-            pltpu.SemaphoreType.DMA((5,)),
+            pltpu.VMEM((2, length, part), LOW),
+            pltpu.SemaphoreType.DMA((11,)),
+            pltpu.SemaphoreType.DMA((2,)),
+            pltpu.VMEM((in_width, length), LOW),
+            pltpu.VMEM((in_width, length), jnp.float32),
+            heads_sum,
+            heads_sum,
+            pltpu.VMEM((8, length), jnp.float32),
+            heads_kind,
+            heads_kind,
+            heads_kind,
+            pltpu.VMEM((8, in_width), jnp.float32),
             pltpu.VMEM((rows, width), jnp.float32),
             pltpu.VMEM((groups, 3, part, in_width), LOW),
             pltpu.VMEM((groups, in_width, part), LOW),
@@ -1395,7 +1392,7 @@
         + [pltpu.SemaphoreType.DMA((n,)) for n in (devices, devices, groups, groups) * 2],
         COST_FLOPS,
         in_hbm=(2, 3),
-        from_hbm=(8, 9, 10, 11, 12),
+        from_hbm=tuple(range(5, 18)),
     )
 
 
@@ -1440,7 +1437,6 @@
     shifts = (norm_bias[0:1], norm_bias[1:2])
     place = positions(segments)[0]
     start = jnp.arange(length, dtype=jnp.int32) - place
-    low_blocks = start[::BLK] // BLK
     start = start[None, :]
     tables = rotary_tables(place, min(head_width, 128))
 
@@ -1478,22 +1474,22 @@
             (gate_grad, up_grad),
         )
     )
-    *triple, bias_sums = attention_backward(
-        low_blocks, *qkv, start, lse, context_flat, context_grad, tables
-    )
     input_grad, small, parts_qkv, parts_out = scatter_triple(
         groups,
         chips,
-        triple,
+        qkv,
+        start,
+        lse,
+        context_flat,
+        context_grad,
+        tables,
         qkv_all,
         inputs,
         gains[0],
         shifts[0],
         middle_grad,
         sums_two,
-        bias_sums,
         normed_one_all,
-        context_flat,
         attn_grad_all,
     )
 

time: 601 us -> 578 us (0.962)
  the two profiles are of different devices: /device:TPU:0 before, /device:TPU:10 now
where the time goes in v5:
time: 578 us; the launch traced here: 571 us
  Pallas kernels  534 us (92%)
  other arithmetic  22.8 us (4%)
  local copies, waits for them, and re-layouts  12.1 us (2%)
    pallas_call x5, Pallas kernels, line_call(): pl.pallas_call(kernel, out_shape=out_shape, in_specs=ins, out_specs=outs,...  534 us
    sub x6, other arithmetic, adam_update(): return (master - rate * change, one_new, two_new)  20.3 us

profile of v5, /device:TPU:10, one launch (start us, length us, event | category | flops | bytes accessed | tf_op | source)
XLA Modules:
  0.0 570.6 jit_solution(352449083451150139)
XLA Ops:
  0.7 0.1 pad.8.clone
  0.8 0.1 pad.5.clone
  0.8 0.9 compare_select_fusion
  1.7 0.3 reduce-window.6
  2.0 0.2 slice_reduce_fusion
  2.2 0.2 reduce-window.9
  2.4 0.1 fusion.8
  2.5 0.1 broadcast.95
  2.5 0.6 subtract_subtract_fusion.start_ref
  3.1 1.4 fusion.17
  4.6 0.3 multiply_sine_fusion
  4.9 0.2 maximum_maximum_fusion.2
  5.1 0.1 tile.31
  5.2 1.3 copy.56.sin_high_hbm
  6.5 0.1 tile.14
  6.6 1.3 copy.55.sin_low_hbm
  7.9 0.1 tile.12
  8.0 1.3 copy.54.cos_hbm
  9.3 74.4 %gather_project.1 = (bf16[2048,2048]{1,0:T(8,128)(2,1)}, bf16[3,2048,256]{2,1,0:T(8,128)(2,1)}, bf16[256,2048]{1,0:T(8,128)(2,1)}, bf16[352,2048]{1,0:T(8,128)(2...) custom-call(bf16[256,2048]{1,0:T(8,128)(2,1)} %x_hbm.3, ...), custom_call_target="tpu_custom_call" | custom-call | flops 80000000000 | tf_op jit(solution)/shard_map/gather_project/pallas_call | solution.py:549
  83.8 107.0 %scatter_heads.1 = (f32[256,2048]{1,0:T(8,128)}, bf16[2048,256]{1,0:T(8,128)(2,1)}, f32[8,2048]{1,0:T(8,128)}, bf16[2048,2048]{1,0:T(8,128)(2,1)}, bf16[2,704,20...) custom-call(bf16[2048,256]{1,0:T(8,128)(2,1)} %get-tuple-element.59.q_hbm, bf16[2048,256]{1,0:T(8,128)(2,1)} %get-tuple-element.60.k_hbm, ...), custom_call_target="tpu_custom_call" | custom-call | flops 80000000000 | tf_op jit(solution)/shard_map/scatter_heads/pallas_call | solution.py:549
  190.8 130.9 %gather_hidden.1 = (bf16[2048,2048]{1,0:T(8,128)(2,1)}, bf16[2048,704]{1,0:T(8,128)(2,1)}, bf16[2048,704]{1,0:T(8,128)(2,1)}, bf16[2048,704]{1,0:T(8,128)(2,1)},...) custom-call(f32[1,2048]{1,0:T(1,128)} %get-tuple-element.131.gain_ref, f32[1,2048]{1,0:T(1,128)} %get-tuple-element.122.shift_ref, ...), custom_call_target="tpu_custom_call" | custom-call | flops 80000000000 | tf_op jit(solution)/shard_map/gather_hidden/pallas_call | solution.py:549
  321.7 102.0 %gather_context.1 = (bf16[2048,2048]{1,0:T(8,128)(2,1)}, bf16[2048,256]{1,0:T(8,128)(2,1)}, f32[256,2048]{1,0:T(8,128)}, f32[2,2048]{1,0:T(2,128)}, bf16[256,204...) custom-call(f32[256,2048]{1,0:T(8,128)} %get-tuple-element.63.mid_hbm.mid_ref, f32[256,2048]{1,0:T(8,128)} %get-tuple-element.68.ng_hbm, ...), custom_call_target="tpu_custom_call" | custom-call | flops 80000000000 | tf_op jit(solution)/shard_map/gather_context/pallas_call | solution.py:549
  423.7 0.0 copy-start.13
  423.7 0.0 copy-start.14
  423.7 0.0 copy-start.15
  423.7 0.0 copy-start.16
  423.7 0.0 copy-start.12
  423.8 0.0 copy-start.9
  423.8 120.0 %scatter_triple.1 = (bf16[256,2048]{1,0:T(8,128)(2,1)}, f32[8,2048]{1,0:T(8,128)}, bf16[4,3,512,256]{3,2,1,0:T(8,128)(2,1)}, bf16[4,256,512]{2,1,0:T(8,128)(2,1)}) custom-call(s32[1,2048]{1,0:T(1,128)} %subtract_subtract_fusion.start_ref, f32[8,2048]{1,0:T(8,128)} %get-tuple-element.74.lse_ref, f32[1,2048]{1,0:T(1,128)} %get-tuple-element.130.gain_ref, ...), custom_call_target="tpu_custom_call" | custom-call | flops 80000000000 | tf_op jit(solution)/shard_map/scatter_triple/pallas_call | solution.py:549
  543.8 1.4 multiply_subtract_fusion.6
  545.2 0.0 copy-done.13
  545.2 0.0 copy-done.14
  545.2 0.0 copy-done.15
  545.2 0.0 copy-done.16
  545.2 1.7 multiply_subtract_fusion.4
  546.8 0.0 copy-done.12
  546.9 0.0 copy-start.8
  546.9 3.2 multiply_subtract_fusion.3
  550.1 0.0 copy-done.9
  550.1 0.0 copy-done.4
  550.1 0.0 copy-done.8
  550.1 0.0 copy-start
  550.1 0.0 copy-start.5
  550.1 0.0 copy-start.6
  550.1 0.0 copy-start.7
  550.1 0.0 copy-start.3
  550.1 5.0 multiply_subtract_fusion.2
  555.2 0.0 copy-done
  555.2 0.0 copy-done.5
  555.2 0.0 copy-done.6
  555.2 0.0 copy-done.7
  555.2 0.0 slice-start.1
  555.2 0.0 copy-start.1
  555.2 0.0 copy-start.2
  555.2 3.7 multiply_subtract_fusion.1
  558.9 0.0 copy-done.3
  558.9 1.3 slice-done
  560.2 0.4 slice-done.1
  560.6 0.9 copy-done.1
  561.4 0.8 copy-done.2
  562.3 5.3 multiply_subtract_fusion
  567.6 1.0 copy.62
  568.6 0.6 copy-done.11
  569.2 1.0 copy.63
  (11 shorter events, 0.0 us)
Async XLA Ops:
  423.7 121.5 %copy-start.13 = (f32[2,2048]{1,0:T(2,128)S(1)}, f32[2,2048]{1,0:T(2,128)}, u32[]{:S(2)}) copy-start(f32[2,2048]{1,0:T(2,128)} %param.33) | copy-start | bytes 49156
  423.7 121.5 %copy-start.14 = (f32[2,2048]{1,0:T(2,128)S(1)}, f32[2,2048]{1,0:T(2,128)}, u32[]{:S(2)}) copy-start(f32[2,2048]{1,0:T(2,128)} %param.32) | copy-start | bytes 49156
  423.7 121.4 %copy-start.15 = (f32[2,2048]{1,0:T(2,128)S(1)}, f32[2,2048]{1,0:T(2,128)}, u32[]{:S(2)}) copy-start(f32[2,2048]{1,0:T(2,128)} %param.40) | copy-start | bytes 49156
  423.7 121.4 %copy-start.16 = (f32[2,2048]{1,0:T(2,128)S(1)}, f32[2,2048]{1,0:T(2,128)}, u32[]{:S(2)}) copy-start(f32[2,2048]{1,0:T(2,128)} %param.47) | copy-start | bytes 49156
  423.7 123.1 %copy-start.12 = (f32[256,512]{1,0:T(8,128)S(1)}, f32[256,512]{1,0:T(8,128)}, u32[]{:S(2)}) copy-start(f32[256,512]{1,0:T(8,128)} %out_ref.1) | copy-start | bytes 1572868
  423.8 126.3 %copy-start.9 = (f32[704,512]{1,0:T(8,128)S(1)}, f32[704,512]{1,0:T(8,128)}, u32[]{:S(2)}) copy-start(f32[704,512]{1,0:T(8,128)} %param.37) | copy-start | bytes 4325380
  546.8 3.2 copy-start.4
  546.9 3.2 copy-start.8
  550.1 5.1 copy-start
  550.1 5.1 copy-start.5
  550.1 5.1 copy-start.6
  550.1 5.1 copy-start.7
  550.1 8.8 %copy-start.3 = (f32[2,512,704]{1,2,0:T(8,128)S(1)}, f32[2,512,704]{1,2,0:T(8,128)}, u32[]{:S(2)}) copy-start(f32[2,512,704]{1,2,0:T(8,128)} %param.43) | copy-start | bytes 8650756
  555.2 5.0 slice-start
  555.2 5.4 slice-start.1
  555.2 6.2 %copy-start.1 = (f32[2,512,704]{1,2,0:T(8,128)S(1)}, f32[2,512,704]{1,2,0:T(8,128)}, u32[]{:S(2)}) copy-start(f32[2,512,704]{1,2,0:T(8,128)} %param.29) | copy-start | bytes 8650756
  555.2 7.1 %copy-start.2 = (f32[2,512,704]{1,2,0:T(8,128)S(1)}, f32[2,512,704]{1,2,0:T(8,128)}, u32[]{:S(2)}) copy-start(f32[2,512,704]{1,2,0:T(8,128)} %param.36) | copy-start | bytes 8650756
  562.3 5.4 copy-start.10
  567.6 1.6 copy-start.11

commit v6 on v5

--- a/solution.py
+++ b/solution.py
@@ -30,34 +30,6 @@
     return (inner * inverse, jnp.sum(incoming * normed, axis=0), jnp.sum(incoming, axis=0))
 
 
-def positions(segment_ids):
-    length = segment_ids.shape[-1]
-    indices = jnp.broadcast_to(jnp.arange(length, dtype=jnp.int32), segment_ids.shape)
-    before = jnp.concatenate(
-        [jnp.full(segment_ids.shape[:-1] + (1,), -1, jnp.int32), segment_ids[..., :-1]], axis=-1
-    )
-    starts = lax.cummax(jnp.where(segment_ids != before, indices, 0), axis=segment_ids.ndim - 1)
-    return indices - starts
-
-
-def rotary_tables(position_ids, width):
-    half_rot = ROT // 2
-    frequency = 10000.0 ** (-(2.0 * jnp.arange(half_rot, dtype=jnp.float32)) / ROT)
-    angles = position_ids.astype(jnp.float32)[:, None] * frequency
-    cosine, sine = jnp.cos(angles), jnp.sin(angles)
-    zeros = jnp.zeros((angles.shape[0], HD - ROT), jnp.float32)
-    blank = jnp.zeros_like(sine)
-    copies = width // HD
-    return tuple(
-        jnp.tile(jnp.concatenate(parts, axis=1), (1, copies))
-        for parts in (
-            (cosine, cosine, zeros + 1.0),
-            (-sine, blank, zeros),
-            (blank, sine, zeros),
-        )
-    )
-
-
 NEG = -1e30
 BLK = 256
 NT = (((1,), (1,)), ((), ()))
@@ -75,17 +47,18 @@
     return [(lane // HD == h).astype(dtype) for h in range(width // HD)]
 
 
-def rope_tile(tile, cosine, sine_low, sine_high, sign):
+def rope_tile(tile, cosine, sine, sign):
     width = tile.shape[-1]
+    lane = lax.rem(lax.broadcasted_iota(jnp.int32, tile.shape, 1), HD)
     ahead = pltpu.roll(tile, width - ROT // 2, 1)
     behind = pltpu.roll(tile, ROT // 2, 1)
-    return tile * cosine + sign * (ahead * sine_low + behind * sine_high)
+    return tile * cosine + sign * (jnp.where(lane < ROT // 2, ahead, behind) * sine)
 
 
 def attend(number, size, k_ref, v_turned, masked, starts, query_ids, acc, stats):
-    base = pl.multiple_of(number * size, size)
-    keys = k_ref[pl.ds(base, size), :]
-    key_ids = base + lax.broadcasted_iota(jnp.int32, (size, size), 0)
+    base = pl.multiple_of(number * 2 * size, 2 * size)
+    keys = k_ref[pl.ds(base, 2 * size), :]
+    key_ids = base + lax.broadcasted_iota(jnp.int32, (2 * size, size), 0)
     visible = (key_ids >= starts) & (key_ids <= query_ids)
     for h, queries in enumerate(masked):
         scores = jnp.where(visible, dot(keys, queries, NT), NEG)
@@ -99,13 +72,14 @@
         )
         band = slice(h * HD, (h + 1) * HD)
         acc[band, :] = acc[band, :] * fade + dot(
-            v_turned[band, pl.ds(base, size)], prob.astype(jnp.bfloat16)
+            v_turned[band, pl.ds(base, 2 * size)], prob.astype(jnp.bfloat16)
         )
 
 
 MESH = pl.DeviceIdType.MESH
-VMEM_BYTES = 62 << 20
+VMEM_BYTES = (127 << 20) // 2
 LONGEST = 1024
+DOCUMENTS = 4
 TN = (((0,), (0,)), ((), ()))
 LOW = jnp.bfloat16
 
@@ -386,9 +360,13 @@
     def first(self):
         pl.when(self.lag == 1)(lambda: self.produce(0))
 
-    def slot(self, number):
+    def slot(self, number, before_last=None):
         chip, chips = self.place.chip, self.place.chips
-        self.produce(number + self.lag)
+        if before_last is None:
+            self.produce(number + self.lag)
+        else:
+            pl.when(self.lag == 0)(lambda: self.produce(number))
+            pl.when((self.lag == 1) & (number == chips - 2))(before_last)
         right = chips - 1 - (number - chip)
         left = number - (chips - 1 - chip)
         pl.when((number >= chip) & (right > chip))(
@@ -397,6 +375,11 @@
         pl.when((left >= 0) & (left < chip))(
             lambda: self.send(left, chip < chips - 1, self.left)
         )
+        if before_last is not None:
+            count = jnp.where(number < chips - 3, 1, jnp.where(number == chips - 3, 2, 0))
+            pl.when(self.lag == 1)(
+                lambda: each(count, lambda index: self.produce(number + 1 + index))
+            )
 
     def last(self):
         pl.when(self.lag == 0)(lambda: self.produce(self.place.chips - 1))
@@ -575,25 +558,21 @@
     return parts
 
 
-def gather_project(groups, chips, tokens, gain, shift, shards, bias, tables):
+def gather_project(groups, chips, tokens, gain, shift, shards, bias, segments, rates):
     rows, width = tokens.shape
     length = rows * 2 * chips
     qkv_shard, out_shard, down_shard = shards
     part, out_width = qkv_shard.shape[1:]
     upper = down_shard.shape[0] // 2
-    tile = tables[0].shape[1]
+    tile = rates.shape[1]
 
     def kernel(
-        x_ref, gain_ref, shift_ref, qkv_ref, out_ref, down_ref, bias_ref,
-        cos_hbm, sin_low_hbm, sin_high_hbm,
+        x_ref, gain_ref, shift_ref, qkv_ref, out_ref, down_ref, bias_ref, segment_ref, rate_ref,
         kept, weights_kept, out_whole, down_whole, q_ref, k_ref, v_ref,
-        full, weights, qkv_staged, out_staged, down_staged, cos_ref, sin_low_ref, sin_high_ref,
-        load, keep_sem, *sems
+        k_turned, v_turned, start_ref, cos_ref, sin_ref,
+        full, weights, qkv_staged, out_staged, down_staged, load, keep_sem, *sems
     ):
         place = Place(groups, chips)
-        fetches = fetch_all(
-            [(cos_hbm, cos_ref), (sin_low_hbm, sin_low_ref), (sin_high_hbm, sin_high_ref)], load
-        )
         line, one, two, three = split_refs(sems, Gather.SEMS, 2, 2, 2)
         gather = Gather(place, full, line, kept, keep_sem)
         normed, _, _ = layer_norm_parts(
@@ -620,20 +599,37 @@
                         rope_tile(
                             result[:, t * tile : (t + 1) * tile],
                             cos_ref[here, :],
-                            sin_low_ref[here, :],
-                            sin_high_ref[here, :],
+                            sin_ref[here, :],
                             1.0,
                         )
                         for t in range(out_width // tile)
                     ]
                     result = jnp.concatenate(parts, axis=1) if len(parts) > 1 else parts[0]
-                ref[here, :] = result.astype(LOW)
-
+                result = result.astype(LOW)
+                ref[here, :] = result
+                if number > 0:
+                    (k_turned, v_turned)[number - 1][:, here] = result.T
+
+        segment = segment_ref[...]
+        start = jnp.zeros_like(segment)
+        for number in range(1, DOCUMENTS):
+            before = jnp.sum(jnp.where(segment < number, 1, 0), axis=1, keepdims=True)
+            start = jnp.where(segment == number, before, start)
+        start_ref[...] = start
+        lane = lax.rem(lax.broadcasted_iota(jnp.int32, (1, tile), 1), HD)
+        for block in range(length // BLK):
+            here = slice(block * BLK, (block + 1) * BLK)
+            ids = block * BLK + lax.broadcasted_iota(jnp.int32, (1, BLK), 1)
+            spot = (ids - start[:, here]).astype(jnp.float32)
+            angle = jnp.broadcast_to(spot, (tile, BLK)).T * rate_ref[...]
+            sine = jnp.sin(angle)
+            cos_ref[here, :] = jnp.where(lane < ROT, jnp.cos(angle), 1.0)
+            sin_ref[here, :] = jnp.where(
+                lane < ROT // 2, -sine, jnp.where(lane < ROT, sine, 0.0)
+            )
         gather.pass_on(0)
-        for copy in fetches:
-            copy.wait()
         spread_qkv.wait()
-        weights_keep = pltpu.make_async_copy(weights, weights_kept, load.at[3])
+        weights_keep = pltpu.make_async_copy(weights, weights_kept, load.at[0])
         weights_keep.start()
         gather.wait_chip(place.chip)
         work(place.chip)
@@ -653,7 +649,7 @@
         kernel,
         "gather_project",
         1,
-        (tokens, gain, shift, *shards, bias, *tables),
+        (tokens, gain, shift, *shards, bias, segments, rates),
         [
             shape((length, width)),
             shape((3, width, out_width)),
@@ -662,6 +658,10 @@
             head_shape,
             head_shape,
             head_shape,
+            shape((out_width, length)),
+            shape((out_width, length)),
+            shape((1, length), jnp.int32),
+            *(shape((length, tile), jnp.float32) for _ in range(2)),
         ],
         [
             pltpu.VMEM((length, width), LOW),
@@ -669,21 +669,19 @@
             pltpu.VMEM(qkv_shard.shape, LOW),
             pltpu.VMEM(out_shard.shape, LOW),
             pltpu.VMEM((upper, down_shard.shape[1]), LOW),
-            *(pltpu.VMEM((length, tile), jnp.float32) for _ in range(3)),
-            pltpu.SemaphoreType.DMA((4,)),
+            pltpu.SemaphoreType.DMA((1,)),
             pltpu.SemaphoreType.DMA((chips,)),
         ]
         + Gather.scratch(chips)
         + Spread.scratch(groups) * 3,
         COST_FLOPS,
         in_hbm=(0, 1, 2, 3),
-        from_hbm=(7, 8, 9),
-    )
-
-
-def scatter_heads(groups, chips, qkv, start, weight, tokens, grads, shards):
+    )
+
+
+def scatter_heads(groups, chips, queries, keys, values_turned, start, weight, tokens, grads, shards):
     rows, width = tokens.shape
-    length, head_width = qkv[0].shape
+    length, head_width = queries.shape
     heads = head_width // HD
     pair_shard, down_shard = shards
     upper = down_shard.shape[0] // 2
@@ -691,7 +689,7 @@
     def kernel(
         q_hbm, k_hbm, v_hbm, w_hbm, x_hbm, og_hbm, start_ref, pair_ref, down_ref,
         mid_ref, ctx_ref, lse_ref, kept, pair_whole, down_whole,
-        full, q_ref, k_ref, v_ref, w_ref, x_ref, pair_staged, down_staged,
+        full, q_ref, k_ref, w_ref, x_ref, pair_staged, down_staged,
         load, keep_sem, v_turned, acc, stats, *rest
     ):
         place = Place(groups, chips)
@@ -701,7 +699,7 @@
             [
                 (og_hbm, gather.own()),
                 (k_hbm, k_ref),
-                (v_hbm, v_ref),
+                (v_hbm, v_turned),
                 (q_hbm, q_ref),
                 (w_hbm, w_ref),
                 (x_hbm, x_ref),
@@ -717,9 +715,6 @@
         spread_down.start()
         for copy in fetches[1:5]:
             copy.wait()
-        for part in range(length // BLK):
-            here = slice(part * BLK, (part + 1) * BLK)
-            v_turned[:, here] = v_ref[here, :].T
         masks = head_masks(head_width, LOW)
 
         def work(chip, core):
@@ -738,7 +733,8 @@
                 attend(number, rows, k_ref, v_turned, masked, starts, query_ids, acc, stats)
                 return 0
 
-            lax.fori_loop(jnp.maximum(block - LONGEST // rows, 0), block + 1, step, 0)
+            first = jnp.maximum(block - LONGEST // rows, 0) // 2
+            lax.fori_loop(first, block // 2 + 1, step, 0)
             for h in range(heads):
                 band = slice(h * HD, (h + 1) * HD)
                 acc[band, :] = acc[band, :] / stats[8 + h : 9 + h, :]
@@ -775,7 +771,7 @@
         kernel,
         "scatter_heads",
         2,
-        (*qkv, weight, tokens, grads, start, *shards),
+        (queries, keys, values_turned, weight, tokens, grads, start, *shards),
         [
             shape((rows, width), jnp.float32),
             shape((length, head_width)),
@@ -786,7 +782,7 @@
         ],
         [
             pltpu.VMEM((length, width), LOW),
-            *(pltpu.VMEM((length, head_width), LOW) for _ in range(3)),
+            *(pltpu.VMEM((length, head_width), LOW) for _ in range(2)),
             pltpu.VMEM((head_width, width), LOW),
             pltpu.VMEM((rows, width), LOW),
             pltpu.VMEM(pair_shard.shape, LOW),
@@ -974,7 +970,8 @@
 
 
 def gather_context(
-    groups, chips, middle, normed_grad, out_grad, gain, shift, weight, hidden_low, down_parts, normed, pair
+    groups, chips, middle, normed_grad, out_grad, gain, shift, weight, context, hidden_low, down_parts,
+    normed, pair
 ):
     rows, width = middle.shape
     length = rows * 2 * chips
@@ -984,10 +981,10 @@
     part = width // groups
 
     def kernel(
-        mid_ref, ng_hbm, og_ref, gain_ref, shift_ref, w_hbm, hid_hbm, down_one, down_two,
+        mid_ref, ng_hbm, og_ref, gain_ref, shift_ref, w_hbm, ctx_hbm, hid_hbm, down_one, down_two,
         a_ref, gg_hbm, ug_hbm,
-        kept, cg_ref, mg_ref, sums_ref, out_ref, landed,
-        full, total, w_ref, hid_ref, down_ref, gg_ref, ug_ref, staged, columns_in, load, keep_sem, *rest
+        kept, cg_ref, mg_ref, sums_ref, out_ref, landed, delta_ref,
+        full, total, w_ref, ctx_ref, hid_ref, down_ref, gg_ref, ug_ref, staged, columns_in, load, keep_sem, *rest
     ):
         place = Place(groups, chips)
         scratch, line, sems = split_refs(rest, Scatter.SCRATCH, Gather.SEMS, 2)
@@ -1008,6 +1005,7 @@
                     (down_two, down_ref.at[upper:hidden]),
                     (hid_hbm, hid_ref),
                     (w_hbm, w_ref),
+                    (ctx_hbm, ctx_ref),
                     (gg_hbm, gg_ref),
                     (ug_hbm, ug_ref),
                 )
@@ -1030,9 +1028,19 @@
         sums_ref[0:1, :] = gain_grad[None, :]
         sums_ref[1:2, :] = shift_grad[None, :]
 
+        select = (
+            lax.broadcasted_iota(jnp.int32, (8, out_width), 1) // HD
+            == lax.broadcasted_iota(jnp.int32, (8, out_width), 0)
+        ).astype(LOW)
+
         def back_work(chip):
             here = pl.ds(pl.multiple_of(chip * 2 * rows, 2 * rows), 2 * rows)
-            cg_ref[here, :] = dot(full[here, :], w_ref[...], NT).astype(LOW)
+            context_grad = dot(full[here, :], w_ref[...], NT).astype(LOW)
+            cg_ref[here, :] = context_grad
+            product = context_grad.astype(jnp.float32) * ctx_ref[here, :].astype(jnp.float32)
+            upper_bits = product.astype(LOW)
+            lower_bits = (product - upper_bits.astype(jnp.float32)).astype(LOW)
+            delta_ref[:, here] = dot(select, upper_bits, NT) + dot(select, lower_bits, NT)
 
         def out_work(chip, core):
             here = pl.ds(pl.multiple_of((chip * 2 + core) * rows, rows), rows)
@@ -1085,7 +1093,7 @@
         kernel,
         "gather_context",
         5,
-        (middle, normed_grad, out_grad, gain, shift, weight, hidden_low, *down_parts, normed, *pair),
+        (middle, normed_grad, out_grad, gain, shift, weight, context, hidden_low, *down_parts, normed, *pair),
         [
             shape((length, width)),
             shape((length, out_width)),
@@ -1093,18 +1101,20 @@
             shape((2, width), jnp.float32),
             shape((rows, width)),
             shape((groups, 2, hidden, part)),
+            shape((8, length), jnp.float32),
         ],
         [
             pltpu.VMEM((length, width), LOW),
             pltpu.VMEM((rows, width), jnp.float32),
             pltpu.VMEM(weight.shape, LOW),
+            pltpu.VMEM((length, out_width), LOW),
             pltpu.VMEM((length, hidden), LOW),
             pltpu.VMEM((hidden, width), LOW),
             pltpu.VMEM((length, hidden), LOW),
             pltpu.VMEM((length, hidden), LOW),
             pltpu.VMEM((groups, 2, hidden, part), LOW),
             pltpu.VMEM((2, length, part), LOW),
-            pltpu.SemaphoreType.DMA((10,)),
+            pltpu.SemaphoreType.DMA((11,)),
             pltpu.SemaphoreType.DMA((chips,)),
         ]
         + Scatter.scratch(chips, rows, width)
@@ -1112,7 +1122,7 @@
         + Spread.scratch(groups),
         COST_FLOPS,
         in_hbm=(0, 2, 5),
-        from_hbm=(1, 5, 6, 7, 8, 9, 10, 11),
+        from_hbm=(1, 5, 6, 7, 8, 9, 10, 11, 12),
     )
 
 
@@ -1127,7 +1137,7 @@
 
 
 def scatter_triple(
-    groups, chips, qkv, start, lse, context, context_grad, tables, weights, tokens, gain, shift,
+    groups, chips, qkv, keys_turned, start, lse, delta, context, context_grad, tables, weights, tokens, gain, shift,
     mid_grad, sums, normed, grads
 ):
     length, in_width = qkv[0].shape
@@ -1139,14 +1149,14 @@
     reach = LONGEST // rows
 
     def kernel(
-        start_ref, lse_ref, gain_ref, shift_ref, sums_ref,
-        q_hbm, k_hbm, v_hbm, cg_hbm, ctx_hbm, cos_hbm, sin_low_hbm, sin_high_hbm,
+        start_ref, lse_ref, delta, gain_ref, shift_ref, sums_ref,
+        q_hbm, k_hbm, v_hbm, turned_hbm, cg_hbm, ctx_hbm, cos_hbm, sin_hbm,
         w_hbm, x_hbm, mg_hbm, a_hbm, full_hbm,
         in_ref, small_ref, landed_qkv, landed_out,
-        q_ref, k_ref, v_ref, cg_ref, ctx_ref, cos_ref, sin_low_ref, sin_high_ref,
+        q_ref, k_ref, v_ref, cg_ref, ctx_ref, cos_ref, sin_ref,
         w_ref, x_ref, mg_ref, columns_in, load, load_columns,
-        k_turned, dq_acc, dk_acc, dv_acc, delta, dq_ref, dk_ref, dv_ref, bias,
-        total, staged_qkv, staged_out, early_spots, early_groups, late_spots, late_groups, *rest
+        k_turned, dq_acc, dk_acc, dv_acc, dq_ref, dk_ref, dv_ref, bias,
+        total, norm_sums, staged_qkv, staged_out, early_spots, early_groups, late_spots, late_groups, *rest
     ):
         place = Place(groups, chips)
         scratch, one, two, sums_sems = split_refs(rest, Scatter.SCRATCH, 2, 2, 8)
@@ -1156,11 +1166,11 @@
                 (q_hbm, q_ref),
                 (v_hbm, v_ref),
                 (cg_hbm, cg_ref),
+                (turned_hbm, k_turned),
+                (cos_hbm, cos_ref),
+                (sin_hbm, sin_ref),
+                (w_hbm, w_ref),
                 (ctx_hbm, ctx_ref),
-                (cos_hbm, cos_ref),
-                (sin_low_hbm, sin_low_ref),
-                (sin_high_hbm, sin_high_ref),
-                (w_hbm, w_ref),
                 (x_hbm, x_ref),
                 (mg_hbm, mg_ref),
             ],
@@ -1170,59 +1180,51 @@
         dk_acc[...] = jnp.zeros_like(dk_acc)
         dv_acc[...] = jnp.zeros_like(dv_acc)
         bias[...] = jnp.zeros_like(bias)
-        place.barrier(True, True)
         spots, count = place.spot, 2 * chips
         early_a = SmallSum(early_spots, spots, count, place.fellow, sums_sems[0:2])
         early_b = SmallSum(early_groups, place.group, groups, place.peer, sums_sems[2:4])
         late_a = SmallSum(late_spots, spots, count, place.fellow, sums_sems[4:6])
         late_b = SmallSum(late_groups, place.group, groups, place.peer, sums_sems[6:8])
-        for copy in fetches[:9]:
+        for copy in fetches[:8]:
             copy.wait()
+        place.barrier(True, True)
         masks = head_masks(in_width, LOW)
-        select = (
-            lax.broadcasted_iota(jnp.int32, (8, in_width), 1) // HD
-            == lax.broadcasted_iota(jnp.int32, (8, in_width), 0)
-        ).astype(jnp.float32)
-
-        def set_up(block):
-            here = pl.ds(pl.multiple_of(block * rows, rows), rows)
-            k_turned[:, here] = k_ref[here, :].T
-            product = cg_ref[here, :].astype(jnp.float32) * ctx_ref[here, :].astype(jnp.float32)
-            delta[:, here] = dot(select, product, NT, lax.Precision.HIGHEST)
-
-        each(2 * chips, set_up)
-
-        def attend_back(query_block, key_block):
+        def attend_back(query_block, key_chip):
             base_q = pl.multiple_of(query_block * rows, rows)
-            base_k = pl.multiple_of(key_block * rows, rows)
-            rows_q, rows_k = pl.ds(base_q, rows), pl.ds(base_k, rows)
+            base_k = pl.multiple_of(key_chip * 2 * rows, 2 * rows)
+            rows_q, rows_k = pl.ds(base_q, rows), pl.ds(base_k, 2 * rows)
             queries = (q_ref[rows_q, :] * 0.125).astype(LOW)
             incoming = cg_ref[rows_q, :]
             keys, vals = k_ref[rows_k, :], v_ref[rows_k, :]
-            key_ids = base_k + lax.broadcasted_iota(jnp.int32, (rows, rows), 0)
+            key_ids = base_k + lax.broadcasted_iota(jnp.int32, (2 * rows, rows), 0)
             query_ids = base_q + lax.broadcasted_iota(jnp.int32, (1, rows), 1)
             visible = (key_ids >= start_ref[:, rows_q]) & (key_ids <= query_ids)
-            dk, dv = dk_acc[rows_k, :], dv_acc[rows_k, :]
+            probs, dscores, all_queries, all_incoming = [], [], [], []
             for h in range(heads):
                 masked, incoming_masked = queries * masks[h], incoming * masks[h]
                 scores = dot(keys, masked, NT)
                 prob = jnp.where(visible, jnp.exp(scores - lse_ref[h : h + 1, rows_q]), 0.0)
                 dprob = dot(vals, incoming_masked, NT)
                 dscore = (prob * (dprob - delta[h : h + 1, rows_q])).astype(LOW)
-                dv = dv + dot(prob.astype(LOW), incoming_masked)
-                dk = dk + dot(dscore, masked)
                 band = slice(h * HD, (h + 1) * HD)
                 dq_acc[band, rows_q] += dot(k_turned[band, rows_k], dscore)
-            dk_acc[rows_k, :] = dk
-            dv_acc[rows_k, :] = dv
+                probs.append(prob.astype(LOW))
+                dscores.append(dscore)
+                all_queries.append(masked)
+                all_incoming.append(incoming_masked)
+            dv_acc[rows_k, :] += dot(
+                jnp.concatenate(probs, axis=1), jnp.concatenate(all_incoming, axis=0)
+            )
+            dk_acc[rows_k, :] += dot(
+                jnp.concatenate(dscores, axis=1), jnp.concatenate(all_queries, axis=0)
+            )
 
         def turn_back(values, here):
             parts = [
                 rope_tile(
                     values[:, t * tile : (t + 1) * tile],
                     cos_ref[here, :],
-                    sin_low_ref[here, :],
-                    sin_high_ref[here, :],
+                    sin_ref[here, :],
                     -1.0,
                 )
                 for t in range(in_width // tile)
@@ -1241,13 +1243,12 @@
                 @pl.when(done == 0)
                 def _():
                     def one(number):
-                        query_block = upper * 2 + number // 2
-                        key_block = lower * 2 + number % 2
-                        pl.when(
-                            (key_block <= query_block) & (query_block - key_block <= reach)
-                        )(lambda: attend_back(query_block, key_block))
-
-                    each(4, one)
+                        query_block = upper * 2 + number
+                        pl.when(query_block - (lower * 2 + 1) <= reach)(
+                            lambda: attend_back(query_block, lower)
+                        )
+
+                    each(2, one)
 
             each(chips, with_chip)
 
@@ -1308,30 +1309,44 @@
         scatter = PreparedScatter(place, work, scratch, prepare)
         scatter.first()
 
+        def fills():
+            each(groups, fill_qkv)
+
         def step(number):
-            scatter.slot(number)
+            scatter.slot(number, fills)
 
             @pl.when(number == 0)
             def _():
                 early_a.begin(sums_ref[...])
-                for copy in fetches[9:]:
+                for copy in fetches[8:]:
                     copy.wait()
                 each(groups, fill_out)
 
         each(chips - 1, step)
         scatter.last()
-        each(groups, fill_qkv)
+        pl.when(scatter.lag == 0)(fills)
         early_groups[place.group] = jnp.zeros(early_groups.shape[1:], jnp.float32)
         early_groups[place.group, 4:7, 0:in_width] = bias[0:3, :]
         early_groups[place.group, 0:2, :] = early_a.result()
         early_b.begin(early_groups[place.group])
-        _, plain, inverse = layer_norm_parts(
-            x_ref[...].astype(jnp.float32), gain_ref[...], shift_ref[...]
-        )
         scatter.own(total)
-        back, gain_grad, shift_grad = layer_norm_back(total[...], plain, inverse, gain_ref[...])
-        late_a.begin(jnp.concatenate([gain_grad[None, :], shift_grad[None, :]], axis=0))
-        in_ref[...] = (mg_ref[...] + back).astype(LOW)
+        size = rows // 4
+        norm_sums[...] = jnp.zeros_like(norm_sums)
+
+        def norm_back(block):
+            here = pl.ds(pl.multiple_of(block * size, size), size)
+            _, plain, inverse = layer_norm_parts(
+                x_ref[here, :].astype(jnp.float32), gain_ref[...], shift_ref[...]
+            )
+            back, gain_grad, shift_grad = layer_norm_back(
+                total[here, :], plain, inverse, gain_ref[...]
+            )
+            in_ref[here, :] = (mg_ref[here, :] + back).astype(LOW)
+            norm_sums[0:1, :] += gain_grad[None, :]
+            norm_sums[1:2, :] += shift_grad[None, :]
+
+        each(4, norm_back)
+        late_a.begin(norm_sums[...])
         scatter.drain()
         late_b.begin(late_a.result())
         first = early_b.result()
@@ -1352,8 +1367,8 @@
         "scatter_triple",
         6,
         (
-            start, lse, gain, shift, sums,
-            *qkv, context_grad, context, *tables, weights, tokens, mid_grad, normed, grads,
+            start, lse, delta, gain, shift, sums,
+            *qkv, keys_turned, context_grad, context, *tables, weights, tokens, mid_grad, normed, grads,
         ),
         [
             shape((rows, width)),
@@ -1363,7 +1378,7 @@
         ],
         [
             *(heads_kind for _ in range(5)),
-            *(pltpu.VMEM((length, tile), jnp.float32) for _ in range(3)),
+            *(pltpu.VMEM((length, tile), jnp.float32) for _ in range(2)),
             pltpu.VMEM(weights.shape, LOW),
             pltpu.VMEM((rows, width), LOW),
             pltpu.VMEM((rows, width), jnp.float32),
@@ -1374,12 +1389,12 @@
             pltpu.VMEM((in_width, length), jnp.float32),
             heads_sum,
             heads_sum,
-            pltpu.VMEM((8, length), jnp.float32),
             heads_kind,
             heads_kind,
             heads_kind,
             pltpu.VMEM((8, in_width), jnp.float32),
             pltpu.VMEM((rows, width), jnp.float32),
+            pltpu.VMEM((2, width), jnp.float32),
             pltpu.VMEM((groups, 3, part, in_width), LOW),
             pltpu.VMEM((groups, in_width, part), LOW),
             pltpu.VMEM((devices, 2, width), jnp.float32),
@@ -1392,7 +1407,7 @@
         + [pltpu.SemaphoreType.DMA((n,)) for n in (devices, devices, groups, groups) * 2],
         COST_FLOPS,
         in_hbm=(2, 3),
-        from_hbm=tuple(range(5, 18)),
+        from_hbm=tuple(range(6, 19)),
     )
 
 
@@ -1431,17 +1446,16 @@
     second_gain,
     second_shift,
 ):
-    length = segments.shape[1]
     head_width = w_qkv.shape[2]
     gains = (norm_gain[0:1], norm_gain[1:2])
     shifts = (norm_bias[0:1], norm_bias[1:2])
-    place = positions(segments)[0]
-    start = jnp.arange(length, dtype=jnp.int32) - place
-    start = start[None, :]
-    tables = rotary_tables(place, min(head_width, 128))
+    half = jnp.arange(ROT // 2, dtype=jnp.float32)
+    rates = 10000.0 ** (-(2.0 * half) / ROT)
+    rates = jnp.concatenate([rates, rates, jnp.zeros((HD - ROT,), jnp.float32)])
+    rates = jnp.tile(rates, min(head_width, 128) // HD)[None, :]
 
     gate_up_turned = jnp.swapaxes(w_gate_up, 1, 2)
-    normed_one_all, qkv_all, out_all, down_one, *qkv = gather_project(
+    normed_one_all, qkv_all, out_all, down_one, *rest = gather_project(
         groups,
         chips,
         inputs,
@@ -1449,16 +1463,27 @@
         shifts[0],
         (w_qkv, w_out, w_down),
         qkv_bias,
-        tables,
-    )
+        segments,
+        rates,
+    )
+    qkv, (keys_turned, values_turned, start), tables = rest[:3], rest[3:6], rest[6:]
     middle, context_flat, lse, mlp_grad, pair_all, down_two = scatter_heads(
-        groups, chips, qkv, start, out_all, inputs, out_grad, (gate_up_turned, w_down)
+        groups,
+        chips,
+        qkv[0],
+        qkv[1],
+        values_turned,
+        start,
+        out_all,
+        inputs,
+        out_grad,
+        (gate_up_turned, w_down),
     )
     down_parts = (down_one, down_two)
     normed_two_all, hidden_low, gate_grad, up_grad, normed_two_grad, parts_down = hidden_layers(
         groups, chips, middle, gains[1], shifts[1], pair_all, down_parts, mlp_grad
     )
-    attn_grad_all, context_grad, middle_grad, sums_two, outputs, parts_pair = (
+    attn_grad_all, context_grad, middle_grad, sums_two, outputs, parts_pair, delta = (
         gather_context(
             groups,
             chips,
@@ -1468,6 +1493,7 @@
             gains[1],
             shifts[1],
             out_all,
+            context_flat,
             hidden_low,
             down_parts,
             normed_two_all,
@@ -1478,8 +1504,10 @@
         groups,
         chips,
         qkv,
+        keys_turned,
         start,
         lse,
+        delta,
         context_flat,
         context_grad,
         tables,

time: 578 us -> 569 us (0.984)
  the two profiles are of different devices: /device:TPU:10 before, /device:TPU:0 now
where the time goes in v6:
time: 569 us; the launch traced here: 560 us
  Pallas kernels  529 us (93%)
  other arithmetic  20.9 us (4%)
  local copies, waits for them, and re-layouts  8.07 us (1%)
    pallas_call x5, Pallas kernels, line_call(): pl.pallas_call(kernel, out_shape=out_shape, in_specs=ins, out_specs=outs,...  529 us
    sub x6, other arithmetic, adam_update(): return (master - rate * change, one_new, two_new)  20.8 us

profile of v6, /device:TPU:0, one launch (start us, length us, event | category | flops | bytes accessed | tf_op | source)
XLA Modules:
  0.0 559.5 jit_solution(10498481033409542699)
XLA Ops:
  0.7 0.1 pad_maximum_fusion
  0.8 0.6 broadcast_in_dim_tile.3.rate_ref
  1.4 1.4 fusion.14
  2.8 82.7 %gather_project.1 = (bf16[2048,2048]{1,0:T(8,128)(2,1)}, bf16[3,2048,256]{2,1,0:T(8,128)(2,1)}, bf16[256,2048]{1,0:T(8,128)(2,1)}, bf16[352,2048]{1,0:T(8,128)(2...) custom-call(bf16[256,2048]{1,0:T(8,128)(2,1)} %x_hbm.3, ...), custom_call_target="tpu_custom_call" | custom-call | flops 80000000000 | tf_op jit(solution)/shard_map/gather_project/pallas_call | solution.py:532
  85.5 103.1 %scatter_heads.1 = (f32[256,2048]{1,0:T(8,128)}, bf16[2048,256]{1,0:T(8,128)(2,1)}, f32[8,2048]{1,0:T(8,128)}, bf16[2048,2048]{1,0:T(8,128)(2,1)}, bf16[2,704,20...) custom-call(bf16[2048,256]{1,0:T(8,128)(2,1)} %get-tuple-element.65.q_hbm, bf16[2048,256]{1,0:T(8,128)(2,1)} %get-tuple-element.66.k_hbm, ...), custom_call_target="tpu_custom_call" | custom-call | flops 80000000000 | tf_op jit(solution)/shard_map/scatter_heads/pallas_call | solution.py:532
  188.6 130.2 %gather_hidden.1 = (bf16[2048,2048]{1,0:T(8,128)(2,1)}, bf16[2048,704]{1,0:T(8,128)(2,1)}, bf16[2048,704]{1,0:T(8,128)(2,1)}, bf16[2048,704]{1,0:T(8,128)(2,1)},...) custom-call(f32[1,2048]{1,0:T(1,128)} %get-tuple-element.137.gain_ref, f32[1,2048]{1,0:T(1,128)} %get-tuple-element.132.shift_ref, ...), custom_call_target="tpu_custom_call" | custom-call | flops 80000000000 | tf_op jit(solution)/shard_map/gather_hidden/pallas_call | solution.py:532
  318.8 101.3 %gather_context.1 = (bf16[2048,2048]{1,0:T(8,128)(2,1)}, bf16[2048,256]{1,0:T(8,128)(2,1)}, f32[256,2048]{1,0:T(8,128)}, f32[2,2048]{1,0:T(2,128)}, bf16[256,204...) custom-call(f32[256,2048]{1,0:T(8,128)} %get-tuple-element.70.mid_hbm.mid_ref, ...), custom_call_target="tpu_custom_call" | custom-call | flops 80000000000 | tf_op jit(solution)/shard_map/gather_context/pallas_call | solution.py:532
  420.1 0.0 copy-start.17
  420.1 0.0 copy-start.18
  420.1 0.0 copy-start.19
  420.1 0.0 copy-start.11
  420.1 0.0 copy-start.12
  420.1 0.0 copy-start.13
  420.2 0.0 copy-start.14
  420.2 0.0 copy-start.15
  420.2 0.0 copy-start.16
  420.2 112.0 %scatter_triple.1 = (bf16[256,2048]{1,0:T(8,128)(2,1)}, f32[8,2048]{1,0:T(8,128)}, bf16[4,3,512,256]{3,2,1,0:T(8,128)(2,1)}, bf16[4,256,512]{2,1,0:T(8,128)(2,1)}) custom-call(s32[1,2048]{1,0:T(1,128)} %get-tuple-element.69.start_ref, f32[8,2048]{1,0:T(8,128)} %get-tuple-element.82.lse_ref, f32[8,2048]{1,0:T(8,128)} %get-tuple-element.83.delta, ...), custom_call_target="tpu_custom_call" | custom-call | flops 80000000000 | tf_op jit(solution)/shard_map/scatter_triple/pallas_call | solution.py:532
  532.2 0.0 copy-done.17
  532.2 0.0 copy-done.18
  532.2 0.0 copy-done.19
  532.2 1.3 multiply_subtract_fusion.6
  533.5 0.0 copy-done.11
  533.5 0.0 copy-done.12
  533.5 0.0 copy-done.13
  533.5 0.0 copy-done.14
  533.6 0.0 copy-done.15
  533.6 0.0 copy-done.16
  533.6 1.7 multiply_subtract_fusion.4
  535.2 0.0 copy-start.4
  535.2 0.0 copy-start.8
  535.2 3.3 multiply_subtract_fusion.3
  538.6 0.0 copy-done.4
  538.6 0.0 copy-done.8
  538.6 0.0 copy-start
  538.6 0.0 copy-start.5
  538.6 0.0 copy-start.6
  538.6 0.0 copy-start.7
  538.6 0.0 copy-start.3
  538.6 5.5 multiply_subtract_fusion.2
  544.1 0.0 slice-start
  544.1 0.0 copy-done
  544.1 0.0 copy-done.5
  544.1 0.0 copy-done.6
  544.1 0.0 copy-done.7
  544.1 0.0 slice-start.1
  544.2 0.0 copy-start.1
  544.2 0.0 copy-start.2
  544.2 3.7 multiply_subtract_fusion.1
  547.9 0.0 copy-done.3
  547.9 1.3 slice-done
  549.1 0.4 slice-done.1
  549.5 0.9 copy-done.1
  550.4 0.8 copy-done.2
  551.2 0.0 copy-start.9
  551.2 5.3 multiply_subtract_fusion
  556.6 0.0 copy-start.10
  556.6 0.0 copy-done.9
  556.6 1.0 copy.56
  557.5 0.6 copy-done.10
  558.2 1.0 copy.57
  (4 shorter events, 0.0 us)
Async XLA Ops:
  420.1 112.1 %copy-start.17 = (f32[3,256]{1,0:T(4,128)S(1)}, f32[3,256]{1,0:T(4,128)}, u32[]{:S(2)}) copy-start(f32[3,256]{1,0:T(4,128)} %bias_ref.1) | copy-start | bytes 9220
  420.1 112.1 %copy-start.18 = (f32[3,256]{1,0:T(4,128)S(1)}, f32[3,256]{1,0:T(4,128)}, u32[]{:S(2)}) copy-start(f32[3,256]{1,0:T(4,128)} %param.38) | copy-start | bytes 9220
  420.1 112.1 %copy-start.19 = (f32[3,256]{1,0:T(4,128)S(1)}, f32[3,256]{1,0:T(4,128)}, u32[]{:S(2)}) copy-start(f32[3,256]{1,0:T(4,128)} %param.45) | copy-start | bytes 9220
  420.1 113.4 %copy-start.11 = (f32[2,2048]{1,0:T(2,128)S(1)}, f32[2,2048]{1,0:T(2,128)}, u32[]{:S(2)}) copy-start(f32[2,2048]{1,0:T(2,128)} %param.33) | copy-start | bytes 49156
  420.1 113.4 %copy-start.12 = (f32[2,2048]{1,0:T(2,128)S(1)}, f32[2,2048]{1,0:T(2,128)}, u32[]{:S(2)}) copy-start(f32[2,2048]{1,0:T(2,128)} %param.32) | copy-start | bytes 49156
  420.1 113.4 %copy-start.13 = (f32[2,2048]{1,0:T(2,128)S(1)}, f32[2,2048]{1,0:T(2,128)}, u32[]{:S(2)}) copy-start(f32[2,2048]{1,0:T(2,128)} %param.40) | copy-start | bytes 49156
  420.2 113.4 %copy-start.14 = (f32[2,2048]{1,0:T(2,128)S(1)}, f32[2,2048]{1,0:T(2,128)}, u32[]{:S(2)}) copy-start(f32[2,2048]{1,0:T(2,128)} %param.47) | copy-start | bytes 49156
  420.2 113.4 %copy-start.15 = (f32[2,2048]{1,0:T(2,128)S(1)}, f32[2,2048]{1,0:T(2,128)}, u32[]{:S(2)}) copy-start(f32[2,2048]{1,0:T(2,128)} %param.46) | copy-start | bytes 49156
  420.2 113.4 %copy-start.16 = (f32[2,2048]{1,0:T(2,128)S(1)}, f32[2,2048]{1,0:T(2,128)}, u32[]{:S(2)}) copy-start(f32[2,2048]{1,0:T(2,128)} %param.39) | copy-start | bytes 49156
  535.2 3.3 copy-start.4
  535.2 3.3 copy-start.8
  538.6 5.5 copy-start
  538.6 5.5 copy-start.5
  538.6 5.5 copy-start.6
  538.6 5.5 copy-start.7
  538.6 9.2 %copy-start.3 = (f32[2,512,704]{1,2,0:T(8,128)S(1)}, f32[2,512,704]{1,2,0:T(8,128)}, u32[]{:S(2)}) copy-start(f32[2,512,704]{1,2,0:T(8,128)} %param.43) | copy-start | bytes 8650756
  544.1 5.0 slice-start
  544.1 5.4 slice-start.1
  544.2 6.2 %copy-start.1 = (f32[2,512,704]{1,2,0:T(8,128)S(1)}, f32[2,512,704]{1,2,0:T(8,128)}, u32[]{:S(2)}) copy-start(f32[2,512,704]{1,2,0:T(8,128)} %param.29) | copy-start | bytes 8650756
  544.2 7.1 %copy-start.2 = (f32[2,512,704]{1,2,0:T(8,128)S(1)}, f32[2,512,704]{1,2,0:T(8,128)}, u32[]{:S(2)}) copy-start(f32[2,512,704]{1,2,0:T(8,128)} %param.36) | copy-start | bytes 8650756
  551.2 5.4 copy-start.9
  556.6 1.6 copy-start.10

commit v7 on v6

--- a/solution.py
+++ b/solution.py
@@ -111,7 +111,7 @@
     def fellow(self, offset):
         return (self.group, lax.rem(self.spot + offset, 2 * self.chips))
 
-    def barrier(self, with_groups=False, with_all_spots=False):
+    def greet(self, with_groups=False, with_all_spots=False):
         semaphore = pltpu.get_barrier_semaphore()
 
         def greet(target):
@@ -130,7 +130,10 @@
             for offset in range(1, self.groups):
                 greet(self.peer(offset))
             count = count + self.groups - 1
-        pl.semaphore_wait(semaphore, count)
+        self.awaited = count
+
+    def meet(self):
+        pl.semaphore_wait(pltpu.get_barrier_semaphore(), self.awaited)
 
 
 def each(count, use):
@@ -573,15 +576,21 @@
         full, weights, qkv_staged, out_staged, down_staged, load, keep_sem, *sems
     ):
         place = Place(groups, chips)
+        place.greet(True)
         line, one, two, three = split_refs(sems, Gather.SEMS, 2, 2, 2)
         gather = Gather(place, full, line, kept, keep_sem)
-        normed, _, _ = layer_norm_parts(
-            x_ref[...].astype(jnp.float32), gain_ref[...], shift_ref[...]
-        )
-        gather.own()[...] = normed.astype(LOW)
+        size = rows // HALVES
+        for half in range(HALVES):
+            normed, _, _ = layer_norm_parts(
+                x_ref[half * size : (half + 1) * size, :].astype(jnp.float32),
+                gain_ref[...],
+                shift_ref[...],
+            )
+            gather.block(place.chip, place.core, half)[...] = normed.astype(LOW)
+            if half == 0:
+                place.meet()
+            gather.begin((half,))
         spread_qkv = Spread(place, qkv_ref, qkv_staged, weights, 1, one)
-        place.barrier(True)
-        gather.begin()
         spread_qkv.start()
         spread_out = Spread(place, out_ref, out_staged, out_whole, 1, two)
         spread_out.start()
@@ -693,6 +702,7 @@
         load, keep_sem, v_turned, acc, stats, *rest
     ):
         place = Place(groups, chips)
+        place.greet(True)
         scratch, line, one, two = split_refs(rest, Scatter.SCRATCH, Gather.SEMS, 2, 2)
         gather = Gather(place, full, line, kept, keep_sem)
         fetches = fetch_all(
@@ -706,8 +716,8 @@
             ],
             load,
         )
-        place.barrier(True)
         fetches[0].wait()
+        place.meet()
         gather.begin()
         spread_pair = Spread(place, pair_ref, pair_staged, pair_whole, 2, one)
         spread_pair.start()
@@ -816,6 +826,7 @@
         full, og_ref, pair_ref, down_ref, hid_ref, held, staged, mine, load, keep_sem, store_sem, *rest
     ):
         place = Place(groups, chips)
+        place.greet(True)
         first, second, line, sems = split_refs(rest, Scatter.SCRATCH, Scatter.SCRATCH, Gather.SEMS, 2)
         fetches = fetch_all(
             [
@@ -834,11 +845,15 @@
         ]
         exchange = Exchange(place, staged, landed, sems)
         fetches[0].wait()
-        normed, _, _ = layer_norm_parts(sum_ref[...], gain_ref[...], shift_ref[...])
-        gather.own()[...] = normed.astype(LOW)
-        place.barrier(True)
         at_end = (place.chip == 0) | (place.chip == chips - 1)
-        gather.begin((0,))
+        for half in range(HALVES):
+            normed, _, _ = layer_norm_parts(
+                sum_ref[half * size : (half + 1) * size, :], gain_ref[...], shift_ref[...]
+            )
+            gather.block(place.chip, place.core, half)[...] = normed.astype(LOW)
+            if half == 0:
+                place.meet()
+                gather.begin((0,))
         pl.when(at_end)(lambda: gather.begin((1,)))
         for copy in fetches[1:]:
             copy.wait()
@@ -987,6 +1002,7 @@
         full, total, w_ref, ctx_ref, hid_ref, down_ref, gg_ref, ug_ref, staged, columns_in, load, keep_sem, *rest
     ):
         place = Place(groups, chips)
+        place.greet(True)
         scratch, line, sems = split_refs(rest, Scatter.SCRATCH, Gather.SEMS, 2)
 
         def fetch(offset):
@@ -1015,18 +1031,27 @@
             copy.start()
         fetch(1).start()
         gather = Gather(place, full, line, kept, keep_sem)
-        _, plain, inverse = layer_norm_parts(mid_ref[...], gain_ref[...], shift_ref[...])
         arrive.wait()
-        back, gain_grad, shift_grad = layer_norm_back(total[...], plain, inverse, gain_ref[...])
-        mid_grad = og_ref[...].astype(jnp.float32) + back
-        total[...] = mid_grad
+        size = rows // HALVES
+        for half in range(HALVES):
+            here = slice(half * size, (half + 1) * size)
+            _, plain, inverse = layer_norm_parts(mid_ref[here, :], gain_ref[...], shift_ref[...])
+            back, gain_grad, shift_grad = layer_norm_back(
+                total[here, :], plain, inverse, gain_ref[...]
+            )
+            mid_grad = og_ref[here, :].astype(jnp.float32) + back
+            total[here, :] = mid_grad
+            gather.block(place.chip, place.core, half)[...] = mid_grad.astype(LOW)
+            if half == 0:
+                place.meet()
+                sums_ref[0:1, :] = gain_grad[None, :]
+                sums_ref[1:2, :] = shift_grad[None, :]
+            else:
+                sums_ref[0:1, :] += gain_grad[None, :]
+                sums_ref[1:2, :] += shift_grad[None, :]
+            gather.begin((half,))
         keep = pltpu.make_async_copy(total, mg_ref, load.at[2])
         keep.start()
-        gather.own()[...] = mid_grad.astype(LOW)
-        place.barrier(True)
-        gather.begin()
-        sums_ref[0:1, :] = gain_grad[None, :]
-        sums_ref[1:2, :] = shift_grad[None, :]
 
         select = (
             lax.broadcasted_iota(jnp.int32, (8, out_width), 1) // HD
@@ -1159,6 +1184,7 @@
         total, norm_sums, staged_qkv, staged_out, early_spots, early_groups, late_spots, late_groups, *rest
     ):
         place = Place(groups, chips)
+        place.greet(True, True)
         scratch, one, two, sums_sems = split_refs(rest, Scatter.SCRATCH, 2, 2, 8)
         fetches = fetch_all(
             [
@@ -1187,7 +1213,7 @@
         late_b = SmallSum(late_groups, place.group, groups, place.peer, sums_sems[6:8])
         for copy in fetches[:8]:
             copy.wait()
-        place.barrier(True, True)
+        place.meet()
         masks = head_masks(in_width, LOW)
         def attend_back(query_block, key_chip):
             base_q = pl.multiple_of(query_block * rows, rows)

time: 569 us -> 562 us (0.988)
  Pallas kernels: 529 us -> 522 us
    pallas_call x5, Pallas kernels: 529 us -> 522 us  [line_call(): pl.pallas_call(kernel, out_shape=out_shape, in_specs=ins, out_specs=outs,...]
where the time goes in v7:
time: 562 us; the launch traced here: 552 us
  Pallas kernels  522 us (93%)
  other arithmetic  20.9 us (4%)
  local copies, waits for them, and re-layouts  8.07 us (1%)
    pallas_call x5, Pallas kernels, line_call(): pl.pallas_call(kernel, out_shape=out_shape, in_specs=ins, out_specs=outs,...  522 us
    sub x6, other arithmetic, adam_update(): return (master - rate * change, one_new, two_new)  20.8 us

profile of v7, /device:TPU:0, one launch (start us, length us, event | category | flops | bytes accessed | tf_op | source)
XLA Modules:
  0.0 552.1 jit_solution(7262883579258154271)
XLA Ops:
  0.7 0.1 pad_maximum_fusion
  0.8 0.6 broadcast_in_dim_tile.3.rate_ref
  1.4 1.4 fusion.14
  2.8 81.8 %gather_project.1 = (bf16[2048,2048]{1,0:T(8,128)(2,1)}, bf16[3,2048,256]{2,1,0:T(8,128)(2,1)}, bf16[256,2048]{1,0:T(8,128)(2,1)}, bf16[352,2048]{1,0:T(8,128)(2...) custom-call(bf16[256,2048]{1,0:T(8,128)(2,1)} %x_hbm.3, ...), custom_call_target="tpu_custom_call" | custom-call | flops 80000000000 | tf_op jit(solution)/shard_map/gather_project/pallas_call | solution.py:535
  84.6 103.2 %scatter_heads.1 = (f32[256,2048]{1,0:T(8,128)}, bf16[2048,256]{1,0:T(8,128)(2,1)}, f32[8,2048]{1,0:T(8,128)}, bf16[2048,2048]{1,0:T(8,128)(2,1)}, bf16[2,704,20...) custom-call(bf16[2048,256]{1,0:T(8,128)(2,1)} %get-tuple-element.65.q_hbm, bf16[2048,256]{1,0:T(8,128)(2,1)} %get-tuple-element.66.k_hbm, ...), custom_call_target="tpu_custom_call" | custom-call | flops 80000000000 | tf_op jit(solution)/shard_map/scatter_heads/pallas_call | solution.py:535
  187.8 128.9 %gather_hidden.1 = (bf16[2048,2048]{1,0:T(8,128)(2,1)}, bf16[2048,704]{1,0:T(8,128)(2,1)}, bf16[2048,704]{1,0:T(8,128)(2,1)}, bf16[2048,704]{1,0:T(8,128)(2,1)},...) custom-call(f32[1,2048]{1,0:T(1,128)} %get-tuple-element.137.gain_ref, f32[1,2048]{1,0:T(1,128)} %get-tuple-element.132.shift_ref, ...), custom_call_target="tpu_custom_call" | custom-call | flops 80000000000 | tf_op jit(solution)/shard_map/gather_hidden/pallas_call | solution.py:535
  316.7 99.4 %gather_context.1 = (bf16[2048,2048]{1,0:T(8,128)(2,1)}, bf16[2048,256]{1,0:T(8,128)(2,1)}, f32[256,2048]{1,0:T(8,128)}, f32[2,2048]{1,0:T(2,128)}, bf16[256,204...) custom-call(f32[256,2048]{1,0:T(8,128)} %get-tuple-element.70.mid_hbm.mid_ref, ...), custom_call_target="tpu_custom_call" | custom-call | flops 80000000000 | tf_op jit(solution)/shard_map/gather_context/pallas_call | solution.py:535
  416.1 0.0 copy-start.17
  416.1 0.0 copy-start.18
  416.1 0.0 copy-start.19
  416.1 0.0 copy-start.11
  416.2 0.0 copy-start.12
  416.2 0.0 copy-start.13
  416.2 0.0 copy-start.14
  416.2 0.0 copy-start.15
  416.2 0.0 copy-start.16
  416.2 108.6 %scatter_triple.1 = (bf16[256,2048]{1,0:T(8,128)(2,1)}, f32[8,2048]{1,0:T(8,128)}, bf16[4,3,512,256]{3,2,1,0:T(8,128)(2,1)}, bf16[4,256,512]{2,1,0:T(8,128)(2,1)}) custom-call(s32[1,2048]{1,0:T(1,128)} %get-tuple-element.69.start_ref, f32[8,2048]{1,0:T(8,128)} %get-tuple-element.82.lse_ref, f32[8,2048]{1,0:T(8,128)} %get-tuple-element.83.delta, ...), custom_call_target="tpu_custom_call" | custom-call | flops 80000000000 | tf_op jit(solution)/shard_map/scatter_triple/pallas_call | solution.py:535
  524.8 0.0 copy-done.17
  524.8 0.0 copy-done.18
  524.8 0.0 copy-done.19
  524.8 1.3 multiply_subtract_fusion.6
  526.1 0.0 copy-done.11
  526.1 0.0 copy-done.12
  526.2 0.0 copy-done.13
  526.2 0.0 copy-done.14
  526.2 0.0 copy-done.15
  526.2 0.0 copy-done.16
  526.2 1.7 multiply_subtract_fusion.4
  527.8 0.0 copy-start.4
  527.8 0.0 copy-start.8
  527.9 3.3 multiply_subtract_fusion.3
  531.2 0.0 copy-done.4
  531.2 0.0 copy-done.8
  531.2 0.0 copy-start
  531.2 0.0 copy-start.5
  531.2 0.0 copy-start.6
  531.2 0.0 copy-start.7
  531.2 0.0 copy-start.3
  531.3 5.5 multiply_subtract_fusion.2
  536.7 0.0 slice-start
  536.7 0.0 copy-done
  536.7 0.0 copy-done.5
  536.7 0.0 copy-done.6
  536.7 0.0 copy-done.7
  536.8 0.0 slice-start.1
  536.8 0.0 copy-start.1
  536.8 0.0 copy-start.2
  536.8 3.7 multiply_subtract_fusion.1
  540.5 0.0 copy-done.3
  540.5 1.3 slice-done
  541.7 0.4 slice-done.1
  542.1 0.9 copy-done.1
  543.0 0.8 copy-done.2
  543.8 0.0 copy-start.9
  543.8 5.3 multiply_subtract_fusion
  549.2 0.0 copy-start.10
  549.2 0.0 copy-done.9
  549.2 1.0 copy.56
  550.2 0.6 copy-done.10
  550.8 1.0 copy.57
  (4 shorter events, 0.0 us)
Async XLA Ops:
  416.1 108.7 %copy-start.17 = (f32[3,256]{1,0:T(4,128)S(1)}, f32[3,256]{1,0:T(4,128)}, u32[]{:S(2)}) copy-start(f32[3,256]{1,0:T(4,128)} %bias_ref.1) | copy-start | bytes 9220
  416.1 108.7 %copy-start.18 = (f32[3,256]{1,0:T(4,128)S(1)}, f32[3,256]{1,0:T(4,128)}, u32[]{:S(2)}) copy-start(f32[3,256]{1,0:T(4,128)} %param.38) | copy-start | bytes 9220
  416.1 108.7 %copy-start.19 = (f32[3,256]{1,0:T(4,128)S(1)}, f32[3,256]{1,0:T(4,128)}, u32[]{:S(2)}) copy-start(f32[3,256]{1,0:T(4,128)} %param.45) | copy-start | bytes 9220
  416.1 110.0 %copy-start.11 = (f32[2,2048]{1,0:T(2,128)S(1)}, f32[2,2048]{1,0:T(2,128)}, u32[]{:S(2)}) copy-start(f32[2,2048]{1,0:T(2,128)} %param.33) | copy-start | bytes 49156
  416.2 110.0 %copy-start.12 = (f32[2,2048]{1,0:T(2,128)S(1)}, f32[2,2048]{1,0:T(2,128)}, u32[]{:S(2)}) copy-start(f32[2,2048]{1,0:T(2,128)} %param.32) | copy-start | bytes 49156
  416.2 110.0 %copy-start.13 = (f32[2,2048]{1,0:T(2,128)S(1)}, f32[2,2048]{1,0:T(2,128)}, u32[]{:S(2)}) copy-start(f32[2,2048]{1,0:T(2,128)} %param.40) | copy-start | bytes 49156
  416.2 110.0 %copy-start.14 = (f32[2,2048]{1,0:T(2,128)S(1)}, f32[2,2048]{1,0:T(2,128)}, u32[]{:S(2)}) copy-start(f32[2,2048]{1,0:T(2,128)} %param.47) | copy-start | bytes 49156
  416.2 110.0 %copy-start.15 = (f32[2,2048]{1,0:T(2,128)S(1)}, f32[2,2048]{1,0:T(2,128)}, u32[]{:S(2)}) copy-start(f32[2,2048]{1,0:T(2,128)} %param.46) | copy-start | bytes 49156
  416.2 110.0 %copy-start.16 = (f32[2,2048]{1,0:T(2,128)S(1)}, f32[2,2048]{1,0:T(2,128)}, u32[]{:S(2)}) copy-start(f32[2,2048]{1,0:T(2,128)} %param.39) | copy-start | bytes 49156
  527.8 3.3 copy-start.4
  527.8 3.3 copy-start.8
  531.2 5.5 %copy-start = (bf16[4,3,512,256]{3,2,1,0:T(8,128)(2,1)S(1)}, bf16[4,3,512,256]{3,2,1,0:T(8,128)(2,1)}, u32[]{:S(2)}) copy-start(bf16[4,3,512,256]{3,2,1,0:T(8,128)(2,1)} %get-tuple-element.95) | copy-start | bytes 9437188
  531.2 5.5 %copy-start.5 = (f32[3,512,256]{2,1,0:T(8,128)S(1)}, f32[3,512,256]{2,1,0:T(8,128)}, u32[]{:S(2)}) copy-start(f32[3,512,256]{2,1,0:T(8,128)} %qkv_ref.1) | copy-start | bytes 4718596
  531.2 5.5 copy-start.6
  531.2 5.5 copy-start.7
  531.2 9.2 %copy-start.3 = (f32[2,512,704]{1,2,0:T(8,128)S(1)}, f32[2,512,704]{1,2,0:T(8,128)}, u32[]{:S(2)}) copy-start(f32[2,512,704]{1,2,0:T(8,128)} %param.43) | copy-start | bytes 8650756
  536.7 5.0 slice-start
  536.8 5.4 slice-start.1
  536.8 6.2 %copy-start.1 = (f32[2,512,704]{1,2,0:T(8,128)S(1)}, f32[2,512,704]{1,2,0:T(8,128)}, u32[]{:S(2)}) copy-start(f32[2,512,704]{1,2,0:T(8,128)} %param.29) | copy-start | bytes 8650756
  536.8 7.1 %copy-start.2 = (f32[2,512,704]{1,2,0:T(8,128)S(1)}, f32[2,512,704]{1,2,0:T(8,128)}, u32[]{:S(2)}) copy-start(f32[2,512,704]{1,2,0:T(8,128)} %param.36) | copy-start | bytes 8650756
  543.8 5.4 copy-start.9
  549.2 1.6 copy-start.10
